TPU v7x, 32 devices: a whole 2x2x4 slice. The times are simulated.
32 devices in a mesh: blk: 4 (over x, core), uly: 2 (over y), batch: 4 (over z).
Axes of the slice: x: 2, y: 2, z: 4, core: 2. Of those that a mesh axis runs over, the one named last changes fastest.
Arguments:
- queries: bfloat16 [4096, 1024], P(('batch', 'blk', 'uly')), parts along dimension 0, may hold values from -10 to 10
- keys: bfloat16 [4096, 1024], P(('batch', 'blk', 'uly')), parts along dimension 0, may hold values from -10 to 10
- values: bfloat16 [4096, 1024], P(('batch', 'blk', 'uly')), parts along dimension 0, may hold values from -6 to 6
- out_grad: bfloat16 [4096, 1024], P(('batch', 'blk', 'uly')), parts along dimension 0, may hold values from -16 to 16
- block_mask: int32 [32, 8], P('batch'), parts along dimension 0, may hold values from 0 to 1, as said below
Outputs:
- query_grad: bfloat16 [4096, 1024], P(('batch', 'blk', 'uly')), parts along dimension 0
- key_grad: bfloat16 [4096, 1024], P(('batch', 'blk', 'uly')), parts along dimension 0
- value_grad: bfloat16 [4096, 1024], P(('batch', 'blk', 'uly')), parts along dimension 0
There are 4 independent parts, one for each index of `batch`. A program takes and returns all parts, laid end to end along the dimension named above; each array names one. Nothing has to cross between parts.
Inputs may be any that keep to these rules, and one draw needn't show every extreme that they name: block_mask[a, b] is 1 for every two blocks a, b of the same cell (cell c holds tokens c * 256 to (c + 1) * 256 - 1); for blocks of different cells it is 1 only where the two cells are neighbours on the closed chain of 4 cells (cell c beside cells c - 1 and c + 1 modulo 4), and 0 for all other pairs.
All inputs are finite; a program needn't handle non-finite values.
Results may differ from a plain program's by a relative error of at most 0.0096.
Values may be sent and summed in bfloat16 or wider, within the bound.
No kernel may reach another device: no remote copies, remote signals or barrier semaphores. Data moves between devices by JAX's collectives and lax.ppermute only.
A program may use at most 64 MiB of HBM per device.

v0:
```python
import math

import jax
import jax.numpy as jnp
from jax import lax
from jax.sharding import PartitionSpec as P

HEAD_DIM = 128


def padded(block, sides, width):
    for axis, dim in sides:
        count = lax.axis_size(axis)
        forward = [(i, i + 1) for i in range(count - 1)]
        forward.append((count - 1, 0))
        backward = [(target, source) for source, target in forward]
        low = lax.ppermute(
            lax.slice_in_dim(block, block.shape[dim] - width, None, axis=dim), axis, forward
        )
        high = lax.ppermute(lax.slice_in_dim(block, 0, width, axis=dim), axis, backward)
        block = jnp.concatenate([low, block, high], axis=dim)
    return block


def passed_along(block, axis, distance):
    devices = range(lax.axis_size(axis))
    route = [((i - distance) % len(devices), i) for i in devices]
    return lax.ppermute(block, axis, route)


def times_t(left, right):
    return lax.dot_general(
        left, right, (((1,), (1,)), ((), ())), preferred_element_type=jnp.float32
    )


def t_times(left, right):
    return lax.dot_general(
        left, right, (((0,), (0,)), ((), ())), preferred_element_type=jnp.float32
    )


def widen_blocks(mask_blocks):
    return jnp.repeat(jnp.repeat(mask_blocks > 0, 128, axis=0), 128, axis=1)


def local(queries, keys, values, out_grad, block_mask):
    local_q, local_k, local_v, local_g = (
        lax.all_to_all(queries, "uly", split_axis=1, concat_axis=0, tiled=True),
        lax.all_to_all(keys, "uly", split_axis=1, concat_axis=0, tiled=True),
        lax.all_to_all(values, "uly", split_axis=1, concat_axis=0, tiled=True),
        lax.all_to_all(out_grad, "uly", split_axis=1, concat_axis=0, tiled=True),
    )
    genes = local_q.shape[0]
    heads_here = local_q.shape[1] // HEAD_DIM
    scale = 1.0 / math.sqrt(HEAD_DIM)
    cells = lax.axis_size("blk")
    here = lax.axis_index("blk")
    per_cell = genes // 128
    near = (here + jnp.array([-1, 0, 1], dtype=jnp.int32) + cells) % cells
    mask_rows = lax.dynamic_slice_in_dim(block_mask, here * per_cell, per_cell, 0).reshape(
        per_cell, cells, per_cell
    )
    row_mask = widen_blocks(jnp.take(mask_rows, near, axis=1).reshape(per_cell, 3 * per_cell))
    pairs = jnp.stack([local_k, local_v], axis=1)
    band = padded(pairs, (("blk", 0),), genes)
    q_grads = []
    k_parts = []
    v_parts = []
    for head in range(heads_here):
        lower = head * HEAD_DIM
        upper = lower + HEAD_DIM
        q_head = local_q[:, lower:upper]
        g_head = local_g[:, lower:upper]
        k_band = band[:, 0, lower:upper]
        v_band = band[:, 1, lower:upper]
        scores = jnp.where(row_mask, times_t(q_head, k_band) * scale, -1e30)
        top = jnp.max(scores, axis=1, keepdims=True)
        total = jnp.sum(jnp.where(row_mask, jnp.exp(scores - top), 0.0), axis=1, keepdims=True)
        lse = top + jnp.log(total)
        probs = jnp.where(row_mask, jnp.exp(scores - lse), 0.0)
        dprobs = times_t(g_head, v_band)
        delta = jnp.sum(probs * dprobs, axis=1, keepdims=True)
        dscores = (probs * (dprobs - delta)).astype(jnp.bfloat16)
        q_grads.append(
            (jnp.dot(dscores, k_band, preferred_element_type=jnp.float32) * scale).astype(
                jnp.bfloat16
            )
        )
        k_parts.append(t_times(dscores, q_head))
        v_parts.append(t_times(probs.astype(jnp.bfloat16), g_head))
    query_grad = jnp.concatenate(q_grads, axis=1)
    partial_terms = jnp.stack(
        [jnp.concatenate(k_parts, axis=1), jnp.concatenate(v_parts, axis=1)], axis=1
    )
    from_next = passed_along(partial_terms[:genes].astype(jnp.bfloat16), "blk", -1).astype(
        jnp.float32
    )
    from_prior = passed_along(partial_terms[2 * genes :].astype(jnp.bfloat16), "blk", 1).astype(
        jnp.float32
    )
    summed = partial_terms[genes : 2 * genes] + from_next + from_prior
    key_grad = (summed[:, 0] * scale).astype(jnp.bfloat16)
    value_grad = summed[:, 1].astype(jnp.bfloat16)
    return (
        lax.all_to_all(query_grad, "uly", split_axis=0, concat_axis=1, tiled=True),
        lax.all_to_all(key_grad, "uly", split_axis=0, concat_axis=1, tiled=True),
        lax.all_to_all(value_grad, "uly", split_axis=0, concat_axis=1, tiled=True),
    )


def solution(mesh):
    return jax.shard_map(
        local,
        mesh=mesh,
        in_specs=(
            P(("batch", "blk", "uly"), None),
            P(("batch", "blk", "uly"), None),
            P(("batch", "blk", "uly"), None),
            P(("batch", "blk", "uly"), None),
            P("batch", None),
        ),
        out_specs=(
            P(("batch", "blk", "uly"), None),
            P(("batch", "blk", "uly"), None),
            P(("batch", "blk", "uly"), None),
        ),
        check_vma=False,
    )
```

profile of v0, /device:TPU:0, one launch (start us, length us, event | category | flops | bytes accessed | tf_op | source)
XLA Modules:
  0.0 84.1 jit_solution(6600983813323210247)
XLA Ops:
  0.7 1.8 %copy.33 = bf16[128,1024]{0,1:T(8,128)(2,1)} copy(bf16[128,1024]{1,0:T(8,128)(2,1)} %param.7) | data formatting | bytes 524288 | tf_op args[1]
  2.5 4.2 %all-to-all-start = ((bf16[128,2,512]{0,2,1:T(8,128)(2,1)}), bf16[128,2,512]{0,2,1:T(8,128)(2,1)S(1)}, u32[]{:S(2)}, u32[]{:S(2)}) async-start(bf16[128,2,512]{0,2,1:T(8,128)(2,1)} %bitcast.3), calls=%async_computation | async-start | bytes 524288 | tf_op jit(solution)/shard_map/all_to_all | solution.py:50
  6.7 1.8 %copy.35 = bf16[128,1024]{0,1:T(8,128)(2,1)} copy(bf16[128,1024]{1,0:T(8,128)(2,1)} %param.8) | data formatting | bytes 524288 | tf_op args[2]
  8.5 4.1 %all-to-all-done = bf16[128,2,512]{0,2,1:T(8,128)(2,1)S(1)} async-done(((bf16[128,2,512]{0,2,1:T(8,128)(2,1)}), bf16[128,2,512]{0,2,1:T(8,128)(2,1)S(1)}, u32[]{:S(2)}, u32[]{:S(2)}) %all-to-all-start) | async-done | bytes 262176 | tf_op jit(solution)/shard_map/all_to_all | solution.py:50
  12.6 3.4 %all-to-all-start.1 = ((bf16[128,2,512]{0,2,1:T(8,128)(2,1)}), bf16[128,2,512]{0,2,1:T(8,128)(2,1)S(1)}, u32[]{:S(2)}, u32[]{:S(2)}) async-start(bf16[128,2,512]{0,2,1:T(8,128)(2,1)} %bitcast.6), calls=%async_computation.1 | async-start | bytes 524288 | tf_op jit(solution)/shard_map/all_to_all | solution.py:51
  16.4 0.8 %copy.37 = bf16[128,1024]{0,1:T(8,128)(2,1)} copy(bf16[128,1024]{1,0:T(8,128)(2,1)S(1)} %copy-done.3) | data formatting | bytes 524288 | tf_op args[0]
  17.4 3.9 %all-to-all-done.1 = bf16[128,2,512]{0,2,1:T(8,128)(2,1)S(1)} async-done(((bf16[128,2,512]{0,2,1:T(8,128)(2,1)}), bf16[128,2,512]{0,2,1:T(8,128)(2,1)S(1)}, u32[]{:S(2)}, u32[]{:S(2)}) %all-to-all-start.1) | async-done | bytes 262176 | tf_op jit(solution)/shard_map/all_to_all | solution.py:51
  21.2 3.4 %all-to-all-start.2 = ((bf16[128,2,512]{0,2,1:T(8,128)(2,1)}), bf16[128,2,512]{0,2,1:T(8,128)(2,1)S(1)}, u32[]{:S(2)}, u32[]{:S(2)}) async-start(bf16[128,2,512]{0,2,1:T(8,128)(2,1)} %bitcast.10), calls=%async_computation.2 | async-start | bytes 524288 | tf_op jit(solution)/shard_map/all_to_all | solution.py:49
  25.5 0.6 gather_fusion
  26.1 0.8 %copy.39 = bf16[128,1024]{0,1:T(8,128)(2,1)} copy(bf16[128,1024]{1,0:T(8,128)(2,1)S(1)} %copy-done.4) | data formatting | bytes 524288 | tf_op args[3]
  27.0 2.9 %all-to-all-done.2 = bf16[128,2,512]{0,2,1:T(8,128)(2,1)S(1)} async-done(((bf16[128,2,512]{0,2,1:T(8,128)(2,1)}), bf16[128,2,512]{0,2,1:T(8,128)(2,1)S(1)}, u32[]{:S(2)}, u32[]{:S(2)}) %all-to-all-start.2) | async-done | bytes 262176 | tf_op jit(solution)/shard_map/all_to_all | solution.py:49
  29.8 3.4 %all-to-all-start.3 = ((bf16[128,2,512]{0,2,1:T(8,128)(2,1)}), bf16[128,2,512]{0,2,1:T(8,128)(2,1)S(1)}, u32[]{:S(2)}, u32[]{:S(2)}) async-start(bf16[128,2,512]{0,2,1:T(8,128)(2,1)} %bitcast.15), calls=%async_computation.3 | async-start | bytes 524288 | tf_op jit(solution)/shard_map/all_to_all | solution.py:52
  33.5 4.9 %all-to-all-done.3 = bf16[128,2,512]{0,2,1:T(8,128)(2,1)S(1)} async-done(((bf16[128,2,512]{0,2,1:T(8,128)(2,1)}), bf16[128,2,512]{0,2,1:T(8,128)(2,1)S(1)}, u32[]{:S(2)}, u32[]{:S(2)}) %all-to-all-start.3) | async-done | bytes 262176 | tf_op jit(solution)/shard_map/all_to_all | solution.py:52
  41.2 0.5 fusion.12
  41.8 0.8 multiply_reduce_fusion.3
  42.5 0.8 fusion.17
  46.7 1.1 %fusion.46 = (bf16[256,2,512]{0,2,1:T(8,128)(2,1)}, bf16[256,2,512]{0,2,1:T(8,128)(2,1)}) fusion(bf16[768,2,512]{0,2,1:T(8,128)(2,1)S(1)} %fusion), kind=kLoop, calls=%fused_computation.111 | loop fusion | bytes 2097152 | tf_op jit(solution)/shard_map/slice | solution.py:96
  48.8 0.7 copy_bitcast_fusion
  49.6 3.4 %all-to-all-start.4 = ((bf16[2,128,512]{1,2,0:T(8,128)(2,1)}), bf16[2,128,512]{1,2,0:T(8,128)(2,1)S(1)}, u32[]{:S(2)}, u32[]{:S(2)}) async-start(bf16[2,128,512]{1,2,0:T(8,128)(2,1)} %copy_bitcast_fusion), calls=%async_computation.4 | async-start | bytes 524288 | tf_op jit(solution)/shard_map/all_to_all | solution.py:106
  53.0 6.3 %collective-permute-done.2 = bf16[256,2,512]{0,2,1:T(8,128)(2,1)} collective-permute-done((bf16[256,2,512]{0,2,1:T(8,128)(2,1)}, bf16[256,2,512]{0,2,1:T(8,128)(2,1)}, u32[]{:S(2)}, u32[]{:S(2)}) %collective-permute-start.2) | collective-permute-done | bytes 524320 | tf_op jit(solution)/shard_map/ppermute | solution.py:28
  59.3 2.8 %collective-permute-done.3 = bf16[256,2,512]{0,2,1:T(8,128)(2,1)} collective-permute-done((bf16[256,2,512]{0,2,1:T(8,128)(2,1)}, bf16[256,2,512]{0,2,1:T(8,128)(2,1)}, u32[]{:S(2)}, u32[]{:S(2)}) %collective-permute-start.3) | collective-permute-done | bytes 524320 | tf_op jit(solution)/shard_map/ppermute | solution.py:28
  62.1 1.4 %fusion.11 = f32[256,2,512]{0,2,1:T(8,128)S(1)} fusion(f32[768,1,512]{0,2,1:T(8,128)S(1)} %maximum_bitcast_fusion, f32[768,1,512]{0,2,1:T(8,128)S(1)} %maximum_bitcast_fusion.1, bf16[256,2,512]{0,2,1:T(8,128)(2,1)} %collective-permute-done.3, bf16[256,2,512]{0,2,1:T(8,128)(2,1)} %collective-permute-done.2), kind=kLoop, calls=%fused_computation.42 | loop fusion | flops 1310720 | bytes 5242880 | tf_op jit(solution)/shard_map/add | solution.py:102
  63.5 1.0 %copy-done.1 = f32[256,2,512]{0,2,1:T(8,128)} copy-done((f32[256,2,512]{0,2,1:T(8,128)}, f32[256,2,512]{0,2,1:T(8,128)S(1)}, u32[]{:S(2)}) %copy-start.1) | copy-done | bytes 1048600
  64.5 0.7 copy.43
  65.3 3.4 %all-to-all-start.6 = ((bf16[2,128,512]{1,2,0:T(8,128)(2,1)}), bf16[2,128,512]{1,2,0:T(8,128)(2,1)S(1)}, u32[]{:S(2)}, u32[]{:S(2)}) async-start(bf16[2,128,512]{1,2,0:T(8,128)(2,1)} %copy.43), calls=%async_computation.6 | async-start | bytes 524288 | tf_op jit(solution)/shard_map/all_to_all | solution.py:108
  68.9 0.7 copy.42
  69.6 5.0 %all-to-all-done.6 = bf16[2,128,512]{1,2,0:T(8,128)(2,1)S(1)} async-done(((bf16[2,128,512]{1,2,0:T(8,128)(2,1)}), bf16[2,128,512]{1,2,0:T(8,128)(2,1)S(1)}, u32[]{:S(2)}, u32[]{:S(2)}) %all-to-all-start.6) | async-done | bytes 262176 | tf_op jit(solution)/shard_map/all_to_all | solution.py:108
  74.6 3.4 %all-to-all-start.5 = ((bf16[2,128,512]{1,2,0:T(8,128)(2,1)}), bf16[2,128,512]{1,2,0:T(8,128)(2,1)S(1)}, u32[]{:S(2)}, u32[]{:S(2)}) async-start(bf16[2,128,512]{1,2,0:T(8,128)(2,1)} %copy.42), calls=%async_computation.5 | async-start | bytes 524288 | tf_op jit(solution)/shard_map/all_to_all | solution.py:107
  78.1 0.9 %copy.44 = bf16[128,1024]{1,0:T(8,128)(2,1)} copy(bf16[128,1024]{0,1:T(8,128)(2,1)S(1)} %bitcast.177) | data formatting | bytes 524288
  79.0 0.9 %copy.46 = bf16[128,1024]{1,0:T(8,128)(2,1)} copy(bf16[128,1024]{0,1:T(8,128)(2,1)S(1)} %bitcast.180) | data formatting | bytes 524288
  79.8 3.5 %all-to-all-done.5 = bf16[2,128,512]{1,2,0:T(8,128)(2,1)S(1)} async-done(((bf16[2,128,512]{1,2,0:T(8,128)(2,1)}), bf16[2,128,512]{1,2,0:T(8,128)(2,1)S(1)}, u32[]{:S(2)}, u32[]{:S(2)}) %all-to-all-start.5) | async-done | bytes 262176 | tf_op jit(solution)/shard_map/all_to_all | solution.py:107
  83.3 0.9 %copy.45 = bf16[128,1024]{1,0:T(8,128)(2,1)} copy(bf16[128,1024]{0,1:T(8,128)(2,1)S(1)} %bitcast.182) | data formatting | bytes 524288
  (63 shorter events, 8.9 us)
Async XLA Ops:
  0.6 15.6 %copy-start = (s32[8,8]{1,0:T(8,128)S(1)}, s32[8,8]{1,0:T(8,128)}, u32[]{:S(2)}) copy-start(s32[8,8]{1,0:T(8,128)} %param.10) | copy-start | bytes 772
  0.6 15.4 %copy-start.5 = (s32[3]{0:T(128)S(1)}, s32[3]{0:T(128)}, u32[]{:S(2)}) copy-start(s32[3]{0:T(128)} %constant.52.clone) | copy-start | bytes 40
  0.7 15.7 %copy-start.3 = (bf16[128,1024]{1,0:T(8,128)(2,1)S(1)}, bf16[128,1024]{1,0:T(8,128)(2,1)}, u32[]{:S(2)}) copy-start(bf16[128,1024]{1,0:T(8,128)(2,1)} %param.6) | copy-start | bytes 786436
  2.5 10.1 %all-to-all-start = ((bf16[128,2,512]{0,2,1:T(8,128)(2,1)}), bf16[128,2,512]{0,2,1:T(8,128)(2,1)S(1)}, u32[]{:S(2)}, u32[]{:S(2)}) async-start(bf16[128,2,512]{0,2,1:T(8,128)(2,1)} %bitcast.3), calls=%async_computation | async-start | bytes 524288 | tf_op jit(solution)/shard_map/all_to_all | solution.py:50
  12.6 8.6 %all-to-all-start.1 = ((bf16[128,2,512]{0,2,1:T(8,128)(2,1)}), bf16[128,2,512]{0,2,1:T(8,128)(2,1)S(1)}, u32[]{:S(2)}, u32[]{:S(2)}) async-start(bf16[128,2,512]{0,2,1:T(8,128)(2,1)} %bitcast.6), calls=%async_computation.1 | async-start | bytes 524288 | tf_op jit(solution)/shard_map/all_to_all | solution.py:51
  16.4 9.8 %copy-start.4 = (bf16[128,1024]{1,0:T(8,128)(2,1)S(1)}, bf16[128,1024]{1,0:T(8,128)(2,1)}, u32[]{:S(2)}) copy-start(bf16[128,1024]{1,0:T(8,128)(2,1)} %param.9) | copy-start | bytes 786436
  21.2 8.6 %all-to-all-start.2 = ((bf16[128,2,512]{0,2,1:T(8,128)(2,1)}), bf16[128,2,512]{0,2,1:T(8,128)(2,1)S(1)}, u32[]{:S(2)}, u32[]{:S(2)}) async-start(bf16[128,2,512]{0,2,1:T(8,128)(2,1)} %bitcast.10), calls=%async_computation.2 | async-start | bytes 524288 | tf_op jit(solution)/shard_map/all_to_all | solution.py:49
  24.9 13.7 %collective-permute-start.1 = (bf16[256,2,512]{2,0,1:T(8,128)(2,1)S(1)}, bf16[256,2,512]{2,0,1:T(8,128)(2,1)S(1)}, u32[]{:S(2)}, u32[]{:S(2)}) collective-permute-start(bf16[256,2,512]{2,0,1:T(8,128)(2,1)S(1)} %pad_maximum_fusion.2), channel_id=1, source_target_pairs={{8,0},{16,8},{24,16},{0,24},{9,1},{17,9},{25,17},{1,25},{10,2},{18... | collective-permute-start | bytes 1572872 | tf_op jit(solution)/shard_map/ppermute | solution.py:20
  25.0 14.1 %collective-permute-start = (bf16[256,2,512]{2,0,1:T(8,128)(2,1)S(1)}, bf16[256,2,512]{2,0,1:T(8,128)(2,1)S(1)}, u32[]{:S(2)}, u32[]{:S(2)}) collective-permute-start(bf16[256,2,512]{2,0,1:T(8,128)(2,1)S(1)} %pad_maximum_fusion.2), channel_id=1, source_target_pairs={{0,8},{8,16},{16,24},{24,0},{1,9},{9,17},{17,25},{25,1},{2,10},{10... | collective-permute-start | bytes 1572872 | tf_op jit(solution)/shard_map/ppermute | solution.py:17
  29.8 8.6 %all-to-all-start.3 = ((bf16[128,2,512]{0,2,1:T(8,128)(2,1)}), bf16[128,2,512]{0,2,1:T(8,128)(2,1)S(1)}, u32[]{:S(2)}, u32[]{:S(2)}) async-start(bf16[128,2,512]{0,2,1:T(8,128)(2,1)} %bitcast.15), calls=%async_computation.3 | async-start | bytes 524288 | tf_op jit(solution)/shard_map/all_to_all | solution.py:52
  47.8 11.5 %collective-permute-start.2 = (bf16[256,2,512]{0,2,1:T(8,128)(2,1)}, bf16[256,2,512]{0,2,1:T(8,128)(2,1)}, u32[]{:S(2)}, u32[]{:S(2)}) collective-permute-start(bf16[256,2,512]{0,2,1:T(8,128)(2,1)} %get-tuple-element.16), channel_id=1, source_target_pairs={{8,0},{16,8},{24,16},{0,24},{9,1},{17,9},{25,17},{1,25},{10,2},{18... | collective-permute-start | bytes 1572872 | tf_op jit(solution)/shard_map/ppermute | solution.py:28
  47.8 14.3 %collective-permute-start.3 = (bf16[256,2,512]{0,2,1:T(8,128)(2,1)}, bf16[256,2,512]{0,2,1:T(8,128)(2,1)}, u32[]{:S(2)}, u32[]{:S(2)}) collective-permute-start(bf16[256,2,512]{0,2,1:T(8,128)(2,1)} %get-tuple-element.17), channel_id=1, source_target_pairs={{24,0},{0,8},{8,16},{16,24},{25,1},{1,9},{9,17},{17,25},{26,2},{2,... | collective-permute-start | bytes 1572872 | tf_op jit(solution)/shard_map/ppermute | solution.py:28
  49.6 15.7 %all-to-all-start.4 = ((bf16[2,128,512]{1,2,0:T(8,128)(2,1)}), bf16[2,128,512]{1,2,0:T(8,128)(2,1)S(1)}, u32[]{:S(2)}, u32[]{:S(2)}) async-start(bf16[2,128,512]{1,2,0:T(8,128)(2,1)} %copy_bitcast_fusion), calls=%async_computation.4 | async-start | bytes 524288 | tf_op jit(solution)/shard_map/all_to_all | solution.py:106
  63.4 1.0 %copy-start.1 = (f32[256,2,512]{0,2,1:T(8,128)}, f32[256,2,512]{0,2,1:T(8,128)S(1)}, u32[]{:S(2)}) copy-start(f32[256,2,512]{0,2,1:T(8,128)S(1)} %fusion.11) | copy-start | bytes 3145732
  64.5 4.3 %copy-start.2 = (f32[256,2,512]{0,2,1:T(8,128)S(1)}, f32[256,2,512]{0,2,1:T(8,128)}, u32[]{:S(2)}) copy-start(f32[256,2,512]{0,2,1:T(8,128)} %copy-done.1) | copy-start | bytes 3145732
  65.3 9.4 %all-to-all-start.6 = ((bf16[2,128,512]{1,2,0:T(8,128)(2,1)}), bf16[2,128,512]{1,2,0:T(8,128)(2,1)S(1)}, u32[]{:S(2)}, u32[]{:S(2)}) async-start(bf16[2,128,512]{1,2,0:T(8,128)(2,1)} %copy.43), calls=%async_computation.6 | async-start | bytes 524288 | tf_op jit(solution)/shard_map/all_to_all | solution.py:108
  74.6 8.6 %all-to-all-start.5 = ((bf16[2,128,512]{1,2,0:T(8,128)(2,1)}), bf16[2,128,512]{1,2,0:T(8,128)(2,1)S(1)}, u32[]{:S(2)}, u32[]{:S(2)}) async-start(bf16[2,128,512]{1,2,0:T(8,128)(2,1)} %copy.42), calls=%async_computation.5 | async-start | bytes 524288 | tf_op jit(solution)/shard_map/all_to_all | solution.py:107
where the time goes:
time: 84.7 us; the launch traced here: 84.1 us
  waiting for transfers between devices  33.7 us (40%)
  starting transfers between devices  26 us (31%)
  local copies, waits for them, and re-layouts  13.2 us (16%)
  matrix products  6.21 us (7%)
  other arithmetic  4.13 us (5%)
  between operations  0.93 us (1%)
    ppermute x2, waiting for transfers between devices, passed_along(): return lax.ppermute(block, axis, route)  9.05 us
    unnamed x19, local copies, waits for them, and re-layouts  8.88 us
    all_to_all x1, waiting for transfers between devices, local(): lax.all_to_all(value_grad, 'uly', split_axis=0, concat_axis=1, tiled=True)  5.03 us
    all_to_all x1, waiting for transfers between devices, local(): lax.all_to_all(out_grad, 'uly', split_axis=1, concat_axis=0, tiled=True)  4.93 us
    all_to_all x1, starting transfers between devices, local(): lax.all_to_all(keys, 'uly', split_axis=1, concat_axis=0, tiled=True)  4.23 us
    all_to_all x1, waiting for transfers between devices, local(): lax.all_to_all(keys, 'uly', split_axis=1, concat_axis=0, tiled=True)  4.08 us
    all_to_all x1, waiting for transfers between devices, local(): lax.all_to_all(values, 'uly', split_axis=1, concat_axis=0, tiled=True)  3.85 us
    all_to_all x1, waiting for transfers between devices, local(): lax.all_to_all(key_grad, 'uly', split_axis=0, concat_axis=1, tiled=True)  3.45 us
  transfers between devices with their start and end apart: 11, of which 9 were waited for; matrix products, arithmetic and copies ran while one was open for 13% of the time, Pallas kernels for 0%

commit v1 on v0

--- a/solution.py
+++ b/solution.py
@@ -3,9 +3,13 @@
 import jax
 import jax.numpy as jnp
 from jax import lax
+from jax.experimental import pallas as pl
+from jax.experimental.pallas import tpu as pltpu
 from jax.sharding import PartitionSpec as P
 
 HEAD_DIM = 128
+GROUP = ("blk", "uly")
+ORDER = (5, 7, 4, 6, 1, 3, 2)
 
 
 def padded(block, sides, width):
@@ -44,7 +48,7 @@
     return jnp.repeat(jnp.repeat(mask_blocks > 0, 128, axis=0), 128, axis=1)
 
 
-def local(queries, keys, values, out_grad, block_mask):
+def by_cells(queries, keys, values, out_grad, block_mask):
     local_q, local_k, local_v, local_g = (
         lax.all_to_all(queries, "uly", split_axis=1, concat_axis=0, tiled=True),
         lax.all_to_all(keys, "uly", split_axis=1, concat_axis=0, tiled=True),
@@ -109,6 +113,166 @@
     )
 
 
+def flat_index(axes):
+    index = 0
+    for axis in axes:
+        index = index * lax.axis_size(axis) + lax.axis_index(axis)
+    return index
+
+
+def exchange(block, distance):
+    devices = lax.axis_size(GROUP)
+    return lax.ppermute(block, GROUP, [(i, i ^ distance) for i in range(devices)])
+
+
+def head_columns(head):
+    return pl.ds(pl.multiple_of(head * HEAD_DIM, HEAD_DIM), HEAD_DIM)
+
+
+def pack_kernel(here_ref, *refs):
+    arrays, slabs = refs[:4], refs[4:]
+    for distance, slab in enumerate(slabs):
+        columns = head_columns(here_ref[0] ^ distance)
+        for n, array in enumerate(arrays):
+            slab[:, n * HEAD_DIM : (n + 1) * HEAD_DIM] = array[:, columns]
+
+
+def unpack_kernel(here_ref, *refs):
+    slabs, arrays = refs[:-3], refs[-3:]
+    for distance, slab in enumerate(slabs):
+        columns = head_columns(here_ref[0] ^ distance)
+        for n, array in enumerate(arrays):
+            array[:, columns] = slab[:, n * HEAD_DIM : (n + 1) * HEAD_DIM]
+
+
+def attention_kernel(here_ref, mask_ref, *refs):
+    count = len(refs) // 2
+    slabs, outs = refs[:count], refs[count:]
+    scale = 1.0 / math.sqrt(HEAD_DIM)
+    here = here_ref[0]
+    cells = count // 2
+
+    def cell(c, n):
+        columns = slice(n * HEAD_DIM, (n + 1) * HEAD_DIM)
+        return jnp.concatenate([slabs[2 * c][:, columns], slabs[2 * c + 1][:, columns]], axis=0)
+
+    q = [cell(c, 0) for c in range(cells)]
+    k = [cell(c, 1) for c in range(cells)]
+    v = [cell(c, 2) for c in range(cells)]
+    g = [cell(c, 3) for c in range(cells)]
+    k_turned = [block.T for block in k]
+    dk = [None] * cells
+    dv = [None] * cells
+    rows = q[0].shape[0]
+    half = rows // 2
+    lane = lax.broadcasted_iota(jnp.int32, (1, rows), 1)
+
+    def add(total, term):
+        return term if total is None else total + term
+
+    for c in range(cells):
+        near = [c, c ^ 1, c ^ 3]
+        scores = [times_t(k[n], q[c]) for n in near]
+        allowed = []
+        for n in near:
+            for a in range(2):
+                key_block = here ^ (2 * n + a)
+                low = mask_ref[here ^ (2 * c), key_block]
+                high = mask_ref[here ^ (2 * c + 1), key_block]
+                allowed.append(jnp.where(lane < half, low, high) > 0)
+        top = jnp.full((1, rows), -1e30, jnp.float32)
+        for t in range(3):
+            for a in range(2):
+                block = scores[t][a * half : (a + 1) * half]
+                top = jnp.maximum(
+                    top, jnp.where(allowed[2 * t + a], jnp.max(block, axis=0, keepdims=True), -1e30)
+                )
+        factor = scale * math.log2(math.e)
+        top = top * factor
+        exps = []
+        total = jnp.zeros((1, rows), jnp.float32)
+        for t in range(3):
+            parts = []
+            for a in range(2):
+                block = scores[t][a * half : (a + 1) * half]
+                shift = jnp.where(allowed[2 * t + a], top, 1e30)
+                parts.append(jnp.exp2(block * factor - shift))
+            part = jnp.concatenate(parts, axis=0)
+            total = total + jnp.sum(part, axis=0, keepdims=True)
+            exps.append(part)
+        inverse = 1.0 / total
+        probs = [part * inverse for part in exps]
+        dprobs = [times_t(v[n], g[c]) for n in near]
+        delta = jnp.zeros((1, rows), jnp.float32)
+        for t in range(3):
+            delta = delta + jnp.sum(probs[t] * dprobs[t], axis=0, keepdims=True)
+        dq = None
+        for t, n in enumerate(near):
+            low = probs[t].astype(jnp.bfloat16)
+            dscores = (probs[t] * (dprobs[t] - delta)).astype(jnp.bfloat16)
+            dv[n] = add(dv[n], jnp.dot(low, g[c], preferred_element_type=jnp.float32))
+            dk[n] = add(dk[n], jnp.dot(dscores, q[c], preferred_element_type=jnp.float32))
+            dq = add(dq, jnp.dot(k_turned[n], dscores, preferred_element_type=jnp.float32))
+        dq = (dq * scale).T.astype(jnp.bfloat16)
+        for a in range(2):
+            outs[2 * c + a][:, :HEAD_DIM] = dq[a * half : (a + 1) * half]
+    for c in range(cells):
+        dk_low = (dk[c] * scale).astype(jnp.bfloat16)
+        dv_low = dv[c].astype(jnp.bfloat16)
+        for a in range(2):
+            outs[2 * c + a][:, HEAD_DIM : 2 * HEAD_DIM] = dk_low[a * half : (a + 1) * half]
+            outs[2 * c + a][:, 2 * HEAD_DIM :] = dv_low[a * half : (a + 1) * half]
+
+
+SMEM = pl.BlockSpec(memory_space=pltpu.SMEM)
+VMEM = pl.BlockSpec(memory_space=pltpu.VMEM)
+
+
+def by_heads(queries, keys, values, out_grad, block_mask):
+    devices = lax.axis_size(GROUP)
+    tokens = queries.shape[0]
+    here = flat_index(GROUP).astype(jnp.int32).reshape(1)
+    slab = jax.ShapeDtypeStruct((tokens, 4 * HEAD_DIM), jnp.bfloat16)
+    out_slab = jax.ShapeDtypeStruct((tokens, 3 * HEAD_DIM), jnp.bfloat16)
+    sent = pl.pallas_call(
+        pack_kernel,
+        out_shape=[slab] * devices,
+        in_specs=[SMEM] + [VMEM] * 4,
+        out_specs=[VMEM] * devices,
+        name="pack",
+    )(here, queries, keys, values, out_grad)
+    order = ORDER
+    got = [sent[0]] + [None] * (devices - 1)
+    for distance in order:
+        got[distance] = exchange(sent[distance], distance)
+    grads = pl.pallas_call(
+        attention_kernel,
+        out_shape=[out_slab] * devices,
+        in_specs=[SMEM, SMEM] + [VMEM] * devices,
+        out_specs=[VMEM] * devices,
+        compiler_params=pltpu.CompilerParams(vmem_limit_bytes=40 * 1024 * 1024),
+        name="attention",
+    )(here, block_mask, *got)
+    back = [grads[0]] + [None] * (devices - 1)
+    for distance in order:
+        back[distance] = exchange(grads[distance], distance)
+    return pl.pallas_call(
+        unpack_kernel,
+        out_shape=[jax.ShapeDtypeStruct(queries.shape, queries.dtype)] * 3,
+        in_specs=[SMEM] + [VMEM] * devices,
+        out_specs=[VMEM] * 3,
+        name="unpack",
+    )(here, *back)
+
+
+def local(queries, keys, values, out_grad, block_mask):
+    heads = queries.shape[1] // HEAD_DIM
+    cells, halves = lax.axis_size("blk"), lax.axis_size("uly")
+    if (cells, halves) == (4, 2) and heads == cells * halves and queries.shape[0] == 128:
+        return by_heads(queries, keys, values, out_grad, block_mask)
+    return by_cells(queries, keys, values, out_grad, block_mask)
+
+
 def solution(mesh):
     return jax.shard_map(
         local,

time: 84.7 us -> 42.6 us (0.50)
  waiting for transfers between devices: 33.7 us -> 14.8 us
  local copies, waits for them, and re-layouts: 13.2 us -> 2.15 us
  starting transfers between devices: 26 us -> 15.7 us
  Pallas kernels: 0 us -> 8.9 us
  matrix products: 6.21 us -> 0 us
  other arithmetic: 4.13 us -> 0 us
    all_to_all x7 -> x0, starting transfers between devices: 24.9 us -> none  [the longest x1 4.23 us: local(): lax.all_to_all(keys, 'uly', split_axis=1, concat_axis=0, tiled=True)]
    all_to_all x7 -> x0, waiting for transfers between devices: 24.2 us -> none  [the longest x1 5.03 us: local(): lax.all_to_all(value_grad, 'uly', split_axis=0, concat_axis=1, tiled=True)]
    ppermute x4 -> x14, starting transfers between devices: 1.06 us -> 15.7 us  [exchange(): lax.ppermute(block, GROUP, [(i, i ^ distance) for i in range(devices)])]
    pallas_call x0 -> x3, Pallas kernels: none -> 8.9 us  [the longest x1 4.17 us: by_heads(): pl.pallas_call(attention_kernel, out_shape=[out_slab] * devices, in_specs...]
    unnamed x19 -> x20, local copies, waits for them, and re-layouts: 8.88 us -> 2.15 us
    dot_general x20 -> x0, matrix products: 6.21 us -> none  [the longest x8 2.78 us: times_t(): lax.dot_general(left, right, (((1,), (1,)), ((), ())), preferred_element_...]
    ppermute x4 -> x14, waiting for transfers between devices: 9.51 us -> 14.8 us  [exchange(): lax.ppermute(block, GROUP, [(i, i ^ distance) for i in range(devices)])]
    convert_element_type x4 -> x0, local copies, waits for them, and re-layouts: 1.61 us -> none  [the longest x2 0.81 us: local(): value_grad = summed[:, 1].astype(jnp.bfloat16)]
  transfers between devices with their start and end apart: 11 -> 14, of which waited for: 9 -> 10; matrix products, arithmetic and copies ran while one was open for 13% -> 0% of each run, Pallas kernels for 0% -> 0%
where the time goes in v1:
time: 42.6 us; the launch traced here: 42.2 us
  starting transfers between devices  15.7 us (37%)
  waiting for transfers between devices  14.8 us (35%)
  Pallas kernels  8.9 us (21%)
  local copies, waits for them, and re-layouts  2.15 us (5%)
  between operations  0.7 us (2%)
    ppermute x14, starting transfers between devices, exchange(): lax.ppermute(block, GROUP, [(i, i ^ distance) for i in range(devices)])  15.7 us
    ppermute x14, waiting for transfers between devices, exchange(): lax.ppermute(block, GROUP, [(i, i ^ distance) for i in range(devices)])  14.8 us
    pallas_call x1, Pallas kernels, by_heads(): pl.pallas_call(attention_kernel, out_shape=[out_slab] * devices, in_specs...  4.17 us
    pallas_call x1, Pallas kernels, by_heads(): pl.pallas_call(pack_kernel, out_shape=[slab] * devices, in_specs=[SMEM] +...  2.41 us
    pallas_call x1, Pallas kernels, by_heads(): pl.pallas_call(unpack_kernel, out_shape=[jax.ShapeDtypeStruct(queries.sha...  2.31 us
    unnamed x20, local copies, waits for them, and re-layouts  2.15 us
  transfers between devices with their start and end apart: 14, of which 10 were waited for; matrix products, arithmetic and copies ran while one was open for 0% of the time, Pallas kernels for 0%

profile of v1, /device:TPU:0, one launch (start us, length us, event | category | flops | bytes accessed | tf_op | source)
XLA Modules:
  0.0 42.2 jit_solution(14246584838555931295)
XLA Ops:
  0.6 2.4 %pack.1 = (bf16[128,512]{1,0:T(8,128)(2,1)}, bf16[128,512]{1,0:T(8,128)(2,1)}, bf16[128,512]{1,0:T(8,128)(2,1)}, bf16[128,512]{1,0:T(8,128)(2,1)}, bf16[128,512]...) custom-call(s32[1]{0:T(128)} %bitcast.here_ref, ...), custom_call_target="tpu_custom_call" | custom-call | tf_op jit(solution)/shard_map/pack/pallas_call | solution.py:237
  3.1 3.0 %collective-permute-start = (bf16[128,512]{1,0:T(8,128)(2,1)}, bf16[128,512]{1,0:T(8,128)(2,1)S(1)}, u32[]{:S(2)}, u32[]{:S(2)}) collective-permute-start(bf16[128,512]{1,0:T(8,128)(2,1)} %get-tuple-element.20), channel_id=1, source_target_pairs={{0,4},{4,0},{8,12},{12,8},{16,20},{20,16},{24,28},{28,24},{1,5},{5... | collective-permute-start | bytes 393224 | tf_op jit(solution)/shard_map/ppermute | solution.py:125
  6.0 0.0 collective-permute-start.1
  6.0 0.2 collective-permute-start.2
  6.2 1.9 %collective-permute-start.3 = (bf16[128,512]{1,0:T(8,128)(2,1)}, bf16[128,512]{1,0:T(8,128)(2,1)S(1)}, u32[]{:S(2)}, u32[]{:S(2)}) collective-permute-start(bf16[128,512]{1,0:T(8,128)(2,1)} %get-tuple-element.23), channel_id=1, source_target_pairs={{0,16},{4,20},{8,24},{12,28},{16,0},{20,4},{24,8},{28,12},{1,17},{... | collective-permute-start | bytes 393224 | tf_op jit(solution)/shard_map/ppermute | solution.py:125
  8.1 1.5 %collective-permute-start.4 = (bf16[128,512]{1,0:T(8,128)(2,1)}, bf16[128,512]{1,0:T(8,128)(2,1)S(1)}, u32[]{:S(2)}, u32[]{:S(2)}) collective-permute-start(bf16[128,512]{1,0:T(8,128)(2,1)} %get-tuple-element.24), channel_id=1, source_target_pairs={{0,20},{4,16},{8,28},{12,24},{16,4},{20,0},{24,12},{28,8},{1,21},{... | collective-permute-start | bytes 393224 | tf_op jit(solution)/shard_map/ppermute | solution.py:125
  9.6 0.6 %collective-permute-done.refs_1_ = bf16[128,512]{1,0:T(8,128)(2,1)S(1)} collective-permute-done((bf16[128,512]{1,0:T(8,128)(2,1)}, bf16[128,512]{1,0:T(8,128)(2,1)S(1)}, u32[]{:S(2)}, u32[]{:S(2)}) %collective-permute-start) | collective-permute-done | bytes 131104 | tf_op jit(solution)/shard_map/ppermute | solution.py:125
  10.2 0.0 collective-permute-start.5
  10.2 0.0 collective-permute-done.1.refs_2_
  10.2 3.6 %collective-permute-start.6 = (bf16[128,512]{1,0:T(8,128)(2,1)}, bf16[128,512]{1,0:T(8,128)(2,1)S(1)}, u32[]{:S(2)}, u32[]{:S(2)}) collective-permute-start(bf16[128,512]{1,0:T(8,128)(2,1)} %get-tuple-element.26), channel_id=1, source_target_pairs={{0,28},{4,24},{8,20},{12,16},{16,12},{20,8},{24,4},{28,0},{1,29},{... | collective-permute-start | bytes 393224 | tf_op jit(solution)/shard_map/ppermute | solution.py:125
  13.8 0.6 %collective-permute-done.2.refs_3_ = bf16[128,512]{1,0:T(8,128)(2,1)S(1)} collective-permute-done((bf16[128,512]{1,0:T(8,128)(2,1)}, bf16[128,512]{1,0:T(8,128)(2,1)S(1)}, u32[]{:S(2)}, u32[]{:S(2)}) %collective-permute-start.2) | collective-permute-done | bytes 131104 | tf_op jit(solution)/shard_map/ppermute | solution.py:125
  14.4 0.0 collective-permute-done.3.refs_4_
  14.4 2.3 %collective-permute-done.4.refs_5_ = bf16[128,512]{1,0:T(8,128)(2,1)S(1)} collective-permute-done((bf16[128,512]{1,0:T(8,128)(2,1)}, bf16[128,512]{1,0:T(8,128)(2,1)S(1)}, u32[]{:S(2)}, u32[]{:S(2)}) %collective-permute-start.4) | collective-permute-done | bytes 131104 | tf_op jit(solution)/shard_map/ppermute | solution.py:125
  16.7 1.2 %collective-permute-done.5.refs_6_ = bf16[128,512]{1,0:T(8,128)(2,1)S(1)} collective-permute-done((bf16[128,512]{1,0:T(8,128)(2,1)}, bf16[128,512]{1,0:T(8,128)(2,1)S(1)}, u32[]{:S(2)}, u32[]{:S(2)}) %collective-permute-start.5) | collective-permute-done | bytes 131104 | tf_op jit(solution)/shard_map/ppermute | solution.py:125
  18.0 3.0 %collective-permute-done.6.refs_7_ = bf16[128,512]{1,0:T(8,128)(2,1)S(1)} collective-permute-done((bf16[128,512]{1,0:T(8,128)(2,1)}, bf16[128,512]{1,0:T(8,128)(2,1)S(1)}, u32[]{:S(2)}, u32[]{:S(2)}) %collective-permute-start.6) | collective-permute-done | bytes 131104 | tf_op jit(solution)/shard_map/ppermute | solution.py:125
  20.9 0.9 %copy-done = bf16[128,512]{1,0:T(8,128)(2,1)S(1)} copy-done((bf16[128,512]{1,0:T(8,128)(2,1)S(1)}, bf16[128,512]{1,0:T(8,128)(2,1)}, u32[]{:S(2)}) %copy-start) | copy-done | bytes 131096
  21.8 4.2 %attention.1 = (bf16[128,384]{1,0:T(8,128)(2,1)S(1)}, bf16[128,384]{1,0:T(8,128)(2,1)S(1)}, bf16[128,384]{1,0:T(8,128)(2,1)S(1)}, bf16[128,384]{1,0:T(8,128)(2,1...) custom-call(s32[1]{0:T(128)} %bitcast.here_ref, ...), custom_call_target="tpu_custom_call" | custom-call | tf_op jit(solution)/shard_map/attention/pallas_call | solution.py:248
  26.0 0.6 %copy-done.1 = bf16[128,384]{1,0:T(8,128)(2,1)} copy-done((bf16[128,384]{1,0:T(8,128)(2,1)}, bf16[128,384]{1,0:T(8,128)(2,1)S(1)}, u32[]{:S(2)}) %copy-start.1) | copy-done | bytes 98328
  26.7 0.4 collective-permute-start.7
  27.1 0.3 collective-permute-start.8
  27.3 1.4 %collective-permute-start.9 = (bf16[128,384]{1,0:T(8,128)(2,1)S(1)}, bf16[128,384]{1,0:T(8,128)(2,1)S(1)}, u32[]{:S(2)}, u32[]{:S(2)}) collective-permute-start(bf16[128,384]{1,0:T(8,128)(2,1)S(1)} %get-tuple-element.30), channel_id=1, source_target_pairs={{0,12},{4,8},{8,4},{12,0},{16,28},{20,24},{24,20},{28,16},{1,13},{... | collective-permute-start | bytes 294920 | tf_op jit(solution)/shard_map/ppermute | solution.py:125
  28.8 1.5 %collective-permute-start.10 = (bf16[128,384]{1,0:T(8,128)(2,1)S(1)}, bf16[128,384]{1,0:T(8,128)(2,1)S(1)}, u32[]{:S(2)}, u32[]{:S(2)}) collective-permute-start(bf16[128,384]{1,0:T(8,128)(2,1)S(1)} %get-tuple-element.31), channel_id=1, source_target_pairs={{0,16},{4,20},{8,24},{12,28},{16,0},{20,4},{24,8},{28,12},{1,17},{... | collective-permute-start | bytes 294920 | tf_op jit(solution)/shard_map/ppermute | solution.py:125
  30.3 0.4 collective-permute-start.11
  30.7 1.6 %collective-permute-done.7.refs_1_ = bf16[128,384]{1,0:T(8,128)(2,1)S(1)} collective-permute-done((bf16[128,384]{1,0:T(8,128)(2,1)S(1)}, bf16[128,384]{1,0:T(8,128)(2,1)S(1)}, u32[]{:S(2)}, u32[]{:S(2)}) %collective-permute-start.7) | collective-permute-done | bytes 98336 | tf_op jit(solution)/shard_map/ppermute | solution.py:125
  32.2 0.5 %collective-permute-start.12 = (bf16[128,384]{1,0:T(8,128)(2,1)S(1)}, bf16[128,384]{1,0:T(8,128)(2,1)S(1)}, u32[]{:S(2)}, u32[]{:S(2)}) collective-permute-start(bf16[128,384]{1,0:T(8,128)(2,1)S(1)} %get-tuple-element.33), channel_id=1, source_target_pairs={{0,24},{4,28},{8,16},{12,20},{16,8},{20,12},{24,0},{28,4},{1,25},{... | collective-permute-start | bytes 294920 | tf_op jit(solution)/shard_map/ppermute | solution.py:125
  32.7 1.1 %collective-permute-start.13 = (bf16[128,384]{1,0:T(8,128)(2,1)S(1)}, bf16[128,384]{1,0:T(8,128)(2,1)S(1)}, u32[]{:S(2)}, u32[]{:S(2)}) collective-permute-start(bf16[128,384]{1,0:T(8,128)(2,1)S(1)} %get-tuple-element.34), channel_id=1, source_target_pairs={{0,28},{4,24},{8,20},{12,16},{16,12},{20,8},{24,4},{28,0},{1,29},{... | collective-permute-start | bytes 294920 | tf_op jit(solution)/shard_map/ppermute | solution.py:125
  33.8 0.6 %collective-permute-done.10.refs_4_ = bf16[128,384]{1,0:T(8,128)(2,1)S(1)} collective-permute-done((bf16[128,384]{1,0:T(8,128)(2,1)S(1)}, bf16[128,384]{1,0:T(8,128)(2,1)S(1)}, u32[]{:S(2)}, u32[]{:S(2)}) %collective-permute-start.10) | collective-permute-done | bytes 98336 | tf_op jit(solution)/shard_map/ppermute | solution.py:125
  34.4 2.3 %collective-permute-done.11.refs_5_ = bf16[128,384]{1,0:T(8,128)(2,1)S(1)} collective-permute-done((bf16[128,384]{1,0:T(8,128)(2,1)S(1)}, bf16[128,384]{1,0:T(8,128)(2,1)S(1)}, u32[]{:S(2)}, u32[]{:S(2)}) %collective-permute-start.11) | collective-permute-done | bytes 98336 | tf_op jit(solution)/shard_map/ppermute | solution.py:125
  36.7 0.8 %collective-permute-done.12.refs_6_ = bf16[128,384]{1,0:T(8,128)(2,1)S(1)} collective-permute-done((bf16[128,384]{1,0:T(8,128)(2,1)S(1)}, bf16[128,384]{1,0:T(8,128)(2,1)S(1)}, u32[]{:S(2)}, u32[]{:S(2)}) %collective-permute-start.12) | collective-permute-done | bytes 98336 | tf_op jit(solution)/shard_map/ppermute | solution.py:125
  37.5 1.7 %collective-permute-done.13.refs_7_ = bf16[128,384]{1,0:T(8,128)(2,1)S(1)} collective-permute-done((bf16[128,384]{1,0:T(8,128)(2,1)S(1)}, bf16[128,384]{1,0:T(8,128)(2,1)S(1)}, u32[]{:S(2)}, u32[]{:S(2)}) %collective-permute-start.13) | collective-permute-done | bytes 98336 | tf_op jit(solution)/shard_map/ppermute | solution.py:125
  39.3 0.6 %copy-done.9 = bf16[128,384]{1,0:T(8,128)(2,1)} copy-done((bf16[128,384]{1,0:T(8,128)(2,1)}, bf16[128,384]{1,0:T(8,128)(2,1)S(1)}, u32[]{:S(2)}) %copy-start.9) | copy-done | bytes 98328
  39.9 2.3 %unpack.1 = (bf16[128,1024]{1,0:T(8,128)(2,1)}, bf16[128,1024]{1,0:T(8,128)(2,1)}, bf16[128,1024]{1,0:T(8,128)(2,1)}) custom-call(s32[1]{0:T(128)} %bitcast.here_ref, bf16[128,384]{1,0:T(8,128)(2,1)} %copy-done.1, bf16[128,384]{1,0:T(8,128)(2,1)} %copy-done.3, bf16[128,384]{1,0:T(8,128)(2,1)} %copy-done.4, bf16[128,384]{1,0:T(8,128)(2,1)} %copy-done.5, ...), custom_call_target="tpu_custom_call" | custom-call | tf_op jit(solution)/shard_map/unpack/pallas_call | solution.py:259
  (19 shorter events, 0.0 us)
Async XLA Ops:
  3.1 7.2 %collective-permute-start = (bf16[128,512]{1,0:T(8,128)(2,1)}, bf16[128,512]{1,0:T(8,128)(2,1)S(1)}, u32[]{:S(2)}, u32[]{:S(2)}) collective-permute-start(bf16[128,512]{1,0:T(8,128)(2,1)} %get-tuple-element.20), channel_id=1, source_target_pairs={{0,4},{4,0},{8,12},{12,8},{16,20},{20,16},{24,28},{28,24},{1,5},{5... | collective-permute-start | bytes 393224 | tf_op jit(solution)/shard_map/ppermute | solution.py:125
  6.0 4.2 %collective-permute-start.1 = (bf16[128,512]{1,0:T(8,128)(2,1)}, bf16[128,512]{1,0:T(8,128)(2,1)S(1)}, u32[]{:S(2)}, u32[]{:S(2)}) collective-permute-start(bf16[128,512]{1,0:T(8,128)(2,1)} %get-tuple-element.21), channel_id=1, source_target_pairs={{0,8},{4,12},{8,0},{12,4},{16,24},{20,28},{24,16},{28,20},{1,9},{5... | collective-permute-start | bytes 393224 | tf_op jit(solution)/shard_map/ppermute | solution.py:125
  6.0 8.4 %collective-permute-start.2 = (bf16[128,512]{1,0:T(8,128)(2,1)}, bf16[128,512]{1,0:T(8,128)(2,1)S(1)}, u32[]{:S(2)}, u32[]{:S(2)}) collective-permute-start(bf16[128,512]{1,0:T(8,128)(2,1)} %get-tuple-element.22), channel_id=1, source_target_pairs={{0,12},{4,8},{8,4},{12,0},{16,28},{20,24},{24,20},{28,16},{1,13},{... | collective-permute-start | bytes 393224 | tf_op jit(solution)/shard_map/ppermute | solution.py:125
  6.2 14.7 %copy-start.2 = (s32[8,8]{1,0:T(8,128)S(1)}, s32[8,8]{1,0:T(8,128)}, u32[]{:S(2)}) copy-start(s32[8,8]{1,0:T(8,128)} %mask_ref.1) | copy-start | bytes 772
  6.2 8.2 %collective-permute-start.3 = (bf16[128,512]{1,0:T(8,128)(2,1)}, bf16[128,512]{1,0:T(8,128)(2,1)S(1)}, u32[]{:S(2)}, u32[]{:S(2)}) collective-permute-start(bf16[128,512]{1,0:T(8,128)(2,1)} %get-tuple-element.23), channel_id=1, source_target_pairs={{0,16},{4,20},{8,24},{12,28},{16,0},{20,4},{24,8},{28,12},{1,17},{... | collective-permute-start | bytes 393224 | tf_op jit(solution)/shard_map/ppermute | solution.py:125
  8.1 8.6 %collective-permute-start.4 = (bf16[128,512]{1,0:T(8,128)(2,1)}, bf16[128,512]{1,0:T(8,128)(2,1)S(1)}, u32[]{:S(2)}, u32[]{:S(2)}) collective-permute-start(bf16[128,512]{1,0:T(8,128)(2,1)} %get-tuple-element.24), channel_id=1, source_target_pairs={{0,20},{4,16},{8,28},{12,24},{16,4},{20,0},{24,12},{28,8},{1,21},{... | collective-permute-start | bytes 393224 | tf_op jit(solution)/shard_map/ppermute | solution.py:125
  10.2 7.7 %collective-permute-start.5 = (bf16[128,512]{1,0:T(8,128)(2,1)}, bf16[128,512]{1,0:T(8,128)(2,1)S(1)}, u32[]{:S(2)}, u32[]{:S(2)}) collective-permute-start(bf16[128,512]{1,0:T(8,128)(2,1)} %get-tuple-element.25), channel_id=1, source_target_pairs={{0,24},{4,28},{8,16},{12,20},{16,8},{20,12},{24,0},{28,4},{1,25},{... | collective-permute-start | bytes 393224 | tf_op jit(solution)/shard_map/ppermute | solution.py:125
  10.2 10.7 %collective-permute-start.6 = (bf16[128,512]{1,0:T(8,128)(2,1)}, bf16[128,512]{1,0:T(8,128)(2,1)S(1)}, u32[]{:S(2)}, u32[]{:S(2)}) collective-permute-start(bf16[128,512]{1,0:T(8,128)(2,1)} %get-tuple-element.26), channel_id=1, source_target_pairs={{0,28},{4,24},{8,20},{12,16},{16,12},{20,8},{24,4},{28,0},{1,29},{... | collective-permute-start | bytes 393224 | tf_op jit(solution)/shard_map/ppermute | solution.py:125
  20.9 0.9 %copy-start = (bf16[128,512]{1,0:T(8,128)(2,1)S(1)}, bf16[128,512]{1,0:T(8,128)(2,1)}, u32[]{:S(2)}) copy-start(bf16[128,512]{1,0:T(8,128)(2,1)} %get-tuple-element.19.refs_0_) | copy-start | bytes 393220
  26.0 0.6 %copy-start.1 = (bf16[128,384]{1,0:T(8,128)(2,1)}, bf16[128,384]{1,0:T(8,128)(2,1)S(1)}, u32[]{:S(2)}) copy-start(bf16[128,384]{1,0:T(8,128)(2,1)S(1)} %get-tuple-element.27.refs_0_) | copy-start | bytes 294916
  26.7 5.6 %collective-permute-start.7 = (bf16[128,384]{1,0:T(8,128)(2,1)S(1)}, bf16[128,384]{1,0:T(8,128)(2,1)S(1)}, u32[]{:S(2)}, u32[]{:S(2)}) collective-permute-start(bf16[128,384]{1,0:T(8,128)(2,1)S(1)} %get-tuple-element.28), channel_id=1, source_target_pairs={{0,4},{4,0},{8,12},{12,8},{16,20},{20,16},{24,28},{28,24},{1,5},{5... | collective-permute-start | bytes 294920 | tf_op jit(solution)/shard_map/ppermute | solution.py:125
  27.1 5.7 %collective-permute-start.8 = (bf16[128,384]{1,0:T(8,128)(2,1)S(1)}, bf16[128,384]{1,0:T(8,128)(2,1)S(1)}, u32[]{:S(2)}, u32[]{:S(2)}) collective-permute-start(bf16[128,384]{1,0:T(8,128)(2,1)S(1)} %get-tuple-element.29), channel_id=1, source_target_pairs={{0,8},{4,12},{8,0},{12,4},{16,24},{20,28},{24,16},{28,20},{1,9},{5... | collective-permute-start | bytes 294920 | tf_op jit(solution)/shard_map/ppermute | solution.py:125
  27.3 6.5 %collective-permute-start.9 = (bf16[128,384]{1,0:T(8,128)(2,1)S(1)}, bf16[128,384]{1,0:T(8,128)(2,1)S(1)}, u32[]{:S(2)}, u32[]{:S(2)}) collective-permute-start(bf16[128,384]{1,0:T(8,128)(2,1)S(1)} %get-tuple-element.30), channel_id=1, source_target_pairs={{0,12},{4,8},{8,4},{12,0},{16,28},{20,24},{24,20},{28,16},{1,13},{... | collective-permute-start | bytes 294920 | tf_op jit(solution)/shard_map/ppermute | solution.py:125
  28.8 5.6 %collective-permute-start.10 = (bf16[128,384]{1,0:T(8,128)(2,1)S(1)}, bf16[128,384]{1,0:T(8,128)(2,1)S(1)}, u32[]{:S(2)}, u32[]{:S(2)}) collective-permute-start(bf16[128,384]{1,0:T(8,128)(2,1)S(1)} %get-tuple-element.31), channel_id=1, source_target_pairs={{0,16},{4,20},{8,24},{12,28},{16,0},{20,4},{24,8},{28,12},{1,17},{... | collective-permute-start | bytes 294920 | tf_op jit(solution)/shard_map/ppermute | solution.py:125
  30.3 6.5 %collective-permute-start.11 = (bf16[128,384]{1,0:T(8,128)(2,1)S(1)}, bf16[128,384]{1,0:T(8,128)(2,1)S(1)}, u32[]{:S(2)}, u32[]{:S(2)}) collective-permute-start(bf16[128,384]{1,0:T(8,128)(2,1)S(1)} %get-tuple-element.32), channel_id=1, source_target_pairs={{0,20},{4,16},{8,28},{12,24},{16,4},{20,0},{24,12},{28,8},{1,21},{... | collective-permute-start | bytes 294920 | tf_op jit(solution)/shard_map/ppermute | solution.py:125
  32.2 7.0 %copy-start.3 = (bf16[128,384]{1,0:T(8,128)(2,1)}, bf16[128,384]{1,0:T(8,128)(2,1)S(1)}, u32[]{:S(2)}) copy-start(bf16[128,384]{1,0:T(8,128)(2,1)S(1)} %collective-permute-done.7.refs_1_) | copy-start | bytes 294916
  32.2 5.3 %collective-permute-start.12 = (bf16[128,384]{1,0:T(8,128)(2,1)S(1)}, bf16[128,384]{1,0:T(8,128)(2,1)S(1)}, u32[]{:S(2)}, u32[]{:S(2)}) collective-permute-start(bf16[128,384]{1,0:T(8,128)(2,1)S(1)} %get-tuple-element.33), channel_id=1, source_target_pairs={{0,24},{4,28},{8,16},{12,20},{16,8},{20,12},{24,0},{28,4},{1,25},{... | collective-permute-start | bytes 294920 | tf_op jit(solution)/shard_map/ppermute | solution.py:125
  32.7 6.5 %copy-start.4 = (bf16[128,384]{1,0:T(8,128)(2,1)}, bf16[128,384]{1,0:T(8,128)(2,1)S(1)}, u32[]{:S(2)}) copy-start(bf16[128,384]{1,0:T(8,128)(2,1)S(1)} %collective-permute-done.8.refs_2_) | copy-start | bytes 294916
  32.7 6.5 %collective-permute-start.13 = (bf16[128,384]{1,0:T(8,128)(2,1)S(1)}, bf16[128,384]{1,0:T(8,128)(2,1)S(1)}, u32[]{:S(2)}, u32[]{:S(2)}) collective-permute-start(bf16[128,384]{1,0:T(8,128)(2,1)S(1)} %get-tuple-element.34), channel_id=1, source_target_pairs={{0,28},{4,24},{8,20},{12,16},{16,12},{20,8},{24,4},{28,0},{1,29},{... | collective-permute-start | bytes 294920 | tf_op jit(solution)/shard_map/ppermute | solution.py:125
  33.8 5.5 %copy-start.5 = (bf16[128,384]{1,0:T(8,128)(2,1)}, bf16[128,384]{1,0:T(8,128)(2,1)S(1)}, u32[]{:S(2)}) copy-start(bf16[128,384]{1,0:T(8,128)(2,1)S(1)} %collective-permute-done.9.refs_3_) | copy-start | bytes 294916
  34.4 4.9 %copy-start.6 = (bf16[128,384]{1,0:T(8,128)(2,1)}, bf16[128,384]{1,0:T(8,128)(2,1)S(1)}, u32[]{:S(2)}) copy-start(bf16[128,384]{1,0:T(8,128)(2,1)S(1)} %collective-permute-done.10.refs_4_) | copy-start | bytes 294916
  36.7 2.6 %copy-start.7 = (bf16[128,384]{1,0:T(8,128)(2,1)}, bf16[128,384]{1,0:T(8,128)(2,1)S(1)}, u32[]{:S(2)}) copy-start(bf16[128,384]{1,0:T(8,128)(2,1)S(1)} %collective-permute-done.11.refs_5_) | copy-start | bytes 294916
  37.5 1.8 %copy-start.8 = (bf16[128,384]{1,0:T(8,128)(2,1)}, bf16[128,384]{1,0:T(8,128)(2,1)S(1)}, u32[]{:S(2)}) copy-start(bf16[128,384]{1,0:T(8,128)(2,1)S(1)} %collective-permute-done.12.refs_6_) | copy-start | bytes 294916
  39.3 0.6 %copy-start.9 = (bf16[128,384]{1,0:T(8,128)(2,1)}, bf16[128,384]{1,0:T(8,128)(2,1)S(1)}, u32[]{:S(2)}) copy-start(bf16[128,384]{1,0:T(8,128)(2,1)S(1)} %collective-permute-done.13.refs_7_) | copy-start | bytes 294916

commit v2 on v1

--- a/solution.py
+++ b/solution.py
@@ -1,3 +1,4 @@
+import functools
 import math
 
 import jax
@@ -8,6 +9,7 @@
 from jax.sharding import PartitionSpec as P
 
 HEAD_DIM = 128
+MIB = 1024 * 1024
 GROUP = ("blk", "uly")
 ORDER = (5, 7, 4, 6, 1, 3, 2)
 
@@ -129,27 +131,42 @@
     return pl.ds(pl.multiple_of(head * HEAD_DIM, HEAD_DIM), HEAD_DIM)
 
 
-def pack_kernel(here_ref, *refs):
-    arrays, slabs = refs[:4], refs[4:]
-    for distance, slab in enumerate(slabs):
-        columns = head_columns(here_ref[0] ^ distance)
+def pack_kernel(distances, *refs):
+    arrays, slabs, sems = refs[:4], refs[4:-1], refs[-1]
+    here = flat_index(GROUP)
+    copies = []
+    for i, (distance, slab) in enumerate(zip(distances, slabs)):
+        columns = head_columns(here ^ distance)
         for n, array in enumerate(arrays):
-            slab[:, n * HEAD_DIM : (n + 1) * HEAD_DIM] = array[:, columns]
-
-
-def unpack_kernel(here_ref, *refs):
-    slabs, arrays = refs[:-3], refs[-3:]
-    for distance, slab in enumerate(slabs):
-        columns = head_columns(here_ref[0] ^ distance)
+            into = slab.at[:, n * HEAD_DIM : (n + 1) * HEAD_DIM]
+            copies.append(pltpu.make_async_copy(array.at[:, columns], into, sems.at[i, n]))
+    for copy in copies:
+        copy.start()
+    for copy in copies:
+        copy.wait()
+
+
+def unpack_kernel(distances, *refs):
+    slabs, arrays, sems = refs[:-4], refs[-4:-1], refs[-1]
+    here = flat_index(GROUP)
+    copies = []
+    for i, (distance, slab) in enumerate(zip(distances, slabs)):
+        columns = head_columns(here ^ distance)
         for n, array in enumerate(arrays):
-            array[:, columns] = slab[:, n * HEAD_DIM : (n + 1) * HEAD_DIM]
-
-
-def attention_kernel(here_ref, mask_ref, *refs):
-    count = len(refs) // 2
-    slabs, outs = refs[:count], refs[count:]
+            part = slab.at[:, n * HEAD_DIM : (n + 1) * HEAD_DIM]
+            copies.append(pltpu.make_async_copy(part, array.at[:, columns], sems.at[i, n]))
+    for copy in copies:
+        copy.start()
+    for copy in copies:
+        copy.wait()
+
+
+def attention_kernel(order, mask_ref, *refs):
+    count = len(order)
+    slabs = [refs[order.index(distance)] for distance in range(count)]
+    outs = [refs[count + order.index(distance)] for distance in range(count)]
     scale = 1.0 / math.sqrt(HEAD_DIM)
-    here = here_ref[0]
+    here = flat_index(GROUP)
     cells = count // 2
 
     def cell(c, n):
@@ -226,43 +243,52 @@
 
 SMEM = pl.BlockSpec(memory_space=pltpu.SMEM)
 VMEM = pl.BlockSpec(memory_space=pltpu.VMEM)
+ANY = pl.BlockSpec(memory_space=pl.ANY)
+
+
+def pack(arrays, distances, name):
+    tokens = arrays[0].shape[0]
+    return pl.pallas_call(
+        functools.partial(pack_kernel, distances),
+        out_shape=[jax.ShapeDtypeStruct((tokens, 4 * HEAD_DIM), jnp.bfloat16)] * len(distances),
+        in_specs=[ANY] * 4,
+        out_specs=[ANY] * len(distances),
+        scratch_shapes=[pltpu.SemaphoreType.DMA((len(distances), 4))],
+        compiler_params=pltpu.CompilerParams(vmem_limit_bytes=MIB),
+        name=name,
+    )(*arrays)
 
 
 def by_heads(queries, keys, values, out_grad, block_mask):
     devices = lax.axis_size(GROUP)
     tokens = queries.shape[0]
-    here = flat_index(GROUP).astype(jnp.int32).reshape(1)
-    slab = jax.ShapeDtypeStruct((tokens, 4 * HEAD_DIM), jnp.bfloat16)
-    out_slab = jax.ShapeDtypeStruct((tokens, 3 * HEAD_DIM), jnp.bfloat16)
-    sent = pl.pallas_call(
-        pack_kernel,
-        out_shape=[slab] * devices,
-        in_specs=[SMEM] + [VMEM] * 4,
+    arrays = [
+        pltpu.with_memory_space_constraint(array, pltpu.HBM)
+        for array in (queries, keys, values, out_grad)
+    ]
+    sent = {}
+    for distances, name in ((ORDER[:2], "pack_first"), (ORDER[2:] + (0,), "pack_rest")):
+        sent.update(zip(distances, pack(arrays, distances, name)))
+    order = ORDER + (0,)
+    got = [exchange(sent[distance], distance) for distance in ORDER] + [sent[0]]
+    grads = pl.pallas_call(
+        functools.partial(attention_kernel, order),
+        out_shape=[jax.ShapeDtypeStruct((tokens, 3 * HEAD_DIM), jnp.bfloat16)] * devices,
+        in_specs=[SMEM] + [VMEM] * devices,
         out_specs=[VMEM] * devices,
-        name="pack",
-    )(here, queries, keys, values, out_grad)
-    order = ORDER
-    got = [sent[0]] + [None] * (devices - 1)
-    for distance in order:
-        got[distance] = exchange(sent[distance], distance)
-    grads = pl.pallas_call(
-        attention_kernel,
-        out_shape=[out_slab] * devices,
-        in_specs=[SMEM, SMEM] + [VMEM] * devices,
-        out_specs=[VMEM] * devices,
-        compiler_params=pltpu.CompilerParams(vmem_limit_bytes=40 * 1024 * 1024),
+        compiler_params=pltpu.CompilerParams(vmem_limit_bytes=40 * MIB),
         name="attention",
-    )(here, block_mask, *got)
-    back = [grads[0]] + [None] * (devices - 1)
-    for distance in order:
-        back[distance] = exchange(grads[distance], distance)
+    )(block_mask, *got)
+    back = [exchange(grad, distance) for grad, distance in zip(grads, ORDER)] + [grads[-1]]
     return pl.pallas_call(
-        unpack_kernel,
+        functools.partial(unpack_kernel, order),
         out_shape=[jax.ShapeDtypeStruct(queries.shape, queries.dtype)] * 3,
-        in_specs=[SMEM] + [VMEM] * devices,
-        out_specs=[VMEM] * 3,
+        in_specs=[ANY] * devices,
+        out_specs=[ANY] * 3,
+        scratch_shapes=[pltpu.SemaphoreType.DMA((devices, 3))],
+        compiler_params=pltpu.CompilerParams(vmem_limit_bytes=MIB),
         name="unpack",
-    )(here, *back)
+    )(*back)
 
 
 def local(queries, keys, values, out_grad, block_mask):

time: 42.6 us -> 35.6 us (0.84)
  waiting for transfers between devices: 14.8 us -> 12.5 us
  local copies, waits for them, and re-layouts: 2.15 us -> 0.01 us
  Pallas kernels: 8.9 us -> 7.61 us
  starting transfers between devices: 15.7 us -> 14.5 us
    ppermute x14, waiting for transfers between devices: 14.8 us -> 12.5 us  [exchange(): lax.ppermute(block, GROUP, [(i, i ^ distance) for i in range(devices)])]
    unnamed x20 -> x2, local copies, waits for them, and re-layouts: 2.15 us -> 0.01 us
    pallas_call x3 -> x4, Pallas kernels: 8.9 us -> 7.61 us  [the longest x1 4.27 us: by_heads(): pl.pallas_call(functools.partial(attention_kernel, order), out_shape=[jax...]
    ppermute x14, starting transfers between devices: 15.7 us -> 14.5 us  [exchange(): lax.ppermute(block, GROUP, [(i, i ^ distance) for i in range(devices)])]
  transfers between devices with their start and end apart: 14 -> 14, of which waited for: 10 -> 9; matrix products, arithmetic and copies ran while one was open for 0% -> 0% of each run, Pallas kernels for 0% -> 4%
where the time goes in v2:
time: 35.6 us; the launch traced here: 35.3 us
  starting transfers between devices  14.5 us (41%)
  waiting for transfers between devices  12.5 us (35%)
  Pallas kernels  7.61 us (21%)
  between operations  0.67 us (2%)
    ppermute x14, starting transfers between devices, exchange(): lax.ppermute(block, GROUP, [(i, i ^ distance) for i in range(devices)])  14.5 us
    ppermute x14, waiting for transfers between devices, exchange(): lax.ppermute(block, GROUP, [(i, i ^ distance) for i in range(devices)])  12.5 us
    pallas_call x1, Pallas kernels, by_heads(): pl.pallas_call(functools.partial(attention_kernel, order), out_shape=[jax...  4.27 us
    pallas_call x2, Pallas kernels, pack(): pl.pallas_call(functools.partial(pack_kernel, distances), out_shape=[jax....  2.27 us
    pallas_call x1, Pallas kernels, by_heads(): pl.pallas_call(functools.partial(unpack_kernel, order), out_shape=[jax.Sh...  1.07 us
  transfers between devices with their start and end apart: 14, of which 9 were waited for; matrix products, arithmetic and copies ran while one was open for 0% of the time, Pallas kernels for 4%

profile of v2, /device:TPU:0, one launch (start us, length us, event | category | flops | bytes accessed | tf_op | source)
XLA Modules:
  0.0 35.3 jit_solution(11471141336879804966)
XLA Ops:
  0.6 1.0 %pack_first.1 = (bf16[128,512]{1,0:T(8,128)(2,1)S(1)}, bf16[128,512]{1,0:T(8,128)(2,1)S(1)}) custom-call(bf16[128,1024]{1,0:T(8,128)(2,1)} %refs_0_.3, bf16[128,1024]{1,0:T(8,128)(2,1)} %refs_1_.3, bf16[128,1024]{1,0:T(8,128)(2,1)} %refs_2_.3, bf16[128,1024]{1,0:T(8,128)(2,1)} %refs_3_.3), custom_call_target="tpu_custom_call" | custom-call | tf_op jit(solution)/shard_map/pack_first/pallas_call | solution.py:251
  1.6 4.0 %collective-permute-start = (bf16[128,512]{1,0:T(8,128)(2,1)S(1)}, bf16[128,512]{1,0:T(8,128)(2,1)S(1)}, u32[]{:S(2)}, u32[]{:S(2)}) collective-permute-start(bf16[128,512]{1,0:T(8,128)(2,1)S(1)} %get-tuple-element.19), channel_id=1, source_target_pairs={{0,20},{4,16},{8,28},{12,24},{16,4},{20,0},{24,12},{28,8},{1,21},{... | collective-permute-start | bytes 393224 | tf_op jit(solution)/shard_map/ppermute | solution.py:127
  5.6 0.0 collective-permute-start.1
  5.6 1.3 %pack_rest.1 = (bf16[128,512]{1,0:T(8,128)(2,1)S(1)}, bf16[128,512]{1,0:T(8,128)(2,1)S(1)}, bf16[128,512]{1,0:T(8,128)(2,1)S(1)}, bf16[128,512]{1,0:T(8,128)(2,1...) custom-call(bf16[128,1024]{1,0:T(8,128)(2,1)} %refs_0_.3, bf16[128,1024]{1,0:T(8,128)(2,1)} %refs_1_.3, ...), custom_call_target="tpu_custom_call" | custom-call | tf_op jit(solution)/shard_map/pack_rest/pallas_call | solution.py:251
  6.9 1.2 %collective-permute-start.2 = (bf16[128,512]{1,0:T(8,128)(2,1)S(1)}, bf16[128,512]{1,0:T(8,128)(2,1)S(1)}, u32[]{:S(2)}, u32[]{:S(2)}) collective-permute-start(bf16[128,512]{1,0:T(8,128)(2,1)S(1)} %get-tuple-element.21), channel_id=1, source_target_pairs={{0,16},{4,20},{8,24},{12,28},{16,0},{20,4},{24,8},{28,12},{1,17},{... | collective-permute-start | bytes 393224 | tf_op jit(solution)/shard_map/ppermute | solution.py:127
  8.1 0.6 %collective-permute-start.3 = (bf16[128,512]{1,0:T(8,128)(2,1)S(1)}, bf16[128,512]{1,0:T(8,128)(2,1)S(1)}, u32[]{:S(2)}, u32[]{:S(2)}) collective-permute-start(bf16[128,512]{1,0:T(8,128)(2,1)S(1)} %get-tuple-element.22), channel_id=1, source_target_pairs={{0,24},{4,28},{8,16},{12,20},{16,8},{20,12},{24,0},{28,4},{1,25},{... | collective-permute-start | bytes 393224 | tf_op jit(solution)/shard_map/ppermute | solution.py:127
  8.7 1.7 %collective-permute-start.4 = (bf16[128,512]{1,0:T(8,128)(2,1)S(1)}, bf16[128,512]{1,0:T(8,128)(2,1)S(1)}, u32[]{:S(2)}, u32[]{:S(2)}) collective-permute-start(bf16[128,512]{1,0:T(8,128)(2,1)S(1)} %get-tuple-element.23), channel_id=1, source_target_pairs={{0,4},{4,0},{8,12},{12,8},{16,20},{20,16},{24,28},{28,24},{1,5},{5... | collective-permute-start | bytes 393224 | tf_op jit(solution)/shard_map/ppermute | solution.py:127
  10.4 0.0 collective-permute-done.refs_0_
  10.4 0.0 collective-permute-start.5
  10.5 1.8 %collective-permute-done.1.refs_1_ = bf16[128,512]{1,0:T(8,128)(2,1)S(1)} collective-permute-done((bf16[128,512]{1,0:T(8,128)(2,1)S(1)}, bf16[128,512]{1,0:T(8,128)(2,1)S(1)}, u32[]{:S(2)}, u32[]{:S(2)}) %collective-permute-start.1) | collective-permute-done | bytes 131104 | tf_op jit(solution)/shard_map/ppermute | solution.py:127
  12.3 0.0 collective-permute-start.6
  12.3 3.5 %collective-permute-done.2.refs_2_ = bf16[128,512]{1,0:T(8,128)(2,1)S(1)} collective-permute-done((bf16[128,512]{1,0:T(8,128)(2,1)S(1)}, bf16[128,512]{1,0:T(8,128)(2,1)S(1)}, u32[]{:S(2)}, u32[]{:S(2)}) %collective-permute-start.2) | collective-permute-done | bytes 131104 | tf_op jit(solution)/shard_map/ppermute | solution.py:127
  15.8 1.1 %collective-permute-done.3.refs_3_ = bf16[128,512]{1,0:T(8,128)(2,1)S(1)} collective-permute-done((bf16[128,512]{1,0:T(8,128)(2,1)S(1)}, bf16[128,512]{1,0:T(8,128)(2,1)S(1)}, u32[]{:S(2)}, u32[]{:S(2)}) %collective-permute-start.3) | collective-permute-done | bytes 131104 | tf_op jit(solution)/shard_map/ppermute | solution.py:127
  16.9 0.0 collective-permute-done.4.refs_4_
  16.9 0.4 %collective-permute-done.5.refs_5_ = bf16[128,512]{1,0:T(8,128)(2,1)S(1)} collective-permute-done((bf16[128,512]{1,0:T(8,128)(2,1)S(1)}, bf16[128,512]{1,0:T(8,128)(2,1)S(1)}, u32[]{:S(2)}, u32[]{:S(2)}) %collective-permute-start.5) | collective-permute-done | bytes 131104 | tf_op jit(solution)/shard_map/ppermute | solution.py:127
  17.3 0.0 collective-permute-done.6.refs_6_
  17.3 4.3 %attention.1 = (bf16[128,384]{1,0:T(8,128)(2,1)S(1)}, bf16[128,384]{1,0:T(8,128)(2,1)S(1)}, bf16[128,384]{1,0:T(8,128)(2,1)S(1)}, bf16[128,384]{1,0:T(8,128)(2,1...) custom-call(s32[8,8]{1,0:T(8,128)S(1)} %copy-done, ...), custom_call_target="tpu_custom_call" | custom-call | tf_op jit(solution)/shard_map/attention/pallas_call | solution.py:274
  21.6 2.5 %collective-permute-start.7 = (bf16[128,384]{1,0:T(8,128)(2,1)S(1)}, bf16[128,384]{1,0:T(8,128)(2,1)S(1)}, u32[]{:S(2)}, u32[]{:S(2)}) collective-permute-start(bf16[128,384]{1,0:T(8,128)(2,1)S(1)} %get-tuple-element.27), channel_id=1, source_target_pairs={{0,20},{4,16},{8,28},{12,24},{16,4},{20,0},{24,12},{28,8},{1,21},{... | collective-permute-start | bytes 294920 | tf_op jit(solution)/shard_map/ppermute | solution.py:127
  24.1 0.1 collective-permute-start.8
  24.2 1.5 %collective-permute-start.9 = (bf16[128,384]{1,0:T(8,128)(2,1)S(1)}, bf16[128,384]{1,0:T(8,128)(2,1)S(1)}, u32[]{:S(2)}, u32[]{:S(2)}) collective-permute-start(bf16[128,384]{1,0:T(8,128)(2,1)S(1)} %get-tuple-element.29), channel_id=1, source_target_pairs={{0,16},{4,20},{8,24},{12,28},{16,0},{20,4},{24,8},{28,12},{1,17},{... | collective-permute-start | bytes 294920 | tf_op jit(solution)/shard_map/ppermute | solution.py:127
  25.7 0.4 %collective-permute-start.10 = (bf16[128,384]{1,0:T(8,128)(2,1)S(1)}, bf16[128,384]{1,0:T(8,128)(2,1)S(1)}, u32[]{:S(2)}, u32[]{:S(2)}) collective-permute-start(bf16[128,384]{1,0:T(8,128)(2,1)S(1)} %get-tuple-element.30), channel_id=1, source_target_pairs={{0,24},{4,28},{8,16},{12,20},{16,8},{20,12},{24,0},{28,4},{1,25},{... | collective-permute-start | bytes 294920 | tf_op jit(solution)/shard_map/ppermute | solution.py:127
  26.0 1.4 %collective-permute-start.11 = (bf16[128,384]{1,0:T(8,128)(2,1)S(1)}, bf16[128,384]{1,0:T(8,128)(2,1)S(1)}, u32[]{:S(2)}, u32[]{:S(2)}) collective-permute-start(bf16[128,384]{1,0:T(8,128)(2,1)S(1)} %get-tuple-element.31), channel_id=1, source_target_pairs={{0,4},{4,0},{8,12},{12,8},{16,20},{20,16},{24,28},{28,24},{1,5},{5... | collective-permute-start | bytes 294920 | tf_op jit(solution)/shard_map/ppermute | solution.py:127
  27.5 0.1 collective-permute-done.7.refs_0_
  27.5 0.7 %collective-permute-start.12 = (bf16[128,384]{1,0:T(8,128)(2,1)S(1)}, bf16[128,384]{1,0:T(8,128)(2,1)S(1)}, u32[]{:S(2)}, u32[]{:S(2)}) collective-permute-start(bf16[128,384]{1,0:T(8,128)(2,1)S(1)} %get-tuple-element.32), channel_id=1, source_target_pairs={{0,12},{4,8},{8,4},{12,0},{16,28},{20,24},{24,20},{28,16},{1,13},{... | collective-permute-start | bytes 294920 | tf_op jit(solution)/shard_map/ppermute | solution.py:127
  28.2 1.6 %collective-permute-done.8.refs_1_ = bf16[128,384]{1,0:T(8,128)(2,1)S(1)} collective-permute-done((bf16[128,384]{1,0:T(8,128)(2,1)S(1)}, bf16[128,384]{1,0:T(8,128)(2,1)S(1)}, u32[]{:S(2)}, u32[]{:S(2)}) %collective-permute-start.8) | collective-permute-done | bytes 98336 | tf_op jit(solution)/shard_map/ppermute | solution.py:127
  29.8 0.4 %collective-permute-start.13 = (bf16[128,384]{1,0:T(8,128)(2,1)S(1)}, bf16[128,384]{1,0:T(8,128)(2,1)S(1)}, u32[]{:S(2)}, u32[]{:S(2)}) collective-permute-start(bf16[128,384]{1,0:T(8,128)(2,1)S(1)} %get-tuple-element.33), channel_id=1, source_target_pairs={{0,8},{4,12},{8,0},{12,4},{16,24},{20,28},{24,16},{28,20},{1,9},{5... | collective-permute-start | bytes 294920 | tf_op jit(solution)/shard_map/ppermute | solution.py:127
  30.2 2.1 %collective-permute-done.9.refs_2_ = bf16[128,384]{1,0:T(8,128)(2,1)S(1)} collective-permute-done((bf16[128,384]{1,0:T(8,128)(2,1)S(1)}, bf16[128,384]{1,0:T(8,128)(2,1)S(1)}, u32[]{:S(2)}, u32[]{:S(2)}) %collective-permute-start.9) | collective-permute-done | bytes 98336 | tf_op jit(solution)/shard_map/ppermute | solution.py:127
  32.3 1.0 %collective-permute-done.10.refs_3_ = bf16[128,384]{1,0:T(8,128)(2,1)S(1)} collective-permute-done((bf16[128,384]{1,0:T(8,128)(2,1)S(1)}, bf16[128,384]{1,0:T(8,128)(2,1)S(1)}, u32[]{:S(2)}, u32[]{:S(2)}) %collective-permute-start.10) | collective-permute-done | bytes 98336 | tf_op jit(solution)/shard_map/ppermute | solution.py:127
  33.3 0.0 collective-permute-done.11.refs_4_
  33.3 0.9 %collective-permute-done.12.refs_5_ = bf16[128,384]{1,0:T(8,128)(2,1)S(1)} collective-permute-done((bf16[128,384]{1,0:T(8,128)(2,1)S(1)}, bf16[128,384]{1,0:T(8,128)(2,1)S(1)}, u32[]{:S(2)}, u32[]{:S(2)}) %collective-permute-start.12) | collective-permute-done | bytes 98336 | tf_op jit(solution)/shard_map/ppermute | solution.py:127
  34.2 0.0 collective-permute-done.13.refs_6_
  34.2 1.1 %unpack.1 = (bf16[128,1024]{1,0:T(8,128)(2,1)}, bf16[128,1024]{1,0:T(8,128)(2,1)}, bf16[128,1024]{1,0:T(8,128)(2,1)}) custom-call(bf16[128,384]{1,0:T(8,128)(2,1)S(1)} %collective-permute-done.7.refs_0_, bf16[128,384]{1,0:T(8,128)(2,1)S(1)} %collective-permute-done.8.refs_1_, bf16[128,384]{1,0:T(8,128)(2,1)S(1)} %collective-permute-done.9.refs_2_, ...), custom_call_target="tpu_custom_call" | custom-call | tf_op jit(solution)/shard_map/unpack/pallas_call | solution.py:283
  (2 shorter events, 0.0 us)
Async XLA Ops:
  1.6 8.8 %collective-permute-start = (bf16[128,512]{1,0:T(8,128)(2,1)S(1)}, bf16[128,512]{1,0:T(8,128)(2,1)S(1)}, u32[]{:S(2)}, u32[]{:S(2)}) collective-permute-start(bf16[128,512]{1,0:T(8,128)(2,1)S(1)} %get-tuple-element.19), channel_id=1, source_target_pairs={{0,20},{4,16},{8,28},{12,24},{16,4},{20,0},{24,12},{28,8},{1,21},{... | collective-permute-start | bytes 393224 | tf_op jit(solution)/shard_map/ppermute | solution.py:127
  5.6 6.7 %collective-permute-start.1 = (bf16[128,512]{1,0:T(8,128)(2,1)S(1)}, bf16[128,512]{1,0:T(8,128)(2,1)S(1)}, u32[]{:S(2)}, u32[]{:S(2)}) collective-permute-start(bf16[128,512]{1,0:T(8,128)(2,1)S(1)} %get-tuple-element.20), channel_id=1, source_target_pairs={{0,28},{4,24},{8,20},{12,16},{16,12},{20,8},{24,4},{28,0},{1,29},{... | collective-permute-start | bytes 393224 | tf_op jit(solution)/shard_map/ppermute | solution.py:127
  6.9 8.9 %collective-permute-start.2 = (bf16[128,512]{1,0:T(8,128)(2,1)S(1)}, bf16[128,512]{1,0:T(8,128)(2,1)S(1)}, u32[]{:S(2)}, u32[]{:S(2)}) collective-permute-start(bf16[128,512]{1,0:T(8,128)(2,1)S(1)} %get-tuple-element.21), channel_id=1, source_target_pairs={{0,16},{4,20},{8,24},{12,28},{16,0},{20,4},{24,8},{28,12},{1,17},{... | collective-permute-start | bytes 393224 | tf_op jit(solution)/shard_map/ppermute | solution.py:127
  8.1 9.2 %copy-start = (s32[8,8]{1,0:T(8,128)S(1)}, s32[8,8]{1,0:T(8,128)}, u32[]{:S(2)}) copy-start(s32[8,8]{1,0:T(8,128)} %mask_ref.1) | copy-start | bytes 772
  8.1 8.8 %collective-permute-start.3 = (bf16[128,512]{1,0:T(8,128)(2,1)S(1)}, bf16[128,512]{1,0:T(8,128)(2,1)S(1)}, u32[]{:S(2)}, u32[]{:S(2)}) collective-permute-start(bf16[128,512]{1,0:T(8,128)(2,1)S(1)} %get-tuple-element.22), channel_id=1, source_target_pairs={{0,24},{4,28},{8,16},{12,20},{16,8},{20,12},{24,0},{28,4},{1,25},{... | collective-permute-start | bytes 393224 | tf_op jit(solution)/shard_map/ppermute | solution.py:127
  8.7 8.2 %collective-permute-start.4 = (bf16[128,512]{1,0:T(8,128)(2,1)S(1)}, bf16[128,512]{1,0:T(8,128)(2,1)S(1)}, u32[]{:S(2)}, u32[]{:S(2)}) collective-permute-start(bf16[128,512]{1,0:T(8,128)(2,1)S(1)} %get-tuple-element.23), channel_id=1, source_target_pairs={{0,4},{4,0},{8,12},{12,8},{16,20},{20,16},{24,28},{28,24},{1,5},{5... | collective-permute-start | bytes 393224 | tf_op jit(solution)/shard_map/ppermute | solution.py:127
  10.4 6.9 %collective-permute-start.5 = (bf16[128,512]{1,0:T(8,128)(2,1)S(1)}, bf16[128,512]{1,0:T(8,128)(2,1)S(1)}, u32[]{:S(2)}, u32[]{:S(2)}) collective-permute-start(bf16[128,512]{1,0:T(8,128)(2,1)S(1)} %get-tuple-element.24), channel_id=1, source_target_pairs={{0,12},{4,8},{8,4},{12,0},{16,28},{20,24},{24,20},{28,16},{1,13},{... | collective-permute-start | bytes 393224 | tf_op jit(solution)/shard_map/ppermute | solution.py:127
  12.3 5.0 %collective-permute-start.6 = (bf16[128,512]{1,0:T(8,128)(2,1)S(1)}, bf16[128,512]{1,0:T(8,128)(2,1)S(1)}, u32[]{:S(2)}, u32[]{:S(2)}) collective-permute-start(bf16[128,512]{1,0:T(8,128)(2,1)S(1)} %get-tuple-element.25), channel_id=1, source_target_pairs={{0,8},{4,12},{8,0},{12,4},{16,24},{20,28},{24,16},{28,20},{1,9},{5... | collective-permute-start | bytes 393224 | tf_op jit(solution)/shard_map/ppermute | solution.py:127
  21.6 6.0 %collective-permute-start.7 = (bf16[128,384]{1,0:T(8,128)(2,1)S(1)}, bf16[128,384]{1,0:T(8,128)(2,1)S(1)}, u32[]{:S(2)}, u32[]{:S(2)}) collective-permute-start(bf16[128,384]{1,0:T(8,128)(2,1)S(1)} %get-tuple-element.27), channel_id=1, source_target_pairs={{0,20},{4,16},{8,28},{12,24},{16,4},{20,0},{24,12},{28,8},{1,21},{... | collective-permute-start | bytes 294920 | tf_op jit(solution)/shard_map/ppermute | solution.py:127
  24.1 5.8 %collective-permute-start.8 = (bf16[128,384]{1,0:T(8,128)(2,1)S(1)}, bf16[128,384]{1,0:T(8,128)(2,1)S(1)}, u32[]{:S(2)}, u32[]{:S(2)}) collective-permute-start(bf16[128,384]{1,0:T(8,128)(2,1)S(1)} %get-tuple-element.28), channel_id=1, source_target_pairs={{0,28},{4,24},{8,20},{12,16},{16,12},{20,8},{24,4},{28,0},{1,29},{... | collective-permute-start | bytes 294920 | tf_op jit(solution)/shard_map/ppermute | solution.py:127
  24.2 8.2 %collective-permute-start.9 = (bf16[128,384]{1,0:T(8,128)(2,1)S(1)}, bf16[128,384]{1,0:T(8,128)(2,1)S(1)}, u32[]{:S(2)}, u32[]{:S(2)}) collective-permute-start(bf16[128,384]{1,0:T(8,128)(2,1)S(1)} %get-tuple-element.29), channel_id=1, source_target_pairs={{0,16},{4,20},{8,24},{12,28},{16,0},{20,4},{24,8},{28,12},{1,17},{... | collective-permute-start | bytes 294920 | tf_op jit(solution)/shard_map/ppermute | solution.py:127
  25.7 7.7 %collective-permute-start.10 = (bf16[128,384]{1,0:T(8,128)(2,1)S(1)}, bf16[128,384]{1,0:T(8,128)(2,1)S(1)}, u32[]{:S(2)}, u32[]{:S(2)}) collective-permute-start(bf16[128,384]{1,0:T(8,128)(2,1)S(1)} %get-tuple-element.30), channel_id=1, source_target_pairs={{0,24},{4,28},{8,16},{12,20},{16,8},{20,12},{24,0},{28,4},{1,25},{... | collective-permute-start | bytes 294920 | tf_op jit(solution)/shard_map/ppermute | solution.py:127
  26.0 7.3 %collective-permute-start.11 = (bf16[128,384]{1,0:T(8,128)(2,1)S(1)}, bf16[128,384]{1,0:T(8,128)(2,1)S(1)}, u32[]{:S(2)}, u32[]{:S(2)}) collective-permute-start(bf16[128,384]{1,0:T(8,128)(2,1)S(1)} %get-tuple-element.31), channel_id=1, source_target_pairs={{0,4},{4,0},{8,12},{12,8},{16,20},{20,16},{24,28},{28,24},{1,5},{5... | collective-permute-start | bytes 294920 | tf_op jit(solution)/shard_map/ppermute | solution.py:127
  27.5 6.7 %collective-permute-start.12 = (bf16[128,384]{1,0:T(8,128)(2,1)S(1)}, bf16[128,384]{1,0:T(8,128)(2,1)S(1)}, u32[]{:S(2)}, u32[]{:S(2)}) collective-permute-start(bf16[128,384]{1,0:T(8,128)(2,1)S(1)} %get-tuple-element.32), channel_id=1, source_target_pairs={{0,12},{4,8},{8,4},{12,0},{16,28},{20,24},{24,20},{28,16},{1,13},{... | collective-permute-start | bytes 294920 | tf_op jit(solution)/shard_map/ppermute | solution.py:127
  29.8 4.4 %collective-permute-start.13 = (bf16[128,384]{1,0:T(8,128)(2,1)S(1)}, bf16[128,384]{1,0:T(8,128)(2,1)S(1)}, u32[]{:S(2)}, u32[]{:S(2)}) collective-permute-start(bf16[128,384]{1,0:T(8,128)(2,1)S(1)} %get-tuple-element.33), channel_id=1, source_target_pairs={{0,8},{4,12},{8,0},{12,4},{16,24},{20,28},{24,16},{28,20},{1,9},{5... | collective-permute-start | bytes 294920 | tf_op jit(solution)/shard_map/ppermute | solution.py:127

commit v3 on v0

--- a/solution.py
+++ b/solution.py
@@ -1,11 +1,16 @@
+import functools
 import math
 
 import jax
 import jax.numpy as jnp
 from jax import lax
+from jax.experimental import pallas as pl
+from jax.experimental.pallas import tpu as pltpu
 from jax.sharding import PartitionSpec as P
 
 HEAD_DIM = 128
+MIB = 1024 * 1024
+GROUP = ("blk", "uly")
 
 
 def padded(block, sides, width):
@@ -44,7 +49,7 @@
     return jnp.repeat(jnp.repeat(mask_blocks > 0, 128, axis=0), 128, axis=1)
 
 
-def local(queries, keys, values, out_grad, block_mask):
+def by_cells(queries, keys, values, out_grad, block_mask):
     local_q, local_k, local_v, local_g = (
         lax.all_to_all(queries, "uly", split_axis=1, concat_axis=0, tiled=True),
         lax.all_to_all(keys, "uly", split_axis=1, concat_axis=0, tiled=True),
@@ -109,6 +114,397 @@
     )
 
 
+def flat_index(axes):
+    index = 0
+    for axis in axes:
+        index = index * lax.axis_size(axis) + lax.axis_index(axis)
+    return index
+
+
+def same_core(here):
+    return (here >> 1) & 1
+
+
+def even_places(here):
+    return (here ^ (here >> 1) ^ (here >> 2)) & 1
+
+
+def hop(first, second=None, chooser=same_core):
+    if second is None:
+        return lambda here: first
+    return lambda here: first + (second - first) * chooser(here)
+
+
+STAY = hop(0)
+CORE = hop(2)
+FAR = hop(5)
+FAR_CORE = hop(7)
+SIDE = hop(4, 1)
+OTHER_SIDE = hop(1, 4)
+SIDE_CORE = hop(6, 3, even_places)
+OTHER_SIDE_CORE = hop(3, 6, even_places)
+
+INWARD = (SIDE, FAR_CORE, OTHER_SIDE, SIDE_CORE, OTHER_SIDE_CORE, CORE, FAR)
+OUTWARD = (SIDE, FAR, FAR_CORE, OTHER_SIDE, SIDE_CORE, OTHER_SIDE_CORE, CORE)
+FIRST = 2
+EARLY = 2
+LATE = 5
+DONE = 0
+AFTER = {6: 1}
+EXPONENT = math.log2(math.e) / math.sqrt(HEAD_DIM)
+
+
+def exchange(block, distance):
+    places = range(lax.axis_size(GROUP))
+    return lax.ppermute(block, GROUP, [(i, i ^ distance(i)) for i in places])
+
+
+def part(ref, n):
+    return ref.at[:, n * HEAD_DIM : (n + 1) * HEAD_DIM]
+
+
+def head_of(ref, head):
+    return ref.at[:, pl.ds(pl.multiple_of(head * HEAD_DIM, HEAD_DIM), HEAD_DIM)]
+
+
+def run(copies):
+    for copy in copies:
+        copy.start()
+    for copy in copies:
+        copy.wait()
+
+
+def pack_kernel(distances, *refs):
+    count = len(distances)
+    extras = (len(refs) - 1 - count - 4) // 2
+    sources, outs, sems = refs[: 4 + extras], refs[4 + extras : -1], refs[-1]
+    here = flat_index(GROUP)
+    pairs = list(zip(sources[4:], outs[count:]))
+    for distance, slab in zip(distances, outs):
+        for n, array in enumerate(sources[:4]):
+            pairs.append((head_of(array, here ^ distance(here)), part(slab, n)))
+    run([pltpu.make_async_copy(*pair, sems.at[n]) for n, pair in enumerate(pairs)])
+
+
+def unpack_kernel(distances, *refs):
+    slabs, arrays, sems = refs[: len(distances)], refs[-4:-1], refs[-1]
+    here = flat_index(GROUP)
+    pairs = []
+    for distance, slab in zip(distances, slabs):
+        for n, array in enumerate(arrays):
+            pairs.append((part(slab, n), head_of(array, here ^ distance(here))))
+    run([pltpu.make_async_copy(*pair, sems.at[n]) for n, pair in enumerate(pairs)])
+
+
+def near_cells(c):
+    return (c, c ^ 1, c ^ 3)
+
+
+def key_places(c):
+    return [2 * n + a for n in near_cells(c) for a in range(2)]
+
+
+def blocks_of(value):
+    return [value[r : r + 128] for r in range(0, value.shape[0], 128)]
+
+
+def seen_by(mask_ref, here, key, queries):
+    flags = [jnp.full((1, 128), mask_ref[here ^ query, here ^ key]) for query in queries]
+    return jnp.concatenate(flags, axis=1) > 0
+
+
+def weights(scores, seen, top):
+    return [
+        jnp.exp2(block * EXPONENT - jnp.where(flag, top, 1e30)) for block, flag in zip(scores, seen)
+    ]
+
+
+def top_of(scores, seen):
+    top = jnp.full((1, scores[0].shape[1]), -1e30, jnp.float32)
+    for block, flag in zip(scores, seen):
+        top = jnp.maximum(top, jnp.where(flag, jnp.max(block, axis=0, keepdims=True), -1e30))
+    return top * EXPONENT
+
+
+def sum_of(blocks):
+    total = blocks[0]
+    for block in blocks[1:]:
+        total = total + block
+    return jnp.sum(total, axis=0, keepdims=True)
+
+
+def query_grad(keys, dscores):
+    low = (t_times(keys, dscores) * (1.0 / math.sqrt(HEAD_DIM))).T.astype(jnp.bfloat16)
+    return low.reshape(-1, 128, HEAD_DIM)
+
+
+def early_kernel(distances, mask_ref, *refs):
+    slabs, outs = refs[:-6], refs[-6:]
+    stack_ref, exps_ref, dprobs_ref, stats_ref, done_ref, query_ref = outs
+    here = flat_index(GROUP)
+    for distance, slab in zip(distances, slabs):
+        stack_ref[distance(here)] = slab[...]
+
+    def take(places, n):
+        columns = slice(n * HEAD_DIM, (n + 1) * HEAD_DIM)
+        return jnp.concatenate([stack_ref[place, :, columns] for place in places], axis=0)
+
+    cells = stack_ref.shape[0] // 2
+    present = [[p for p in (2 * c, 2 * c + 1) if p != LATE] for c in range(cells)]
+    for c in range(cells):
+        q, g = take(present[c], 0), take(present[c], 3)
+        width = q.shape[0]
+        keys = [place for place in key_places(c) if place != LATE]
+        scores = [b for n in near_cells(c) for b in blocks_of(times_t(take(present[n], 1), q))]
+        dprobs = [b for n in near_cells(c) for b in blocks_of(times_t(take(present[n], 2), g))]
+        seen = [seen_by(mask_ref, here, key, present[c]) for key in keys]
+        top = top_of(scores, seen)
+        exps = weights(scores, seen, top)
+        total = sum_of(exps)
+        product = sum_of([e * d for e, d in zip(exps, dprobs)])
+        if LATE not in key_places(c):
+            inverse = 1.0 / total
+            delta = product * inverse
+            terms = []
+            for n, (weight, term) in enumerate(zip(exps, dprobs)):
+                probs = weight * inverse
+                terms.append((probs * (term - delta)).astype(jnp.bfloat16))
+                done_ref[0, 128 * n : 128 * (n + 1)] = probs.astype(jnp.bfloat16)
+                done_ref[1, 128 * n : 128 * (n + 1)] = terms[n]
+            query_ref[...] = query_grad(take(key_places(c), 1), jnp.concatenate(terms, axis=0))
+            continue
+        for key, weight, term in zip(keys, exps, dprobs):
+            row = 128 * key_places(c).index(key)
+            exps_ref[c, row : row + 128, :width] = weight
+            dprobs_ref[c, row : row + 128, :width] = term
+        stats_ref[c, 0:1, :width] = top
+        stats_ref[c, 1:2, :width] = total
+        stats_ref[c, 2:3, :width] = product
+
+
+def late_kernel(distances, mask_ref, slab, *refs):
+    stack_ref, exps_ref, dprobs_ref, stats_ref, done_ref, query_ref = refs[:6]
+    outs, out_ref = refs[6:-1], refs[-1]
+    here = flat_index(GROUP)
+    fixed = [distance(here) for distance in distances]
+    fixed = {place: out for place, out in zip(fixed, outs) if isinstance(place, int)}
+    scale = 1.0 / math.sqrt(HEAD_DIM)
+    cells = stack_ref.shape[0] // 2
+
+    def take(places, n):
+        columns = slice(n * HEAD_DIM, (n + 1) * HEAD_DIM)
+        parts = [slab[:, columns] if p == LATE else stack_ref[p, :, columns] for p in places]
+        return jnp.concatenate(parts, axis=0)
+
+    def whole(n):
+        return [take((2 * c, 2 * c + 1), n) for c in range(cells)]
+
+    q, k, v, g = (whole(n) for n in range(4))
+
+    units = [(c, (2 * c, 2 * c + 1)) for c in range(cells) if c not in (DONE, LATE // 2)]
+    units = [(LATE // 2, (place,)) for place in (LATE - 1, LATE)] + units
+    fresh = [[p for p in key_places(c) if LATE in (p, *queries)] for c, queries in units]
+    scores, dprobs, exps, inverse, delta, early_inverse = ([None] * len(units) for _ in range(6))
+    for u, (c, queries) in enumerate(units):
+        groups = [(LATE,)] if LATE not in queries else [(2 * n, 2 * n + 1) for n in near_cells(c)]
+        groups = groups if fresh[u] else []
+        mine_q, mine_g = take(queries, 0), take(queries, 3)
+        scores[u] = [b for keys in groups for b in blocks_of(times_t(take(keys, 1), mine_q))]
+        dprobs[u] = [b for keys in groups for b in blocks_of(times_t(take(keys, 2), mine_g))]
+    seen = [[seen_by(mask_ref, here, p, unit[1]) for p in keys] for unit, keys in zip(units, fresh)]
+    tops = [top_of(blocks, flags) if blocks else None for blocks, flags in zip(scores, seen)]
+    for u, (c, queries) in enumerate(units):
+        early = LATE not in queries
+        if early:
+            top, total, product = (
+                stats_ref[c, n : n + 1, : 128 * len(queries)] for n in range(3)
+            )
+        shrink = None
+        if fresh[u]:
+            new_top = jnp.maximum(top, tops[u]) if early else tops[u]
+            exps[u] = weights(scores[u], seen[u], new_top)
+            new_total = sum_of(exps[u])
+            new_product = sum_of([e * d for e, d in zip(exps[u], dprobs[u])])
+            if early:
+                shrink = jnp.exp2(top - new_top)
+                new_total = new_total + total * shrink
+                new_product = new_product + product * shrink
+            total, product = new_total, new_product
+        inverse[u] = 1.0 / total
+        delta[u] = product * inverse[u]
+        early_inverse[u] = inverse[u] if shrink is None else inverse[u] * shrink
+
+    def finished(u):
+        c, queries = units[u]
+        probs_low, dscores = [], []
+        for n, key in enumerate(key_places(c)):
+            if key in fresh[u]:
+                index = fresh[u].index(key)
+                probs, term = exps[u][index] * inverse[u], dprobs[u][index]
+            else:
+                place = (c, slice(128 * n, 128 * (n + 1)), slice(0, 128 * len(queries)))
+                probs, term = exps_ref[place] * early_inverse[u], dprobs_ref[place]
+            probs_low.append(probs.astype(jnp.bfloat16))
+            dscores.append((probs * (term - delta[u])).astype(jnp.bfloat16))
+        return probs_low, dscores
+
+    def put(n, c, value):
+        low = value.astype(jnp.bfloat16).reshape(2, 128, HEAD_DIM)
+        for place in (2 * c, 2 * c + 1):
+            out = fixed.get(place, out_ref.at[place])
+            out[:, n * HEAD_DIM : (n + 1) * HEAD_DIM] = low[place - 2 * c]
+
+    def joined(blocks, c, axis):
+        return jnp.concatenate([blocks[n] for n in near_cells(c)], axis=axis)
+
+    probs_low = [{} for _ in range(cells)]
+    dscores = [{} for _ in range(cells)]
+
+    def rows_of(c):
+        if c == DONE:
+            pair = [blocks_of(done_ref[n]) for n in range(2)]
+        elif LATE // 2 == c:
+            sides = zip(finished(0), finished(1))
+            pair = [
+                [jnp.concatenate(both, axis=1) for both in zip(left, right)] for left, right in sides
+            ]
+        else:
+            pair = finished(units.index((c, (2 * c, 2 * c + 1))))
+        for t, n in enumerate(near_cells(c)):
+            probs_low[n][c] = jnp.concatenate(pair[0][2 * t : 2 * t + 2], axis=0)
+            dscores[n][c] = jnp.concatenate(pair[1][2 * t : 2 * t + 2], axis=0)
+
+    def put_value_grad(c):
+        low = joined(probs_low[c], c, 1)
+        put(2, c, jnp.dot(low, joined(g, c, 0), preferred_element_type=jnp.float32))
+
+    def put_key_grad(c):
+        low = joined(dscores[c], c, 1)
+        put(1, c, jnp.dot(low, joined(q, c, 0), preferred_element_type=jnp.float32) * scale)
+
+    def put_query_grad(c):
+        if c == DONE:
+            put(0, c, query_ref[...])
+            return
+        terms = jnp.concatenate([dscores[n][c] for n in near_cells(c)], axis=0)
+        put(0, c, query_grad(joined(k, c, 0), terms))
+
+    rows_of(2)
+    rows_of(1)
+    rows_of(3)
+    rows_of(0)
+    put_value_grad(0)
+    put_value_grad(1)
+    put_value_grad(2)
+    put_value_grad(3)
+    put_key_grad(0)
+    put_key_grad(1)
+    put_key_grad(2)
+    put_key_grad(3)
+    put_query_grad(0)
+    put_query_grad(1)
+    put_query_grad(2)
+    put_query_grad(3)
+    for distance, out in zip(distances, outs):
+        if not isinstance(distance(here), int):
+            out[...] = out_ref[distance(here)]
+
+
+SMEM = pl.BlockSpec(memory_space=pltpu.SMEM)
+VMEM = pl.BlockSpec(memory_space=pltpu.VMEM)
+ANY = pl.BlockSpec(memory_space=pl.ANY)
+
+
+def slab_shape(tokens, parts):
+    return jax.ShapeDtypeStruct((tokens, parts * HEAD_DIM), jnp.bfloat16)
+
+
+def pack(arrays, distances, name, *extras):
+    tokens = arrays[0].shape[0]
+    count = len(distances)
+    outs = [slab_shape(tokens, 4)] * count
+    outs += [jax.ShapeDtypeStruct(extra.shape, extra.dtype) for extra in extras]
+    return pl.pallas_call(
+        functools.partial(pack_kernel, distances),
+        out_shape=outs,
+        in_specs=[ANY] * (4 + len(extras)),
+        out_specs=[ANY] * len(outs),
+        scratch_shapes=[pltpu.SemaphoreType.DMA((4 * count + len(extras),))],
+        compiler_params=pltpu.CompilerParams(vmem_limit_bytes=MIB),
+        name=name,
+    )(*arrays, *extras)
+
+
+def unpack(whole, distances, slabs, name, *arrays):
+    count = len(distances)
+    return pl.pallas_call(
+        functools.partial(unpack_kernel, distances),
+        out_shape=[whole] * 3,
+        in_specs=[ANY] * (count + len(arrays)),
+        out_specs=[ANY] * 3,
+        scratch_shapes=[pltpu.SemaphoreType.DMA((3 * count,))],
+        compiler_params=pltpu.CompilerParams(vmem_limit_bytes=MIB),
+        input_output_aliases={count + n: n for n in range(len(arrays))},
+        name=name,
+    )(*slabs, *arrays)
+
+
+def by_heads(queries, keys, values, out_grad, block_mask):
+    devices = lax.axis_size(GROUP)
+    cells = lax.axis_size("blk")
+    tokens = queries.shape[0]
+    *arrays, block_mask = [
+        pltpu.with_memory_space_constraint(array, pltpu.HBM)
+        for array in (queries, keys, values, out_grad, block_mask)
+    ]
+    sent = pack(arrays, INWARD[:FIRST], "pack_first")
+    arrays, sent = lax.optimization_barrier((arrays, sent))
+    *rest, own, block_mask = pack(arrays, INWARD[FIRST:] + (STAY,), "pack_rest", block_mask)
+    got = list(sent) + rest
+    for n, distance in enumerate(INWARD):
+        if n in AFTER:
+            got[n], got[AFTER[n]] = lax.optimization_barrier((got[n], got[AFTER[n]]))
+        got[n] = exchange(got[n], distance)
+    pairs = jax.ShapeDtypeStruct((cells, 6 * tokens, 2 * tokens), jnp.float32)
+    partial = pl.pallas_call(
+        functools.partial(early_kernel, INWARD[:-1] + (STAY,)),
+        out_shape=[
+            jax.ShapeDtypeStruct((devices, tokens, 4 * HEAD_DIM), jnp.bfloat16),
+            pairs,
+            pairs,
+            jax.ShapeDtypeStruct((cells, 8, 2 * tokens), jnp.float32),
+            jax.ShapeDtypeStruct((2, 6 * tokens, 2 * tokens), jnp.bfloat16),
+            jax.ShapeDtypeStruct((2, tokens, HEAD_DIM), jnp.bfloat16),
+        ],
+        in_specs=[SMEM] + [VMEM] * (devices - 1),
+        out_specs=[VMEM] * 6,
+        compiler_params=pltpu.CompilerParams(vmem_limit_bytes=24 * MIB),
+        name="early",
+    )(block_mask, *got[:-1], own)
+    distances = OUTWARD + (STAY,)
+    grads = pl.pallas_call(
+        functools.partial(late_kernel, distances),
+        out_shape=[slab_shape(tokens, 3)] * devices,
+        in_specs=[SMEM] + [VMEM] * 7,
+        out_specs=[VMEM] * devices,
+        scratch_shapes=[pltpu.VMEM((devices, tokens, 3 * HEAD_DIM), jnp.bfloat16)],
+        compiler_params=pltpu.CompilerParams(vmem_limit_bytes=24 * MIB),
+        name="late",
+    )(block_mask, got[-1], *partial)
+    back = [exchange(grad, distance) for grad, distance in zip(grads, OUTWARD)] + [grads[-1]]
+    whole = jax.ShapeDtypeStruct(queries.shape, queries.dtype)
+    grads = unpack(whole, distances[-1:] + distances[:EARLY], back[-1:] + back[:EARLY], "unpack")
+    return unpack(whole, distances[EARLY:-1], back[EARLY:-1], "unpack_last", *grads)
+
+
+def local(queries, keys, values, out_grad, block_mask):
+    heads = queries.shape[1] // HEAD_DIM
+    cells, halves = lax.axis_size("blk"), lax.axis_size("uly")
+    if (cells, halves) == (4, 2) and heads == cells * halves and queries.shape[0] == 128:
+        return by_heads(queries, keys, values, out_grad, block_mask)
+    return by_cells(queries, keys, values, out_grad, block_mask)
+
+
 def solution(mesh):
     return jax.shard_map(
         local,

time: 84.7 us -> 34.4 us (0.41)
  waiting for transfers between devices: 33.7 us -> 9.87 us
  local copies, waits for them, and re-layouts: 13.2 us -> 0 us
  starting transfers between devices: 26 us -> 14.8 us
  Pallas kernels: 0 us -> 8.75 us
  matrix products: 6.21 us -> 0 us
  other arithmetic: 4.13 us -> 0 us
    all_to_all x7 -> x0, starting transfers between devices: 24.9 us -> none  [the longest x1 4.23 us: local(): lax.all_to_all(keys, 'uly', split_axis=1, concat_axis=0, tiled=True)]
    all_to_all x7 -> x0, waiting for transfers between devices: 24.2 us -> none  [the longest x1 5.03 us: local(): lax.all_to_all(value_grad, 'uly', split_axis=0, concat_axis=1, tiled=True)]
    ppermute x4 -> x14, starting transfers between devices: 1.06 us -> 14.8 us  [exchange(): return lax.ppermute(block, GROUP, [(i, i ^ distance(i)) for i in places])]
    unnamed x19 -> x0, local copies, waits for them, and re-layouts: 8.88 us -> none
    pallas_call x0 -> x6, Pallas kernels: none -> 8.75 us  [the longest x1 2.5 us: by_heads(): pl.pallas_call(functools.partial(late_kernel, distances), out_shape=[slab...]
    dot_general x20 -> x0, matrix products: 6.21 us -> none  [the longest x8 2.78 us: times_t(): lax.dot_general(left, right, (((1,), (1,)), ((), ())), preferred_element_...]
    convert_element_type x4 -> x0, local copies, waits for them, and re-layouts: 1.61 us -> none  [the longest x2 0.81 us: local(): value_grad = summed[:, 1].astype(jnp.bfloat16)]
    add x3 -> x0, other arithmetic: 1.39 us -> none  [the longest x1 1.37 us: local(): summed = partial_terms[genes:2 * genes] + from_next + from_prior]
  transfers between devices with their start and end apart: 11 -> 14, of which waited for: 9 -> 6; matrix products, arithmetic and copies ran while one was open for 13% -> 0% of each run, Pallas kernels for 0% -> 13%
where the time goes in v3:
time: 34.4 us; the launch traced here: 34.1 us
  starting transfers between devices  14.8 us (43%)
  waiting for transfers between devices  9.87 us (29%)
  Pallas kernels  8.75 us (25%)
  between operations  0.68 us (2%)
    ppermute x14, starting transfers between devices, exchange(): return lax.ppermute(block, GROUP, [(i, i ^ distance(i)) for i in places])  14.8 us
    ppermute x14, waiting for transfers between devices, exchange(): return lax.ppermute(block, GROUP, [(i, i ^ distance(i)) for i in places])  9.87 us
    pallas_call x1, Pallas kernels, by_heads(): pl.pallas_call(functools.partial(late_kernel, distances), out_shape=[slab...  2.5 us
    pallas_call x2, Pallas kernels, pack(): pl.pallas_call(functools.partial(pack_kernel, distances), out_shape=outs,...  2.3 us
    pallas_call x1, Pallas kernels, by_heads(): pl.pallas_call(functools.partial(early_kernel, INWARD[:-1] + (STAY,)), ou...  2.29 us
    pallas_call x2, Pallas kernels, unpack(): pl.pallas_call(functools.partial(unpack_kernel, distances), out_shape=[wh...  1.68 us
  transfers between devices with their start and end apart: 14, of which 6 were waited for; matrix products, arithmetic and copies ran while one was open for 0% of the time, Pallas kernels for 13%

profile of v3, /device:TPU:0, one launch (start us, length us, event | category | flops | bytes accessed | tf_op | source)
XLA Modules:
  0.0 34.1 jit_solution(716487520197948621)
XLA Ops:
  0.6 1.0 %pack_first.1 = (bf16[128,512]{1,0:T(8,128)(2,1)S(1)}, bf16[128,512]{1,0:T(8,128)(2,1)S(1)}) custom-call(bf16[128,1024]{1,0:T(8,128)(2,1)} %refs_0_.2, bf16[128,1024]{1,0:T(8,128)(2,1)} %refs_1_.2, bf16[128,1024]{1,0:T(8,128)(2,1)} %refs_2_.2, bf16[128,1024]{1,0:T(8,128)(2,1)} %refs_3_.2), custom_call_target="tpu_custom_call" | custom-call | tf_op jit(solution)/shard_map/pack_first/pallas_call | solution.py:427
  1.6 3.4 %collective-permute-start = (bf16[128,512]{1,0:T(8,128)(2,1)S(1)}, bf16[128,512]{1,0:T(8,128)(2,1)S(1)}, u32[]{:S(2)}, u32[]{:S(2)}) collective-permute-start(bf16[128,512]{1,0:T(8,128)(2,1)S(1)} %get-tuple-element.45), channel_id=1, source_target_pairs={{0,28},{4,24},{8,20},{12,16},{16,12},{20,8},{24,4},{28,0},{1,29},{... | collective-permute-start | bytes 393224 | tf_op jit(solution)/shard_map/ppermute | solution.py:159
  5.0 0.5 %collective-permute-start.2 = (bf16[128,512]{1,0:T(8,128)(2,1)S(1)}, bf16[128,512]{1,0:T(8,128)(2,1)S(1)}, u32[]{:S(2)}, u32[]{:S(2)}) collective-permute-start(bf16[128,512]{1,0:T(8,128)(2,1)S(1)} %get-tuple-element.47), channel_id=1, source_target_pairs={{0,16},{4,20},{8,12},{12,8},{16,0},{20,4},{24,28},{28,24},{1,17},{... | collective-permute-start | bytes 393224 | tf_op jit(solution)/shard_map/ppermute | solution.py:159
  5.5 1.3 %pack_rest.1 = (bf16[128,512]{1,0:T(8,128)(2,1)S(1)}, bf16[128,512]{1,0:T(8,128)(2,1)S(1)}, bf16[128,512]{1,0:T(8,128)(2,1)S(1)}, bf16[128,512]{1,0:T(8,128)(2,1...) custom-call(bf16[128,1024]{1,0:T(8,128)(2,1)} %refs_0_.2, ...), custom_call_target="tpu_custom_call" | custom-call | tf_op jit(solution)/shard_map/pack_rest/pallas_call | solution.py:427
  6.9 0.7 %collective-permute-start.3 = (bf16[128,512]{1,0:T(8,128)(2,1)S(1)}, bf16[128,512]{1,0:T(8,128)(2,1)S(1)}, u32[]{:S(2)}, u32[]{:S(2)}) collective-permute-start(bf16[128,512]{1,0:T(8,128)(2,1)S(1)} %get-tuple-element.49), channel_id=1, source_target_pairs={{0,4},{4,0},{8,24},{12,28},{16,20},{20,16},{24,8},{28,12},{1,5},{5... | collective-permute-start | bytes 393224 | tf_op jit(solution)/shard_map/ppermute | solution.py:159
  7.6 1.1 %collective-permute-start.4 = (bf16[128,512]{1,0:T(8,128)(2,1)S(1)}, bf16[128,512]{1,0:T(8,128)(2,1)S(1)}, u32[]{:S(2)}, u32[]{:S(2)}) collective-permute-start(bf16[128,512]{1,0:T(8,128)(2,1)S(1)} %get-tuple-element.50), channel_id=1, source_target_pairs={{0,24},{4,8},{8,4},{12,20},{16,28},{20,12},{24,0},{28,16},{1,25},{... | collective-permute-start | bytes 393224 | tf_op jit(solution)/shard_map/ppermute | solution.py:159
  8.7 1.5 %collective-permute-start.5 = (bf16[128,512]{1,0:T(8,128)(2,1)S(1)}, bf16[128,512]{1,0:T(8,128)(2,1)S(1)}, u32[]{:S(2)}, u32[]{:S(2)}) collective-permute-start(bf16[128,512]{1,0:T(8,128)(2,1)S(1)} %get-tuple-element.51), channel_id=1, source_target_pairs={{0,12},{4,28},{8,16},{12,0},{16,8},{20,24},{24,20},{28,4},{1,13},{... | collective-permute-start | bytes 393224 | tf_op jit(solution)/shard_map/ppermute | solution.py:159
  10.2 0.0 collective-permute-done.refs_1_
  10.2 0.1 collective-permute-start.6
  10.3 2.4 %collective-permute-done.2.refs_0_ = bf16[128,512]{1,0:T(8,128)(2,1)S(1)} collective-permute-done((bf16[128,512]{1,0:T(8,128)(2,1)S(1)}, bf16[128,512]{1,0:T(8,128)(2,1)S(1)}, u32[]{:S(2)}, u32[]{:S(2)}) %collective-permute-start.2) | collective-permute-done | bytes 131104 | tf_op jit(solution)/shard_map/ppermute | solution.py:159
  12.7 1.4 %collective-permute-start.1 = (bf16[128,512]{1,0:T(8,128)(2,1)S(1)}, bf16[128,512]{1,0:T(8,128)(2,1)S(1)}, u32[]{:S(2)}, u32[]{:S(2)}) collective-permute-start(bf16[128,512]{1,0:T(8,128)(2,1)S(1)} %get-tuple-element.46), channel_id=1, source_target_pairs={{0,20},{4,16},{8,28},{12,24},{16,4},{20,0},{24,12},{28,8},{1,21},{... | collective-permute-start | bytes 393224 | tf_op jit(solution)/shard_map/ppermute | solution.py:159
  14.0 0.0 collective-permute-done.3.refs_2_
  14.0 1.5 %collective-permute-done.4.refs_3_ = bf16[128,512]{1,0:T(8,128)(2,1)S(1)} collective-permute-done((bf16[128,512]{1,0:T(8,128)(2,1)S(1)}, bf16[128,512]{1,0:T(8,128)(2,1)S(1)}, u32[]{:S(2)}, u32[]{:S(2)}) %collective-permute-start.4) | collective-permute-done | bytes 131104 | tf_op jit(solution)/shard_map/ppermute | solution.py:159
  15.5 0.0 collective-permute-done.6.refs_5_
  15.5 2.3 %early.1 = (bf16[8,128,512]{2,1,0:T(8,128)(2,1)S(1)}, f32[4,768,256]{2,1,0:T(8,128)S(1)}, f32[4,768,256]{2,1,0:T(8,128)S(1)}, f32[4,8,256]{2,1,0:T(8,128)S(1)}, ...) custom-call(s32[8,8]{1,0:T(8,128)S(1)} %get-tuple-element.43.mask_ref, ...), custom_call_target="tpu_custom_call" | custom-call | tf_op jit(solution)/shard_map/early/pallas_call | solution.py:469
  17.8 0.7 %collective-permute-done.1.slab = bf16[128,512]{1,0:T(8,128)(2,1)S(1)} collective-permute-done((bf16[128,512]{1,0:T(8,128)(2,1)S(1)}, bf16[128,512]{1,0:T(8,128)(2,1)S(1)}, u32[]{:S(2)}, u32[]{:S(2)}) %collective-permute-start.1) | collective-permute-done | bytes 131104 | tf_op jit(solution)/shard_map/ppermute | solution.py:159
  18.5 2.5 %late.1 = (bf16[128,384]{1,0:T(8,128)(2,1)S(1)}, bf16[128,384]{1,0:T(8,128)(2,1)S(1)}, bf16[128,384]{1,0:T(8,128)(2,1)S(1)}, bf16[128,384]{1,0:T(8,128)(2,1)S(1)...) custom-call(s32[8,8]{1,0:T(8,128)S(1)} %get-tuple-element.43.mask_re, ...), custom_call_target="tpu_custom_call" | custom-call | tf_op jit(solution)/shard_map/late/pallas_call | solution.py:485
  21.0 1.6 %collective-permute-start.12 = (bf16[128,384]{1,0:T(8,128)(2,1)S(1)}, bf16[128,384]{1,0:T(8,128)(2,1)S(1)}, u32[]{:S(2)}, u32[]{:S(2)}) collective-permute-start(bf16[128,384]{1,0:T(8,128)(2,1)S(1)} %get-tuple-element.66), channel_id=1, source_target_pairs={{0,16},{4,20},{8,12},{12,8},{16,0},{20,4},{24,28},{28,24},{1,17},{... | collective-permute-start | bytes 294920 | tf_op jit(solution)/shard_map/ppermute | solution.py:159
  22.6 1.1 %collective-permute-start.13 = (bf16[128,384]{1,0:T(8,128)(2,1)S(1)}, bf16[128,384]{1,0:T(8,128)(2,1)S(1)}, u32[]{:S(2)}, u32[]{:S(2)}) collective-permute-start(bf16[128,384]{1,0:T(8,128)(2,1)S(1)} %get-tuple-element.67), channel_id=1, source_target_pairs={{0,20},{4,16},{8,28},{12,24},{16,4},{20,0},{24,12},{28,8},{1,21},{... | collective-permute-start | bytes 294920 | tf_op jit(solution)/shard_map/ppermute | solution.py:159
  23.7 0.7 %collective-permute-start.7 = (bf16[128,384]{1,0:T(8,128)(2,1)S(1)}, bf16[128,384]{1,0:T(8,128)(2,1)S(1)}, u32[]{:S(2)}, u32[]{:S(2)}) collective-permute-start(bf16[128,384]{1,0:T(8,128)(2,1)S(1)} %get-tuple-element.60), channel_id=1, source_target_pairs={{0,28},{4,24},{8,20},{12,16},{16,12},{20,8},{24,4},{28,0},{1,29},{... | collective-permute-start | bytes 294920 | tf_op jit(solution)/shard_map/ppermute | solution.py:159
  24.4 0.4 %collective-permute-start.8 = (bf16[128,384]{1,0:T(8,128)(2,1)S(1)}, bf16[128,384]{1,0:T(8,128)(2,1)S(1)}, u32[]{:S(2)}, u32[]{:S(2)}) collective-permute-start(bf16[128,384]{1,0:T(8,128)(2,1)S(1)} %get-tuple-element.61), channel_id=1, source_target_pairs={{0,4},{4,0},{8,24},{12,28},{16,20},{20,16},{24,8},{28,12},{1,5},{5... | collective-permute-start | bytes 294920 | tf_op jit(solution)/shard_map/ppermute | solution.py:159
  24.7 2.3 %collective-permute-start.9 = (bf16[128,384]{1,0:T(8,128)(2,1)S(1)}, bf16[128,384]{1,0:T(8,128)(2,1)S(1)}, u32[]{:S(2)}, u32[]{:S(2)}) collective-permute-start(bf16[128,384]{1,0:T(8,128)(2,1)S(1)} %get-tuple-element.62), channel_id=1, source_target_pairs={{0,24},{4,8},{8,4},{12,20},{16,28},{20,12},{24,0},{28,16},{1,25},{... | collective-permute-start | bytes 294920 | tf_op jit(solution)/shard_map/ppermute | solution.py:159
  27.0 0.0 collective-permute-done.12.refs_1_
  27.0 0.1 collective-permute-start.10
  27.1 2.2 %collective-permute-done.13.refs_2_ = bf16[128,384]{1,0:T(8,128)(2,1)S(1)} collective-permute-done((bf16[128,384]{1,0:T(8,128)(2,1)S(1)}, bf16[128,384]{1,0:T(8,128)(2,1)S(1)}, u32[]{:S(2)}, u32[]{:S(2)}) %collective-permute-start.13) | collective-permute-done | bytes 98336 | tf_op jit(solution)/shard_map/ppermute | solution.py:159
  29.3 0.0 collective-permute-start.11
  29.3 0.8 %unpack.1 = (bf16[128,1024]{1,0:T(8,128)(2,1)}, bf16[128,1024]{1,0:T(8,128)(2,1)}, bf16[128,1024]{1,0:T(8,128)(2,1)}) custom-call(bf16[128,384]{1,0:T(8,128)(2,1)S(1)} %get-tuple-element.65.refs_0_, bf16[128,384]{1,0:T(8,128)(2,1)S(1)} %collective-permute-done.12.refs_1_, bf16[128,384]{1,0:T(8,128)(2,1)S(1)} %collective-permute-done.13.refs_2_), custom_call_target="tpu_custom_call" | custom-call | tf_op jit(solution)/shard_map/unpack/pallas_call | solution.py:440
  30.1 2.3 %collective-permute-done.8.refs_1_ = bf16[128,384]{1,0:T(8,128)(2,1)S(1)} collective-permute-done((bf16[128,384]{1,0:T(8,128)(2,1)S(1)}, bf16[128,384]{1,0:T(8,128)(2,1)S(1)}, u32[]{:S(2)}, u32[]{:S(2)}) %collective-permute-start.8) | collective-permute-done | bytes 98336 | tf_op jit(solution)/shard_map/ppermute | solution.py:159
  32.5 0.7 %collective-permute-done.9.refs_2_ = bf16[128,384]{1,0:T(8,128)(2,1)S(1)} collective-permute-done((bf16[128,384]{1,0:T(8,128)(2,1)S(1)}, bf16[128,384]{1,0:T(8,128)(2,1)S(1)}, u32[]{:S(2)}, u32[]{:S(2)}) %collective-permute-start.9) | collective-permute-done | bytes 98336 | tf_op jit(solution)/shard_map/ppermute | solution.py:159
  33.2 0.0 collective-permute-done.10.refs_3_
  33.2 0.0 collective-permute-done.11.refs_4_
  33.2 0.9 %unpack_last.1 = (bf16[128,1024]{1,0:T(8,128)(2,1)}, bf16[128,1024]{1,0:T(8,128)(2,1)}, bf16[128,1024]{1,0:T(8,128)(2,1)}) custom-call(bf16[128,384]{1,0:T(8,128)(2,1)S(1)} %collective-permute-done.7.refs_0_, bf16[128,384]{1,0:T(8,128)(2,1)S(1)} %collective-permute-done.8.refs_1_, ...), custom_call_target="tpu_custom_call", output_to_operand_aliasing={{0}: (5, {}), {1}: (6, {}), {2}: (7, {})} | custom-call | tf_op jit(solution)/shard_map/unpack_last/pallas_call | solution.py:440
  (2 shorter events, 0.0 us)
Async XLA Ops:
  1.6 8.6 %collective-permute-start = (bf16[128,512]{1,0:T(8,128)(2,1)S(1)}, bf16[128,512]{1,0:T(8,128)(2,1)S(1)}, u32[]{:S(2)}, u32[]{:S(2)}) collective-permute-start(bf16[128,512]{1,0:T(8,128)(2,1)S(1)} %get-tuple-element.45), channel_id=1, source_target_pairs={{0,28},{4,24},{8,20},{12,16},{16,12},{20,8},{24,4},{28,0},{1,29},{... | collective-permute-start | bytes 393224 | tf_op jit(solution)/shard_map/ppermute | solution.py:159
  5.0 7.7 %collective-permute-start.2 = (bf16[128,512]{1,0:T(8,128)(2,1)S(1)}, bf16[128,512]{1,0:T(8,128)(2,1)S(1)}, u32[]{:S(2)}, u32[]{:S(2)}) collective-permute-start(bf16[128,512]{1,0:T(8,128)(2,1)S(1)} %get-tuple-element.47), channel_id=1, source_target_pairs={{0,16},{4,20},{8,12},{12,8},{16,0},{20,4},{24,28},{28,24},{1,17},{... | collective-permute-start | bytes 393224 | tf_op jit(solution)/shard_map/ppermute | solution.py:159
  6.9 7.2 %collective-permute-start.3 = (bf16[128,512]{1,0:T(8,128)(2,1)S(1)}, bf16[128,512]{1,0:T(8,128)(2,1)S(1)}, u32[]{:S(2)}, u32[]{:S(2)}) collective-permute-start(bf16[128,512]{1,0:T(8,128)(2,1)S(1)} %get-tuple-element.49), channel_id=1, source_target_pairs={{0,4},{4,0},{8,24},{12,28},{16,20},{20,16},{24,8},{28,12},{1,5},{5... | collective-permute-start | bytes 393224 | tf_op jit(solution)/shard_map/ppermute | solution.py:159
  7.6 7.9 %collective-permute-start.4 = (bf16[128,512]{1,0:T(8,128)(2,1)S(1)}, bf16[128,512]{1,0:T(8,128)(2,1)S(1)}, u32[]{:S(2)}, u32[]{:S(2)}) collective-permute-start(bf16[128,512]{1,0:T(8,128)(2,1)S(1)} %get-tuple-element.50), channel_id=1, source_target_pairs={{0,24},{4,8},{8,4},{12,20},{16,28},{20,12},{24,0},{28,16},{1,25},{... | collective-permute-start | bytes 393224 | tf_op jit(solution)/shard_map/ppermute | solution.py:159
  8.7 6.9 %collective-permute-start.5 = (bf16[128,512]{1,0:T(8,128)(2,1)S(1)}, bf16[128,512]{1,0:T(8,128)(2,1)S(1)}, u32[]{:S(2)}, u32[]{:S(2)}) collective-permute-start(bf16[128,512]{1,0:T(8,128)(2,1)S(1)} %get-tuple-element.51), channel_id=1, source_target_pairs={{0,12},{4,28},{8,16},{12,0},{16,8},{20,24},{24,20},{28,4},{1,13},{... | collective-permute-start | bytes 393224 | tf_op jit(solution)/shard_map/ppermute | solution.py:159
  10.2 5.4 %collective-permute-start.6 = (bf16[128,512]{1,0:T(8,128)(2,1)S(1)}, bf16[128,512]{1,0:T(8,128)(2,1)S(1)}, u32[]{:S(2)}, u32[]{:S(2)}) collective-permute-start(bf16[128,512]{1,0:T(8,128)(2,1)S(1)} %get-tuple-element.52), channel_id=1, source_target_pairs={{0,8},{4,12},{8,0},{12,4},{16,24},{20,28},{24,16},{28,20},{1,9},{5... | collective-permute-start | bytes 393224 | tf_op jit(solution)/shard_map/ppermute | solution.py:159
  12.7 5.9 %collective-permute-start.1 = (bf16[128,512]{1,0:T(8,128)(2,1)S(1)}, bf16[128,512]{1,0:T(8,128)(2,1)S(1)}, u32[]{:S(2)}, u32[]{:S(2)}) collective-permute-start(bf16[128,512]{1,0:T(8,128)(2,1)S(1)} %get-tuple-element.46), channel_id=1, source_target_pairs={{0,20},{4,16},{8,28},{12,24},{16,4},{20,0},{24,12},{28,8},{1,21},{... | collective-permute-start | bytes 393224 | tf_op jit(solution)/shard_map/ppermute | solution.py:159
  21.0 6.0 %collective-permute-start.12 = (bf16[128,384]{1,0:T(8,128)(2,1)S(1)}, bf16[128,384]{1,0:T(8,128)(2,1)S(1)}, u32[]{:S(2)}, u32[]{:S(2)}) collective-permute-start(bf16[128,384]{1,0:T(8,128)(2,1)S(1)} %get-tuple-element.66), channel_id=1, source_target_pairs={{0,16},{4,20},{8,12},{12,8},{16,0},{20,4},{24,28},{28,24},{1,17},{... | collective-permute-start | bytes 294920 | tf_op jit(solution)/shard_map/ppermute | solution.py:159
  22.6 6.7 %collective-permute-start.13 = (bf16[128,384]{1,0:T(8,128)(2,1)S(1)}, bf16[128,384]{1,0:T(8,128)(2,1)S(1)}, u32[]{:S(2)}, u32[]{:S(2)}) collective-permute-start(bf16[128,384]{1,0:T(8,128)(2,1)S(1)} %get-tuple-element.67), channel_id=1, source_target_pairs={{0,20},{4,16},{8,28},{12,24},{16,4},{20,0},{24,12},{28,8},{1,21},{... | collective-permute-start | bytes 294920 | tf_op jit(solution)/shard_map/ppermute | solution.py:159
  23.7 6.4 %collective-permute-start.7 = (bf16[128,384]{1,0:T(8,128)(2,1)S(1)}, bf16[128,384]{1,0:T(8,128)(2,1)S(1)}, u32[]{:S(2)}, u32[]{:S(2)}) collective-permute-start(bf16[128,384]{1,0:T(8,128)(2,1)S(1)} %get-tuple-element.60), channel_id=1, source_target_pairs={{0,28},{4,24},{8,20},{12,16},{16,12},{20,8},{24,4},{28,0},{1,29},{... | collective-permute-start | bytes 294920 | tf_op jit(solution)/shard_map/ppermute | solution.py:159
  24.4 8.1 %collective-permute-start.8 = (bf16[128,384]{1,0:T(8,128)(2,1)S(1)}, bf16[128,384]{1,0:T(8,128)(2,1)S(1)}, u32[]{:S(2)}, u32[]{:S(2)}) collective-permute-start(bf16[128,384]{1,0:T(8,128)(2,1)S(1)} %get-tuple-element.61), channel_id=1, source_target_pairs={{0,4},{4,0},{8,24},{12,28},{16,20},{20,16},{24,8},{28,12},{1,5},{5... | collective-permute-start | bytes 294920 | tf_op jit(solution)/shard_map/ppermute | solution.py:159
  24.7 8.5 %collective-permute-start.9 = (bf16[128,384]{1,0:T(8,128)(2,1)S(1)}, bf16[128,384]{1,0:T(8,128)(2,1)S(1)}, u32[]{:S(2)}, u32[]{:S(2)}) collective-permute-start(bf16[128,384]{1,0:T(8,128)(2,1)S(1)} %get-tuple-element.62), channel_id=1, source_target_pairs={{0,24},{4,8},{8,4},{12,20},{16,28},{20,12},{24,0},{28,16},{1,25},{... | collective-permute-start | bytes 294920 | tf_op jit(solution)/shard_map/ppermute | solution.py:159
  27.0 6.2 %collective-permute-start.10 = (bf16[128,384]{1,0:T(8,128)(2,1)S(1)}, bf16[128,384]{1,0:T(8,128)(2,1)S(1)}, u32[]{:S(2)}, u32[]{:S(2)}) collective-permute-start(bf16[128,384]{1,0:T(8,128)(2,1)S(1)} %get-tuple-element.63), channel_id=1, source_target_pairs={{0,12},{4,28},{8,16},{12,0},{16,8},{20,24},{24,20},{28,4},{1,13},{... | collective-permute-start | bytes 294920 | tf_op jit(solution)/shard_map/ppermute | solution.py:159
  29.3 3.9 %collective-permute-start.11 = (bf16[128,384]{1,0:T(8,128)(2,1)S(1)}, bf16[128,384]{1,0:T(8,128)(2,1)S(1)}, u32[]{:S(2)}, u32[]{:S(2)}) collective-permute-start(bf16[128,384]{1,0:T(8,128)(2,1)S(1)} %get-tuple-element.64), channel_id=1, source_target_pairs={{0,8},{4,12},{8,0},{12,4},{16,24},{20,28},{24,16},{28,20},{1,9},{5... | collective-permute-start | bytes 294920 | tf_op jit(solution)/shard_map/ppermute | solution.py:159

commit v4 on v3

--- a/solution.py
+++ b/solution.py
@@ -144,13 +144,13 @@
 SIDE_CORE = hop(6, 3, even_places)
 OTHER_SIDE_CORE = hop(3, 6, even_places)
 
-INWARD = (SIDE, FAR_CORE, OTHER_SIDE, SIDE_CORE, OTHER_SIDE_CORE, CORE, FAR)
+INWARD = (SIDE, FAR_CORE, OTHER_SIDE, SIDE_CORE, OTHER_SIDE_CORE, FAR, CORE)
 OUTWARD = (SIDE, FAR, FAR_CORE, OTHER_SIDE, SIDE_CORE, OTHER_SIDE_CORE, CORE)
 FIRST = 2
 EARLY = 2
 LATE = 5
 DONE = 0
-AFTER = {6: 1}
+AFTER = {5: 0, 6: 1}
 EXPONENT = math.log2(math.e) / math.sqrt(HEAD_DIM)
 
 
@@ -239,8 +239,8 @@
 
 
 def early_kernel(distances, mask_ref, *refs):
-    slabs, outs = refs[:-6], refs[-6:]
-    stack_ref, exps_ref, dprobs_ref, stats_ref, done_ref, query_ref = outs
+    slabs, outs = refs[:-7], refs[-7:]
+    stack_ref, exps_ref, dprobs_ref, stats_ref, seen_ref, done_ref, query_ref = outs
     here = flat_index(GROUP)
     for distance, slab in zip(distances, slabs):
         stack_ref[distance(here)] = slab[...]
@@ -262,7 +262,7 @@
         exps = weights(scores, seen, top)
         total = sum_of(exps)
         product = sum_of([e * d for e, d in zip(exps, dprobs)])
-        if LATE not in key_places(c):
+        if c == DONE:
             inverse = 1.0 / total
             delta = product * inverse
             terms = []
@@ -280,11 +280,14 @@
         stats_ref[c, 0:1, :width] = top
         stats_ref[c, 1:2, :width] = total
         stats_ref[c, 2:3, :width] = product
-
-
-def late_kernel(distances, mask_ref, slab, *refs):
-    stack_ref, exps_ref, dprobs_ref, stats_ref, done_ref, query_ref = refs[:6]
-    outs, out_ref = refs[6:-1], refs[-1]
+        for n, key in enumerate(key_places(c)):
+            flags = seen_by(mask_ref, here, key, (2 * c, 2 * c + 1))
+            seen_ref[c, n : n + 1] = flags.astype(jnp.float32)
+
+
+def late_kernel(distances, slab, *refs):
+    stack_ref, exps_ref, dprobs_ref, stats_ref, seen_ref, done_ref, query_ref = refs[:7]
+    outs, out_ref = refs[7:-1], refs[-1]
     here = flat_index(GROUP)
     fixed = [distance(here) for distance in distances]
     fixed = {place: out for place, out in zip(fixed, outs) if isinstance(place, int)}
@@ -311,7 +314,12 @@
         mine_q, mine_g = take(queries, 0), take(queries, 3)
         scores[u] = [b for keys in groups for b in blocks_of(times_t(take(keys, 1), mine_q))]
         dprobs[u] = [b for keys in groups for b in blocks_of(times_t(take(keys, 2), mine_g))]
-    seen = [[seen_by(mask_ref, here, p, unit[1]) for p in keys] for unit, keys in zip(units, fresh)]
+    seen = []
+    for (c, queries), keys in zip(units, fresh):
+        first = 128 * (queries[0] - 2 * c)
+        columns = slice(first, first + 128 * len(queries))
+        rows = [key_places(c).index(key) for key in keys]
+        seen.append([seen_ref[c, n : n + 1, columns] > 0 for n in rows])
     tops = [top_of(blocks, flags) if blocks else None for blocks, flags in zip(scores, seen)]
     for u, (c, queries) in enumerate(units):
         early = LATE not in queries
@@ -465,32 +473,34 @@
         if n in AFTER:
             got[n], got[AFTER[n]] = lax.optimization_barrier((got[n], got[AFTER[n]]))
         got[n] = exchange(got[n], distance)
+    soon = [n for n, distance in enumerate(INWARD) if distance is not FAR]
     pairs = jax.ShapeDtypeStruct((cells, 6 * tokens, 2 * tokens), jnp.float32)
     partial = pl.pallas_call(
-        functools.partial(early_kernel, INWARD[:-1] + (STAY,)),
+        functools.partial(early_kernel, [INWARD[n] for n in soon] + [STAY]),
         out_shape=[
             jax.ShapeDtypeStruct((devices, tokens, 4 * HEAD_DIM), jnp.bfloat16),
             pairs,
             pairs,
             jax.ShapeDtypeStruct((cells, 8, 2 * tokens), jnp.float32),
+            jax.ShapeDtypeStruct((cells, 8, 2 * tokens), jnp.float32),
             jax.ShapeDtypeStruct((2, 6 * tokens, 2 * tokens), jnp.bfloat16),
             jax.ShapeDtypeStruct((2, tokens, HEAD_DIM), jnp.bfloat16),
         ],
         in_specs=[SMEM] + [VMEM] * (devices - 1),
-        out_specs=[VMEM] * 6,
+        out_specs=[VMEM] * 7,
         compiler_params=pltpu.CompilerParams(vmem_limit_bytes=24 * MIB),
         name="early",
-    )(block_mask, *got[:-1], own)
+    )(block_mask, *[got[n] for n in soon], own)
     distances = OUTWARD + (STAY,)
     grads = pl.pallas_call(
         functools.partial(late_kernel, distances),
         out_shape=[slab_shape(tokens, 3)] * devices,
-        in_specs=[SMEM] + [VMEM] * 7,
+        in_specs=[VMEM] * 8,
         out_specs=[VMEM] * devices,
         scratch_shapes=[pltpu.VMEM((devices, tokens, 3 * HEAD_DIM), jnp.bfloat16)],
         compiler_params=pltpu.CompilerParams(vmem_limit_bytes=24 * MIB),
         name="late",
-    )(block_mask, got[-1], *partial)
+    )(got[INWARD.index(FAR)], *partial)
     back = [exchange(grad, distance) for grad, distance in zip(grads, OUTWARD)] + [grads[-1]]
     whole = jax.ShapeDtypeStruct(queries.shape, queries.dtype)
     grads = unpack(whole, distances[-1:] + distances[:EARLY], back[-1:] + back[:EARLY], "unpack")

time: 34.4 us -> 33.8 us (0.983)
  Pallas kernels: 8.75 us -> 8.14 us
    pallas_call x1, Pallas kernels: 2.5 us -> 1.89 us  [by_heads(): pl.pallas_call(functools.partial(late_kernel, distances), out_shape=[slab...]
where the time goes in v4:
time: 33.8 us; the launch traced here: 33.5 us
  starting transfers between devices  14.8 us (44%)
  waiting for transfers between devices  9.88 us (29%)
  Pallas kernels  8.14 us (24%)
  between operations  0.68 us (2%)
    ppermute x14, starting transfers between devices, exchange(): return lax.ppermute(block, GROUP, [(i, i ^ distance(i)) for i in places])  14.8 us
    ppermute x14, waiting for transfers between devices, exchange(): return lax.ppermute(block, GROUP, [(i, i ^ distance(i)) for i in places])  9.88 us
    pallas_call x2, Pallas kernels, pack(): pl.pallas_call(functools.partial(pack_kernel, distances), out_shape=outs,...  2.3 us
    pallas_call x1, Pallas kernels, by_heads(): pl.pallas_call(functools.partial(early_kernel, [INWARD[n] for n in soon]...  2.28 us
    pallas_call x1, Pallas kernels, by_heads(): pl.pallas_call(functools.partial(late_kernel, distances), out_shape=[slab...  1.89 us
    pallas_call x2, Pallas kernels, unpack(): pl.pallas_call(functools.partial(unpack_kernel, distances), out_shape=[wh...  1.68 us
  transfers between devices with their start and end apart: 14, of which 6 were waited for; matrix products, arithmetic and copies ran while one was open for 0% of the time, Pallas kernels for 13%

profile of v4, /device:TPU:0, one launch (start us, length us, event | category | flops | bytes accessed | tf_op | source)
XLA Modules:
  0.0 33.5 jit_solution(17334664266044511406)
XLA Ops:
  0.6 1.0 %pack_first.1 = (bf16[128,512]{1,0:T(8,128)(2,1)S(1)}, bf16[128,512]{1,0:T(8,128)(2,1)S(1)}) custom-call(bf16[128,1024]{1,0:T(8,128)(2,1)} %refs_0_.2, bf16[128,1024]{1,0:T(8,128)(2,1)} %refs_1_.2, bf16[128,1024]{1,0:T(8,128)(2,1)} %refs_2_.2, bf16[128,1024]{1,0:T(8,128)(2,1)} %refs_3_.2), custom_call_target="tpu_custom_call" | custom-call | tf_op jit(solution)/shard_map/pack_first/pallas_call | solution.py:435
  1.6 3.4 %collective-permute-start.2 = (bf16[128,512]{1,0:T(8,128)(2,1)S(1)}, bf16[128,512]{1,0:T(8,128)(2,1)S(1)}, u32[]{:S(2)}, u32[]{:S(2)}) collective-permute-start(bf16[128,512]{1,0:T(8,128)(2,1)S(1)} %get-tuple-element.52), channel_id=1, source_target_pairs={{0,28},{4,24},{8,20},{12,16},{16,12},{20,8},{24,4},{28,0},{1,29},{... | collective-permute-start | bytes 393224 | tf_op jit(solution)/shard_map/ppermute | solution.py:159
  5.0 0.5 %collective-permute-start = (bf16[128,512]{1,0:T(8,128)(2,1)S(1)}, bf16[128,512]{1,0:T(8,128)(2,1)S(1)}, u32[]{:S(2)}, u32[]{:S(2)}) collective-permute-start(bf16[128,512]{1,0:T(8,128)(2,1)S(1)} %get-tuple-element.47), channel_id=1, source_target_pairs={{0,16},{4,20},{8,12},{12,8},{16,0},{20,4},{24,28},{28,24},{1,17},{... | collective-permute-start | bytes 393224 | tf_op jit(solution)/shard_map/ppermute | solution.py:159
  5.5 1.3 %pack_rest.1 = (bf16[128,512]{1,0:T(8,128)(2,1)S(1)}, bf16[128,512]{1,0:T(8,128)(2,1)S(1)}, bf16[128,512]{1,0:T(8,128)(2,1)S(1)}, bf16[128,512]{1,0:T(8,128)(2,1...) custom-call(bf16[128,1024]{1,0:T(8,128)(2,1)} %refs_0_.2, ...), custom_call_target="tpu_custom_call" | custom-call | tf_op jit(solution)/shard_map/pack_rest/pallas_call | solution.py:435
  6.9 0.7 %collective-permute-start.3 = (bf16[128,512]{1,0:T(8,128)(2,1)S(1)}, bf16[128,512]{1,0:T(8,128)(2,1)S(1)}, u32[]{:S(2)}, u32[]{:S(2)}) collective-permute-start(bf16[128,512]{1,0:T(8,128)(2,1)S(1)} %get-tuple-element.54), channel_id=1, source_target_pairs={{0,4},{4,0},{8,24},{12,28},{16,20},{20,16},{24,8},{28,12},{1,5},{5... | collective-permute-start | bytes 393224 | tf_op jit(solution)/shard_map/ppermute | solution.py:159
  7.6 1.1 %collective-permute-start.4 = (bf16[128,512]{1,0:T(8,128)(2,1)S(1)}, bf16[128,512]{1,0:T(8,128)(2,1)S(1)}, u32[]{:S(2)}, u32[]{:S(2)}) collective-permute-start(bf16[128,512]{1,0:T(8,128)(2,1)S(1)} %get-tuple-element.55), channel_id=1, source_target_pairs={{0,24},{4,8},{8,4},{12,20},{16,28},{20,12},{24,0},{28,16},{1,25},{... | collective-permute-start | bytes 393224 | tf_op jit(solution)/shard_map/ppermute | solution.py:159
  8.7 1.5 %collective-permute-start.5 = (bf16[128,512]{1,0:T(8,128)(2,1)S(1)}, bf16[128,512]{1,0:T(8,128)(2,1)S(1)}, u32[]{:S(2)}, u32[]{:S(2)}) collective-permute-start(bf16[128,512]{1,0:T(8,128)(2,1)S(1)} %get-tuple-element.56), channel_id=1, source_target_pairs={{0,12},{4,28},{8,16},{12,0},{16,8},{20,24},{24,20},{28,4},{1,13},{... | collective-permute-start | bytes 393224 | tf_op jit(solution)/shard_map/ppermute | solution.py:159
  10.2 0.0 collective-permute-done.2.refs_1_
  10.2 0.1 collective-permute-start.6
  10.3 2.4 %collective-permute-done.refs_0_ = bf16[128,512]{1,0:T(8,128)(2,1)S(1)} collective-permute-done((bf16[128,512]{1,0:T(8,128)(2,1)S(1)}, bf16[128,512]{1,0:T(8,128)(2,1)S(1)}, u32[]{:S(2)}, u32[]{:S(2)}) %collective-permute-start) | collective-permute-done | bytes 131104 | tf_op jit(solution)/shard_map/ppermute | solution.py:159
  12.7 1.4 %collective-permute-start.1 = (bf16[128,512]{1,0:T(8,128)(2,1)S(1)}, bf16[128,512]{1,0:T(8,128)(2,1)S(1)}, u32[]{:S(2)}, u32[]{:S(2)}) collective-permute-start(bf16[128,512]{1,0:T(8,128)(2,1)S(1)} %get-tuple-element.48), channel_id=1, source_target_pairs={{0,20},{4,16},{8,28},{12,24},{16,4},{20,0},{24,12},{28,8},{1,21},{... | collective-permute-start | bytes 393224 | tf_op jit(solution)/shard_map/ppermute | solution.py:159
  14.0 1.5 %collective-permute-done.4.refs_3_ = bf16[128,512]{1,0:T(8,128)(2,1)S(1)} collective-permute-done((bf16[128,512]{1,0:T(8,128)(2,1)S(1)}, bf16[128,512]{1,0:T(8,128)(2,1)S(1)}, u32[]{:S(2)}, u32[]{:S(2)}) %collective-permute-start.4) | collective-permute-done | bytes 131104 | tf_op jit(solution)/shard_map/ppermute | solution.py:159
  15.5 0.0 collective-permute-done.5.refs_4_
  15.5 0.0 collective-permute-done.6.refs_5_
  15.5 2.3 %early.1 = (bf16[8,128,512]{2,1,0:T(8,128)(2,1)S(1)}, f32[4,768,256]{2,1,0:T(8,128)S(1)}, f32[4,768,256]{2,1,0:T(8,128)S(1)}, f32[4,8,256]{2,1,0:T(8,128)S(1)}, ...) custom-call(s32[8,8]{1,0:T(8,128)S(1)} %get-tuple-element.49.mask_ref, ...), custom_call_target="tpu_custom_call" | custom-call | tf_op jit(solution)/shard_map/early/pallas_call | solution.py:478
  17.8 0.7 %collective-permute-done.1.slab = bf16[128,512]{1,0:T(8,128)(2,1)S(1)} collective-permute-done((bf16[128,512]{1,0:T(8,128)(2,1)S(1)}, bf16[128,512]{1,0:T(8,128)(2,1)S(1)}, u32[]{:S(2)}, u32[]{:S(2)}) %collective-permute-start.1) | collective-permute-done | bytes 131104 | tf_op jit(solution)/shard_map/ppermute | solution.py:159
  18.5 1.9 %late.1 = (bf16[128,384]{1,0:T(8,128)(2,1)S(1)}, bf16[128,384]{1,0:T(8,128)(2,1)S(1)}, bf16[128,384]{1,0:T(8,128)(2,1)S(1)}, bf16[128,384]{1,0:T(8,128)(2,1)S(1)...) custom-call(bf16[128,512]{1,0:T(8,128)(2,1)S(1)} %collective-permute, ...), custom_call_target="tpu_custom_call" | custom-call | tf_op jit(solution)/shard_map/late/pallas_call | solution.py:495
  20.4 1.6 %collective-permute-start.12 = (bf16[128,384]{1,0:T(8,128)(2,1)S(1)}, bf16[128,384]{1,0:T(8,128)(2,1)S(1)}, u32[]{:S(2)}, u32[]{:S(2)}) collective-permute-start(bf16[128,384]{1,0:T(8,128)(2,1)S(1)} %get-tuple-element.72), channel_id=1, source_target_pairs={{0,16},{4,20},{8,12},{12,8},{16,0},{20,4},{24,28},{28,24},{1,17},{... | collective-permute-start | bytes 294920 | tf_op jit(solution)/shard_map/ppermute | solution.py:159
  22.0 1.1 %collective-permute-start.13 = (bf16[128,384]{1,0:T(8,128)(2,1)S(1)}, bf16[128,384]{1,0:T(8,128)(2,1)S(1)}, u32[]{:S(2)}, u32[]{:S(2)}) collective-permute-start(bf16[128,384]{1,0:T(8,128)(2,1)S(1)} %get-tuple-element.73), channel_id=1, source_target_pairs={{0,20},{4,16},{8,28},{12,24},{16,4},{20,0},{24,12},{28,8},{1,21},{... | collective-permute-start | bytes 294920 | tf_op jit(solution)/shard_map/ppermute | solution.py:159
  23.1 0.7 %collective-permute-start.7 = (bf16[128,384]{1,0:T(8,128)(2,1)S(1)}, bf16[128,384]{1,0:T(8,128)(2,1)S(1)}, u32[]{:S(2)}, u32[]{:S(2)}) collective-permute-start(bf16[128,384]{1,0:T(8,128)(2,1)S(1)} %get-tuple-element.66), channel_id=1, source_target_pairs={{0,28},{4,24},{8,20},{12,16},{16,12},{20,8},{24,4},{28,0},{1,29},{... | collective-permute-start | bytes 294920 | tf_op jit(solution)/shard_map/ppermute | solution.py:159
  23.8 0.4 %collective-permute-start.8 = (bf16[128,384]{1,0:T(8,128)(2,1)S(1)}, bf16[128,384]{1,0:T(8,128)(2,1)S(1)}, u32[]{:S(2)}, u32[]{:S(2)}) collective-permute-start(bf16[128,384]{1,0:T(8,128)(2,1)S(1)} %get-tuple-element.67), channel_id=1, source_target_pairs={{0,4},{4,0},{8,24},{12,28},{16,20},{20,16},{24,8},{28,12},{1,5},{5... | collective-permute-start | bytes 294920 | tf_op jit(solution)/shard_map/ppermute | solution.py:159
  24.1 2.3 %collective-permute-start.9 = (bf16[128,384]{1,0:T(8,128)(2,1)S(1)}, bf16[128,384]{1,0:T(8,128)(2,1)S(1)}, u32[]{:S(2)}, u32[]{:S(2)}) collective-permute-start(bf16[128,384]{1,0:T(8,128)(2,1)S(1)} %get-tuple-element.68), channel_id=1, source_target_pairs={{0,24},{4,8},{8,4},{12,20},{16,28},{20,12},{24,0},{28,16},{1,25},{... | collective-permute-start | bytes 294920 | tf_op jit(solution)/shard_map/ppermute | solution.py:159
  26.4 0.0 collective-permute-done.12.refs_1_
  26.4 0.0 collective-permute-start.10
  26.5 2.2 %collective-permute-done.13.refs_2_ = bf16[128,384]{1,0:T(8,128)(2,1)S(1)} collective-permute-done((bf16[128,384]{1,0:T(8,128)(2,1)S(1)}, bf16[128,384]{1,0:T(8,128)(2,1)S(1)}, u32[]{:S(2)}, u32[]{:S(2)}) %collective-permute-start.13) | collective-permute-done | bytes 98336 | tf_op jit(solution)/shard_map/ppermute | solution.py:159
  28.7 0.0 collective-permute-start.11
  28.7 0.8 %unpack.1 = (bf16[128,1024]{1,0:T(8,128)(2,1)}, bf16[128,1024]{1,0:T(8,128)(2,1)}, bf16[128,1024]{1,0:T(8,128)(2,1)}) custom-call(bf16[128,384]{1,0:T(8,128)(2,1)S(1)} %get-tuple-element.71.refs_0_, bf16[128,384]{1,0:T(8,128)(2,1)S(1)} %collective-permute-done.12.refs_1_, bf16[128,384]{1,0:T(8,128)(2,1)S(1)} %collective-permute-done.13.refs_2_), custom_call_target="tpu_custom_call" | custom-call | tf_op jit(solution)/shard_map/unpack/pallas_call | solution.py:448
  29.5 2.3 %collective-permute-done.8.refs_1_ = bf16[128,384]{1,0:T(8,128)(2,1)S(1)} collective-permute-done((bf16[128,384]{1,0:T(8,128)(2,1)S(1)}, bf16[128,384]{1,0:T(8,128)(2,1)S(1)}, u32[]{:S(2)}, u32[]{:S(2)}) %collective-permute-start.8) | collective-permute-done | bytes 98336 | tf_op jit(solution)/shard_map/ppermute | solution.py:159
  31.8 0.7 %collective-permute-done.9.refs_2_ = bf16[128,384]{1,0:T(8,128)(2,1)S(1)} collective-permute-done((bf16[128,384]{1,0:T(8,128)(2,1)S(1)}, bf16[128,384]{1,0:T(8,128)(2,1)S(1)}, u32[]{:S(2)}, u32[]{:S(2)}) %collective-permute-start.9) | collective-permute-done | bytes 98336 | tf_op jit(solution)/shard_map/ppermute | solution.py:159
  32.6 0.0 collective-permute-done.10.refs_3_
  32.6 0.0 collective-permute-done.11.refs_4_
  32.6 0.9 %unpack_last.1 = (bf16[128,1024]{1,0:T(8,128)(2,1)}, bf16[128,1024]{1,0:T(8,128)(2,1)}, bf16[128,1024]{1,0:T(8,128)(2,1)}) custom-call(bf16[128,384]{1,0:T(8,128)(2,1)S(1)} %collective-permute-done.7.refs_0_, bf16[128,384]{1,0:T(8,128)(2,1)S(1)} %collective-permute-done.8.refs_1_, ...), custom_call_target="tpu_custom_call", output_to_operand_aliasing={{0}: (5, {}), {1}: (6, {}), {2}: (7, {})} | custom-call | tf_op jit(solution)/shard_map/unpack_last/pallas_call | solution.py:448
  (2 shorter events, 0.0 us)
Async XLA Ops:
  1.6 8.6 %collective-permute-start.2 = (bf16[128,512]{1,0:T(8,128)(2,1)S(1)}, bf16[128,512]{1,0:T(8,128)(2,1)S(1)}, u32[]{:S(2)}, u32[]{:S(2)}) collective-permute-start(bf16[128,512]{1,0:T(8,128)(2,1)S(1)} %get-tuple-element.52), channel_id=1, source_target_pairs={{0,28},{4,24},{8,20},{12,16},{16,12},{20,8},{24,4},{28,0},{1,29},{... | collective-permute-start | bytes 393224 | tf_op jit(solution)/shard_map/ppermute | solution.py:159
  5.0 7.7 %collective-permute-start = (bf16[128,512]{1,0:T(8,128)(2,1)S(1)}, bf16[128,512]{1,0:T(8,128)(2,1)S(1)}, u32[]{:S(2)}, u32[]{:S(2)}) collective-permute-start(bf16[128,512]{1,0:T(8,128)(2,1)S(1)} %get-tuple-element.47), channel_id=1, source_target_pairs={{0,16},{4,20},{8,12},{12,8},{16,0},{20,4},{24,28},{28,24},{1,17},{... | collective-permute-start | bytes 393224 | tf_op jit(solution)/shard_map/ppermute | solution.py:159
  6.9 7.2 %collective-permute-start.3 = (bf16[128,512]{1,0:T(8,128)(2,1)S(1)}, bf16[128,512]{1,0:T(8,128)(2,1)S(1)}, u32[]{:S(2)}, u32[]{:S(2)}) collective-permute-start(bf16[128,512]{1,0:T(8,128)(2,1)S(1)} %get-tuple-element.54), channel_id=1, source_target_pairs={{0,4},{4,0},{8,24},{12,28},{16,20},{20,16},{24,8},{28,12},{1,5},{5... | collective-permute-start | bytes 393224 | tf_op jit(solution)/shard_map/ppermute | solution.py:159
  7.6 7.9 %collective-permute-start.4 = (bf16[128,512]{1,0:T(8,128)(2,1)S(1)}, bf16[128,512]{1,0:T(8,128)(2,1)S(1)}, u32[]{:S(2)}, u32[]{:S(2)}) collective-permute-start(bf16[128,512]{1,0:T(8,128)(2,1)S(1)} %get-tuple-element.55), channel_id=1, source_target_pairs={{0,24},{4,8},{8,4},{12,20},{16,28},{20,12},{24,0},{28,16},{1,25},{... | collective-permute-start | bytes 393224 | tf_op jit(solution)/shard_map/ppermute | solution.py:159
  8.7 6.9 %collective-permute-start.5 = (bf16[128,512]{1,0:T(8,128)(2,1)S(1)}, bf16[128,512]{1,0:T(8,128)(2,1)S(1)}, u32[]{:S(2)}, u32[]{:S(2)}) collective-permute-start(bf16[128,512]{1,0:T(8,128)(2,1)S(1)} %get-tuple-element.56), channel_id=1, source_target_pairs={{0,12},{4,28},{8,16},{12,0},{16,8},{20,24},{24,20},{28,4},{1,13},{... | collective-permute-start | bytes 393224 | tf_op jit(solution)/shard_map/ppermute | solution.py:159
  10.2 5.4 %collective-permute-start.6 = (bf16[128,512]{1,0:T(8,128)(2,1)S(1)}, bf16[128,512]{1,0:T(8,128)(2,1)S(1)}, u32[]{:S(2)}, u32[]{:S(2)}) collective-permute-start(bf16[128,512]{1,0:T(8,128)(2,1)S(1)} %get-tuple-element.57), channel_id=1, source_target_pairs={{0,8},{4,12},{8,0},{12,4},{16,24},{20,28},{24,16},{28,20},{1,9},{5... | collective-permute-start | bytes 393224 | tf_op jit(solution)/shard_map/ppermute | solution.py:159
  12.7 5.9 %collective-permute-start.1 = (bf16[128,512]{1,0:T(8,128)(2,1)S(1)}, bf16[128,512]{1,0:T(8,128)(2,1)S(1)}, u32[]{:S(2)}, u32[]{:S(2)}) collective-permute-start(bf16[128,512]{1,0:T(8,128)(2,1)S(1)} %get-tuple-element.48), channel_id=1, source_target_pairs={{0,20},{4,16},{8,28},{12,24},{16,4},{20,0},{24,12},{28,8},{1,21},{... | collective-permute-start | bytes 393224 | tf_op jit(solution)/shard_map/ppermute | solution.py:159
  20.4 6.0 %collective-permute-start.12 = (bf16[128,384]{1,0:T(8,128)(2,1)S(1)}, bf16[128,384]{1,0:T(8,128)(2,1)S(1)}, u32[]{:S(2)}, u32[]{:S(2)}) collective-permute-start(bf16[128,384]{1,0:T(8,128)(2,1)S(1)} %get-tuple-element.72), channel_id=1, source_target_pairs={{0,16},{4,20},{8,12},{12,8},{16,0},{20,4},{24,28},{28,24},{1,17},{... | collective-permute-start | bytes 294920 | tf_op jit(solution)/shard_map/ppermute | solution.py:159
  22.0 6.7 %collective-permute-start.13 = (bf16[128,384]{1,0:T(8,128)(2,1)S(1)}, bf16[128,384]{1,0:T(8,128)(2,1)S(1)}, u32[]{:S(2)}, u32[]{:S(2)}) collective-permute-start(bf16[128,384]{1,0:T(8,128)(2,1)S(1)} %get-tuple-element.73), channel_id=1, source_target_pairs={{0,20},{4,16},{8,28},{12,24},{16,4},{20,0},{24,12},{28,8},{1,21},{... | collective-permute-start | bytes 294920 | tf_op jit(solution)/shard_map/ppermute | solution.py:159
  23.1 6.4 %collective-permute-start.7 = (bf16[128,384]{1,0:T(8,128)(2,1)S(1)}, bf16[128,384]{1,0:T(8,128)(2,1)S(1)}, u32[]{:S(2)}, u32[]{:S(2)}) collective-permute-start(bf16[128,384]{1,0:T(8,128)(2,1)S(1)} %get-tuple-element.66), channel_id=1, source_target_pairs={{0,28},{4,24},{8,20},{12,16},{16,12},{20,8},{24,4},{28,0},{1,29},{... | collective-permute-start | bytes 294920 | tf_op jit(solution)/shard_map/ppermute | solution.py:159
  23.8 8.1 %collective-permute-start.8 = (bf16[128,384]{1,0:T(8,128)(2,1)S(1)}, bf16[128,384]{1,0:T(8,128)(2,1)S(1)}, u32[]{:S(2)}, u32[]{:S(2)}) collective-permute-start(bf16[128,384]{1,0:T(8,128)(2,1)S(1)} %get-tuple-element.67), channel_id=1, source_target_pairs={{0,4},{4,0},{8,24},{12,28},{16,20},{20,16},{24,8},{28,12},{1,5},{5... | collective-permute-start | bytes 294920 | tf_op jit(solution)/shard_map/ppermute | solution.py:159
  24.1 8.4 %collective-permute-start.9 = (bf16[128,384]{1,0:T(8,128)(2,1)S(1)}, bf16[128,384]{1,0:T(8,128)(2,1)S(1)}, u32[]{:S(2)}, u32[]{:S(2)}) collective-permute-start(bf16[128,384]{1,0:T(8,128)(2,1)S(1)} %get-tuple-element.68), channel_id=1, source_target_pairs={{0,24},{4,8},{8,4},{12,20},{16,28},{20,12},{24,0},{28,16},{1,25},{... | collective-permute-start | bytes 294920 | tf_op jit(solution)/shard_map/ppermute | solution.py:159
  26.4 6.2 %collective-permute-start.10 = (bf16[128,384]{1,0:T(8,128)(2,1)S(1)}, bf16[128,384]{1,0:T(8,128)(2,1)S(1)}, u32[]{:S(2)}, u32[]{:S(2)}) collective-permute-start(bf16[128,384]{1,0:T(8,128)(2,1)S(1)} %get-tuple-element.69), channel_id=1, source_target_pairs={{0,12},{4,28},{8,16},{12,0},{16,8},{20,24},{24,20},{28,4},{1,13},{... | collective-permute-start | bytes 294920 | tf_op jit(solution)/shard_map/ppermute | solution.py:159
  28.7 3.9 %collective-permute-start.11 = (bf16[128,384]{1,0:T(8,128)(2,1)S(1)}, bf16[128,384]{1,0:T(8,128)(2,1)S(1)}, u32[]{:S(2)}, u32[]{:S(2)}) collective-permute-start(bf16[128,384]{1,0:T(8,128)(2,1)S(1)} %get-tuple-element.70), channel_id=1, source_target_pairs={{0,8},{4,12},{8,0},{12,4},{16,24},{20,28},{24,16},{28,20},{1,9},{5... | collective-permute-start | bytes 294920 | tf_op jit(solution)/shard_map/ppermute | solution.py:159

commit v5 on v4

--- a/solution.py
+++ b/solution.py
@@ -144,13 +144,13 @@
 SIDE_CORE = hop(6, 3, even_places)
 OTHER_SIDE_CORE = hop(3, 6, even_places)
 
-INWARD = (SIDE, FAR_CORE, OTHER_SIDE, SIDE_CORE, OTHER_SIDE_CORE, FAR, CORE)
-OUTWARD = (SIDE, FAR, FAR_CORE, OTHER_SIDE, SIDE_CORE, OTHER_SIDE_CORE, CORE)
+INWARD = (FAR_CORE, SIDE, CORE, OTHER_SIDE, SIDE_CORE, FAR, OTHER_SIDE_CORE)
+OUTWARD = (FAR, FAR_CORE, SIDE, OTHER_SIDE, SIDE_CORE, OTHER_SIDE_CORE, CORE)
 FIRST = 2
 EARLY = 2
 LATE = 5
 DONE = 0
-AFTER = {5: 0, 6: 1}
+AFTER = {}
 EXPONENT = math.log2(math.e) / math.sqrt(HEAD_DIM)
 
 

time: 33.8 us -> 33.3 us (0.985)
  waiting for transfers between devices: 9.88 us -> 8.57 us
  starting transfers between devices: 14.8 us -> 15.7 us
    ppermute x14, waiting for transfers between devices: 9.88 us -> 8.57 us  [exchange(): return lax.ppermute(block, GROUP, [(i, i ^ distance(i)) for i in places])]
    ppermute x14, starting transfers between devices: 14.8 us -> 15.7 us  [exchange(): return lax.ppermute(block, GROUP, [(i, i ^ distance(i)) for i in places])]
  transfers between devices with their start and end apart: 14 -> 14, of which waited for: 6 -> 9; matrix products, arithmetic and copies ran while one was open for 0% -> 0% of each run, Pallas kernels for 13% -> 13%
where the time goes in v5:
time: 33.3 us; the launch traced here: 33 us
  starting transfers between devices  15.7 us (47%)
  waiting for transfers between devices  8.57 us (26%)
  Pallas kernels  8.14 us (24%)
  between operations  0.67 us (2%)
    ppermute x14, starting transfers between devices, exchange(): return lax.ppermute(block, GROUP, [(i, i ^ distance(i)) for i in places])  15.7 us
    ppermute x14, waiting for transfers between devices, exchange(): return lax.ppermute(block, GROUP, [(i, i ^ distance(i)) for i in places])  8.57 us
    pallas_call x2, Pallas kernels, pack(): pl.pallas_call(functools.partial(pack_kernel, distances), out_shape=outs,...  2.29 us
    pallas_call x1, Pallas kernels, by_heads(): pl.pallas_call(functools.partial(early_kernel, [INWARD[n] for n in soon]...  2.28 us
    pallas_call x1, Pallas kernels, by_heads(): pl.pallas_call(functools.partial(late_kernel, distances), out_shape=[slab...  1.89 us
    pallas_call x2, Pallas kernels, unpack(): pl.pallas_call(functools.partial(unpack_kernel, distances), out_shape=[wh...  1.67 us
  transfers between devices with their start and end apart: 14, of which 9 were waited for; matrix products, arithmetic and copies ran while one was open for 0% of the time, Pallas kernels for 13%

profile of v5, /device:TPU:0, one launch (start us, length us, event | category | flops | bytes accessed | tf_op | source)
XLA Modules:
  0.0 33.0 jit_solution(10828467473521902867)
XLA Ops:
  0.6 1.0 %pack_first.1 = (bf16[128,512]{1,0:T(8,128)(2,1)S(1)}, bf16[128,512]{1,0:T(8,128)(2,1)S(1)}) custom-call(bf16[128,1024]{1,0:T(8,128)(2,1)} %refs_0_.2, bf16[128,1024]{1,0:T(8,128)(2,1)} %refs_1_.2, bf16[128,1024]{1,0:T(8,128)(2,1)} %refs_2_.2, bf16[128,1024]{1,0:T(8,128)(2,1)} %refs_3_.2), custom_call_target="tpu_custom_call" | custom-call | tf_op jit(solution)/shard_map/pack_first/pallas_call | solution.py:435
  1.6 3.4 %collective-permute-start.1 = (bf16[128,512]{1,0:T(8,128)(2,1)S(1)}, bf16[128,512]{1,0:T(8,128)(2,1)S(1)}, u32[]{:S(2)}, u32[]{:S(2)}) collective-permute-start(bf16[128,512]{1,0:T(8,128)(2,1)S(1)} %get-tuple-element.44), channel_id=1, source_target_pairs={{0,28},{4,24},{8,20},{12,16},{16,12},{20,8},{24,4},{28,0},{1,29},{... | collective-permute-start | bytes 393224 | tf_op jit(solution)/shard_map/ppermute | solution.py:159
  5.0 0.5 %collective-permute-start.2 = (bf16[128,512]{1,0:T(8,128)(2,1)S(1)}, bf16[128,512]{1,0:T(8,128)(2,1)S(1)}, u32[]{:S(2)}, u32[]{:S(2)}) collective-permute-start(bf16[128,512]{1,0:T(8,128)(2,1)S(1)} %get-tuple-element.45), channel_id=1, source_target_pairs={{0,16},{4,20},{8,12},{12,8},{16,0},{20,4},{24,28},{28,24},{1,17},{... | collective-permute-start | bytes 393224 | tf_op jit(solution)/shard_map/ppermute | solution.py:159
  5.5 1.3 %pack_rest.1 = (bf16[128,512]{1,0:T(8,128)(2,1)S(1)}, bf16[128,512]{1,0:T(8,128)(2,1)S(1)}, bf16[128,512]{1,0:T(8,128)(2,1)S(1)}, bf16[128,512]{1,0:T(8,128)(2,1...) custom-call(bf16[128,1024]{1,0:T(8,128)(2,1)} %refs_0_.2, ...), custom_call_target="tpu_custom_call" | custom-call | tf_op jit(solution)/shard_map/pack_rest/pallas_call | solution.py:435
  6.9 0.4 %collective-permute-start.3 = (bf16[128,512]{1,0:T(8,128)(2,1)S(1)}, bf16[128,512]{1,0:T(8,128)(2,1)S(1)}, u32[]{:S(2)}, u32[]{:S(2)}) collective-permute-start(bf16[128,512]{1,0:T(8,128)(2,1)S(1)} %get-tuple-element.46), channel_id=1, source_target_pairs={{0,8},{4,12},{8,0},{12,4},{16,24},{20,28},{24,16},{28,20},{1,9},{5... | collective-permute-start | bytes 393224 | tf_op jit(solution)/shard_map/ppermute | solution.py:159
  7.3 1.5 %collective-permute-start.4 = (bf16[128,512]{1,0:T(8,128)(2,1)S(1)}, bf16[128,512]{1,0:T(8,128)(2,1)S(1)}, u32[]{:S(2)}, u32[]{:S(2)}) collective-permute-start(bf16[128,512]{1,0:T(8,128)(2,1)S(1)} %get-tuple-element.47), channel_id=1, source_target_pairs={{0,4},{4,0},{8,24},{12,28},{16,20},{20,16},{24,8},{28,12},{1,5},{5... | collective-permute-start | bytes 393224 | tf_op jit(solution)/shard_map/ppermute | solution.py:159
  8.8 0.0 collective-permute-start.5
  8.8 0.1 collective-permute-done.1.refs_0_
  8.9 2.1 %collective-permute-start.6 = (bf16[128,512]{1,0:T(8,128)(2,1)S(1)}, bf16[128,512]{1,0:T(8,128)(2,1)S(1)}, u32[]{:S(2)}, u32[]{:S(2)}) collective-permute-start(bf16[128,512]{1,0:T(8,128)(2,1)S(1)} %get-tuple-element.49), channel_id=1, source_target_pairs={{0,12},{4,28},{8,16},{12,0},{16,8},{20,24},{24,20},{28,4},{1,13},{... | collective-permute-start | bytes 393224 | tf_op jit(solution)/shard_map/ppermute | solution.py:159
  11.1 1.4 %collective-permute-done.2.refs_1_ = bf16[128,512]{1,0:T(8,128)(2,1)S(1)} collective-permute-done((bf16[128,512]{1,0:T(8,128)(2,1)S(1)}, bf16[128,512]{1,0:T(8,128)(2,1)S(1)}, u32[]{:S(2)}, u32[]{:S(2)}) %collective-permute-start.2) | collective-permute-done | bytes 131104 | tf_op jit(solution)/shard_map/ppermute | solution.py:159
  12.5 1.4 %collective-permute-start = (bf16[128,512]{1,0:T(8,128)(2,1)S(1)}, bf16[128,512]{1,0:T(8,128)(2,1)S(1)}, u32[]{:S(2)}, u32[]{:S(2)}) collective-permute-start(bf16[128,512]{1,0:T(8,128)(2,1)S(1)} %get-tuple-element.42), channel_id=1, source_target_pairs={{0,20},{4,16},{8,28},{12,24},{16,4},{20,0},{24,12},{28,8},{1,21},{... | collective-permute-start | bytes 393224 | tf_op jit(solution)/shard_map/ppermute | solution.py:159
  13.9 0.0 collective-permute-done.3.refs_2_
  14.0 0.0 collective-permute-done.4.refs_3_
  14.0 1.3 %collective-permute-done.5.refs_4_ = bf16[128,512]{1,0:T(8,128)(2,1)S(1)} collective-permute-done((bf16[128,512]{1,0:T(8,128)(2,1)S(1)}, bf16[128,512]{1,0:T(8,128)(2,1)S(1)}, u32[]{:S(2)}, u32[]{:S(2)}) %collective-permute-start.5) | collective-permute-done | bytes 131104 | tf_op jit(solution)/shard_map/ppermute | solution.py:159
  15.3 0.0 collective-permute-done.6.refs_5_
  15.3 2.3 %early.1 = (bf16[8,128,512]{2,1,0:T(8,128)(2,1)S(1)}, f32[4,768,256]{2,1,0:T(8,128)S(1)}, f32[4,768,256]{2,1,0:T(8,128)S(1)}, f32[4,8,256]{2,1,0:T(8,128)S(1)}, ...) custom-call(s32[8,8]{1,0:T(8,128)S(1)} %get-tuple-element.43.mask_ref, ...), custom_call_target="tpu_custom_call" | custom-call | tf_op jit(solution)/shard_map/early/pallas_call | solution.py:478
  17.5 0.8 %collective-permute-done.slab = bf16[128,512]{1,0:T(8,128)(2,1)S(1)} collective-permute-done((bf16[128,512]{1,0:T(8,128)(2,1)S(1)}, bf16[128,512]{1,0:T(8,128)(2,1)S(1)}, u32[]{:S(2)}, u32[]{:S(2)}) %collective-permute-start) | collective-permute-done | bytes 131104 | tf_op jit(solution)/shard_map/ppermute | solution.py:159
  18.4 1.9 %late.1 = (bf16[128,384]{1,0:T(8,128)(2,1)S(1)}, bf16[128,384]{1,0:T(8,128)(2,1)S(1)}, bf16[128,384]{1,0:T(8,128)(2,1)S(1)}, bf16[128,384]{1,0:T(8,128)(2,1)S(1)...) custom-call(bf16[128,512]{1,0:T(8,128)(2,1)S(1)} %collective-permute, ...), custom_call_target="tpu_custom_call" | custom-call | tf_op jit(solution)/shard_map/late/pallas_call | solution.py:495
  20.3 2.4 %collective-permute-start.12 = (bf16[128,384]{1,0:T(8,128)(2,1)S(1)}, bf16[128,384]{1,0:T(8,128)(2,1)S(1)}, u32[]{:S(2)}, u32[]{:S(2)}) collective-permute-start(bf16[128,384]{1,0:T(8,128)(2,1)S(1)} %get-tuple-element.64), channel_id=1, source_target_pairs={{0,20},{4,16},{8,28},{12,24},{16,4},{20,0},{24,12},{28,8},{1,21},{... | collective-permute-start | bytes 294920 | tf_op jit(solution)/shard_map/ppermute | solution.py:159
  22.7 0.9 %collective-permute-start.7 = (bf16[128,384]{1,0:T(8,128)(2,1)S(1)}, bf16[128,384]{1,0:T(8,128)(2,1)S(1)}, u32[]{:S(2)}, u32[]{:S(2)}) collective-permute-start(bf16[128,384]{1,0:T(8,128)(2,1)S(1)} %get-tuple-element.58), channel_id=1, source_target_pairs={{0,16},{4,20},{8,12},{12,8},{16,0},{20,4},{24,28},{28,24},{1,17},{... | collective-permute-start | bytes 294920 | tf_op jit(solution)/shard_map/ppermute | solution.py:159
  23.5 1.5 %collective-permute-start.8 = (bf16[128,384]{1,0:T(8,128)(2,1)S(1)}, bf16[128,384]{1,0:T(8,128)(2,1)S(1)}, u32[]{:S(2)}, u32[]{:S(2)}) collective-permute-start(bf16[128,384]{1,0:T(8,128)(2,1)S(1)} %get-tuple-element.59), channel_id=1, source_target_pairs={{0,4},{4,0},{8,24},{12,28},{16,20},{20,16},{24,8},{28,12},{1,5},{5... | collective-permute-start | bytes 294920 | tf_op jit(solution)/shard_map/ppermute | solution.py:159
  25.0 0.8 %collective-permute-start.9 = (bf16[128,384]{1,0:T(8,128)(2,1)S(1)}, bf16[128,384]{1,0:T(8,128)(2,1)S(1)}, u32[]{:S(2)}, u32[]{:S(2)}) collective-permute-start(bf16[128,384]{1,0:T(8,128)(2,1)S(1)} %get-tuple-element.60), channel_id=1, source_target_pairs={{0,24},{4,8},{8,4},{12,20},{16,28},{20,12},{24,0},{28,16},{1,25},{... | collective-permute-start | bytes 294920 | tf_op jit(solution)/shard_map/ppermute | solution.py:159
  25.9 0.0 collective-permute-done.12.refs_1_
  25.9 0.6 %collective-permute-start.10 = (bf16[128,384]{1,0:T(8,128)(2,1)S(1)}, bf16[128,384]{1,0:T(8,128)(2,1)S(1)}, u32[]{:S(2)}, u32[]{:S(2)}) collective-permute-start(bf16[128,384]{1,0:T(8,128)(2,1)S(1)} %get-tuple-element.61), channel_id=1, source_target_pairs={{0,12},{4,28},{8,16},{12,0},{16,8},{20,24},{24,20},{28,4},{1,13},{... | collective-permute-start | bytes 294920 | tf_op jit(solution)/shard_map/ppermute | solution.py:159
  26.5 2.2 %collective-permute-done.13.refs_2_ = bf16[128,384]{1,0:T(8,128)(2,1)S(1)} collective-permute-done((bf16[128,384]{1,0:T(8,128)(2,1)S(1)}, bf16[128,384]{1,0:T(8,128)(2,1)S(1)}, u32[]{:S(2)}, u32[]{:S(2)}) %collective-permute-start.13) | collective-permute-done | bytes 98336 | tf_op jit(solution)/shard_map/ppermute | solution.py:159
  28.7 0.8 %unpack.1 = (bf16[128,1024]{1,0:T(8,128)(2,1)}, bf16[128,1024]{1,0:T(8,128)(2,1)}, bf16[128,1024]{1,0:T(8,128)(2,1)}) custom-call(bf16[128,384]{1,0:T(8,128)(2,1)S(1)} %get-tuple-element.63.refs_0_, bf16[128,384]{1,0:T(8,128)(2,1)S(1)} %collective-permute-done.12.refs_1_, bf16[128,384]{1,0:T(8,128)(2,1)S(1)} %collective-permute-done.13.refs_2_), custom_call_target="tpu_custom_call" | custom-call | tf_op jit(solution)/shard_map/unpack/pallas_call | solution.py:448
  29.4 0.7 %collective-permute-done.7.refs_0_ = bf16[128,384]{1,0:T(8,128)(2,1)S(1)} collective-permute-done((bf16[128,384]{1,0:T(8,128)(2,1)S(1)}, bf16[128,384]{1,0:T(8,128)(2,1)S(1)}, u32[]{:S(2)}, u32[]{:S(2)}) %collective-permute-start.7) | collective-permute-done | bytes 98336 | tf_op jit(solution)/shard_map/ppermute | solution.py:159
  30.1 0.2 collective-permute-done.8.refs_1_
  30.3 1.7 %collective-permute-done.9.refs_2_ = bf16[128,384]{1,0:T(8,128)(2,1)S(1)} collective-permute-done((bf16[128,384]{1,0:T(8,128)(2,1)S(1)}, bf16[128,384]{1,0:T(8,128)(2,1)S(1)}, u32[]{:S(2)}, u32[]{:S(2)}) %collective-permute-start.9) | collective-permute-done | bytes 98336 | tf_op jit(solution)/shard_map/ppermute | solution.py:159
  32.1 0.1 collective-permute-done.10.refs_3_
  32.1 0.0 collective-permute-done.11.refs_4_
  32.1 0.9 %unpack_last.1 = (bf16[128,1024]{1,0:T(8,128)(2,1)}, bf16[128,1024]{1,0:T(8,128)(2,1)}, bf16[128,1024]{1,0:T(8,128)(2,1)}) custom-call(bf16[128,384]{1,0:T(8,128)(2,1)S(1)} %collective-permute-done.7.refs_0_, bf16[128,384]{1,0:T(8,128)(2,1)S(1)} %collective-permute-done.8.refs_1_, ...), custom_call_target="tpu_custom_call", output_to_operand_aliasing={{0}: (5, {}), {1}: (6, {}), {2}: (7, {})} | custom-call | tf_op jit(solution)/shard_map/unpack_last/pallas_call | solution.py:448
  (2 shorter events, 0.0 us)
Async XLA Ops:
  1.6 7.3 %collective-permute-start.1 = (bf16[128,512]{1,0:T(8,128)(2,1)S(1)}, bf16[128,512]{1,0:T(8,128)(2,1)S(1)}, u32[]{:S(2)}, u32[]{:S(2)}) collective-permute-start(bf16[128,512]{1,0:T(8,128)(2,1)S(1)} %get-tuple-element.44), channel_id=1, source_target_pairs={{0,28},{4,24},{8,20},{12,16},{16,12},{20,8},{24,4},{28,0},{1,29},{... | collective-permute-start | bytes 393224 | tf_op jit(solution)/shard_map/ppermute | solution.py:159
  5.0 7.5 %collective-permute-start.2 = (bf16[128,512]{1,0:T(8,128)(2,1)S(1)}, bf16[128,512]{1,0:T(8,128)(2,1)S(1)}, u32[]{:S(2)}, u32[]{:S(2)}) collective-permute-start(bf16[128,512]{1,0:T(8,128)(2,1)S(1)} %get-tuple-element.45), channel_id=1, source_target_pairs={{0,16},{4,20},{8,12},{12,8},{16,0},{20,4},{24,28},{28,24},{1,17},{... | collective-permute-start | bytes 393224 | tf_op jit(solution)/shard_map/ppermute | solution.py:159
  6.9 7.1 %collective-permute-start.3 = (bf16[128,512]{1,0:T(8,128)(2,1)S(1)}, bf16[128,512]{1,0:T(8,128)(2,1)S(1)}, u32[]{:S(2)}, u32[]{:S(2)}) collective-permute-start(bf16[128,512]{1,0:T(8,128)(2,1)S(1)} %get-tuple-element.46), channel_id=1, source_target_pairs={{0,8},{4,12},{8,0},{12,4},{16,24},{20,28},{24,16},{28,20},{1,9},{5... | collective-permute-start | bytes 393224 | tf_op jit(solution)/shard_map/ppermute | solution.py:159
  7.3 6.6 %collective-permute-start.4 = (bf16[128,512]{1,0:T(8,128)(2,1)S(1)}, bf16[128,512]{1,0:T(8,128)(2,1)S(1)}, u32[]{:S(2)}, u32[]{:S(2)}) collective-permute-start(bf16[128,512]{1,0:T(8,128)(2,1)S(1)} %get-tuple-element.47), channel_id=1, source_target_pairs={{0,4},{4,0},{8,24},{12,28},{16,20},{20,16},{24,8},{28,12},{1,5},{5... | collective-permute-start | bytes 393224 | tf_op jit(solution)/shard_map/ppermute | solution.py:159
  8.8 6.4 %collective-permute-start.5 = (bf16[128,512]{1,0:T(8,128)(2,1)S(1)}, bf16[128,512]{1,0:T(8,128)(2,1)S(1)}, u32[]{:S(2)}, u32[]{:S(2)}) collective-permute-start(bf16[128,512]{1,0:T(8,128)(2,1)S(1)} %get-tuple-element.48), channel_id=1, source_target_pairs={{0,24},{4,8},{8,4},{12,20},{16,28},{20,12},{24,0},{28,16},{1,25},{... | collective-permute-start | bytes 393224 | tf_op jit(solution)/shard_map/ppermute | solution.py:159
  8.9 6.3 %collective-permute-start.6 = (bf16[128,512]{1,0:T(8,128)(2,1)S(1)}, bf16[128,512]{1,0:T(8,128)(2,1)S(1)}, u32[]{:S(2)}, u32[]{:S(2)}) collective-permute-start(bf16[128,512]{1,0:T(8,128)(2,1)S(1)} %get-tuple-element.49), channel_id=1, source_target_pairs={{0,12},{4,28},{8,16},{12,0},{16,8},{20,24},{24,20},{28,4},{1,13},{... | collective-permute-start | bytes 393224 | tf_op jit(solution)/shard_map/ppermute | solution.py:159
  12.5 5.9 %collective-permute-start = (bf16[128,512]{1,0:T(8,128)(2,1)S(1)}, bf16[128,512]{1,0:T(8,128)(2,1)S(1)}, u32[]{:S(2)}, u32[]{:S(2)}) collective-permute-start(bf16[128,512]{1,0:T(8,128)(2,1)S(1)} %get-tuple-element.42), channel_id=1, source_target_pairs={{0,20},{4,16},{8,28},{12,24},{16,4},{20,0},{24,12},{28,8},{1,21},{... | collective-permute-start | bytes 393224 | tf_op jit(solution)/shard_map/ppermute | solution.py:159
  20.3 5.6 %collective-permute-start.12 = (bf16[128,384]{1,0:T(8,128)(2,1)S(1)}, bf16[128,384]{1,0:T(8,128)(2,1)S(1)}, u32[]{:S(2)}, u32[]{:S(2)}) collective-permute-start(bf16[128,384]{1,0:T(8,128)(2,1)S(1)} %get-tuple-element.64), channel_id=1, source_target_pairs={{0,20},{4,16},{8,28},{12,24},{16,4},{20,0},{24,12},{28,8},{1,21},{... | collective-permute-start | bytes 294920 | tf_op jit(solution)/shard_map/ppermute | solution.py:159
  22.7 6.0 %collective-permute-start.13 = (bf16[128,384]{1,0:T(8,128)(2,1)S(1)}, bf16[128,384]{1,0:T(8,128)(2,1)S(1)}, u32[]{:S(2)}, u32[]{:S(2)}) collective-permute-start(bf16[128,384]{1,0:T(8,128)(2,1)S(1)} %get-tuple-element.65), channel_id=1, source_target_pairs={{0,28},{4,24},{8,20},{12,16},{16,12},{20,8},{24,4},{28,0},{1,29},{... | collective-permute-start | bytes 294920 | tf_op jit(solution)/shard_map/ppermute | solution.py:159
  22.7 7.5 %collective-permute-start.7 = (bf16[128,384]{1,0:T(8,128)(2,1)S(1)}, bf16[128,384]{1,0:T(8,128)(2,1)S(1)}, u32[]{:S(2)}, u32[]{:S(2)}) collective-permute-start(bf16[128,384]{1,0:T(8,128)(2,1)S(1)} %get-tuple-element.58), channel_id=1, source_target_pairs={{0,16},{4,20},{8,12},{12,8},{16,0},{20,4},{24,28},{28,24},{1,17},{... | collective-permute-start | bytes 294920 | tf_op jit(solution)/shard_map/ppermute | solution.py:159
  23.5 6.8 %collective-permute-start.8 = (bf16[128,384]{1,0:T(8,128)(2,1)S(1)}, bf16[128,384]{1,0:T(8,128)(2,1)S(1)}, u32[]{:S(2)}, u32[]{:S(2)}) collective-permute-start(bf16[128,384]{1,0:T(8,128)(2,1)S(1)} %get-tuple-element.59), channel_id=1, source_target_pairs={{0,4},{4,0},{8,24},{12,28},{16,20},{20,16},{24,8},{28,12},{1,5},{5... | collective-permute-start | bytes 294920 | tf_op jit(solution)/shard_map/ppermute | solution.py:159
  25.0 7.0 %collective-permute-start.9 = (bf16[128,384]{1,0:T(8,128)(2,1)S(1)}, bf16[128,384]{1,0:T(8,128)(2,1)S(1)}, u32[]{:S(2)}, u32[]{:S(2)}) collective-permute-start(bf16[128,384]{1,0:T(8,128)(2,1)S(1)} %get-tuple-element.60), channel_id=1, source_target_pairs={{0,24},{4,8},{8,4},{12,20},{16,28},{20,12},{24,0},{28,16},{1,25},{... | collective-permute-start | bytes 294920 | tf_op jit(solution)/shard_map/ppermute | solution.py:159
  25.9 6.3 %collective-permute-start.10 = (bf16[128,384]{1,0:T(8,128)(2,1)S(1)}, bf16[128,384]{1,0:T(8,128)(2,1)S(1)}, u32[]{:S(2)}, u32[]{:S(2)}) collective-permute-start(bf16[128,384]{1,0:T(8,128)(2,1)S(1)} %get-tuple-element.61), channel_id=1, source_target_pairs={{0,12},{4,28},{8,16},{12,0},{16,8},{20,24},{24,20},{28,4},{1,13},{... | collective-permute-start | bytes 294920 | tf_op jit(solution)/shard_map/ppermute | solution.py:159
  28.7 3.5 %collective-permute-start.11 = (bf16[128,384]{1,0:T(8,128)(2,1)S(1)}, bf16[128,384]{1,0:T(8,128)(2,1)S(1)}, u32[]{:S(2)}, u32[]{:S(2)}) collective-permute-start(bf16[128,384]{1,0:T(8,128)(2,1)S(1)} %get-tuple-element.62), channel_id=1, source_target_pairs={{0,8},{4,12},{8,0},{12,4},{16,24},{20,28},{24,16},{28,20},{1,9},{5... | collective-permute-start | bytes 294920 | tf_op jit(solution)/shard_map/ppermute | solution.py:159

commit v6 on v5

--- a/solution.py
+++ b/solution.py
@@ -149,6 +149,7 @@
 FIRST = 2
 EARLY = 2
 LATE = 5
+BEYOND = (4, 5, 6, 7)
 DONE = 0
 AFTER = {}
 EXPONENT = math.log2(math.e) / math.sqrt(HEAD_DIM)
@@ -285,24 +286,34 @@
             seen_ref[c, n : n + 1] = flags.astype(jnp.float32)
 
 
-def late_kernel(distances, slab, *refs):
-    stack_ref, exps_ref, dprobs_ref, stats_ref, seen_ref, done_ref, query_ref = refs[:7]
-    outs, out_ref = refs[7:-1], refs[-1]
-    here = flat_index(GROUP)
-    fixed = [distance(here) for distance in distances]
-    fixed = {place: out for place, out in zip(fixed, outs) if isinstance(place, int)}
-    scale = 1.0 / math.sqrt(HEAD_DIM)
-    cells = stack_ref.shape[0] // 2
-
+def taker(slab, stack_ref):
     def take(places, n):
         columns = slice(n * HEAD_DIM, (n + 1) * HEAD_DIM)
         parts = [slab[:, columns] if p == LATE else stack_ref[p, :, columns] for p in places]
         return jnp.concatenate(parts, axis=0)
 
-    def whole(n):
-        return [take((2 * c, 2 * c + 1), n) for c in range(cells)]
-
-    q, k, v, g = (whole(n) for n in range(4))
+    return take
+
+
+def put(out, n, value):
+    out[:, n * HEAD_DIM : (n + 1) * HEAD_DIM] = value.astype(jnp.bfloat16)
+
+
+def put_pair_grads(take, c, probs_low, dscores, outs):
+    q, g = take(key_places(c), 0), take(key_places(c), 3)
+    dk = jnp.dot(dscores, q, preferred_element_type=jnp.float32) * (1.0 / math.sqrt(HEAD_DIM))
+    dv = jnp.dot(probs_low, g, preferred_element_type=jnp.float32)
+    for a, out in enumerate(outs):
+        put(out, 1, dk[128 * a : 128 * (a + 1)])
+        put(out, 2, dv[128 * a : 128 * (a + 1)])
+
+
+def late_kernel(slab, *refs):
+    stack_ref, exps_ref, dprobs_ref, stats_ref, seen_ref, done_ref = refs[:6]
+    outs = dict(zip(BEYOND, refs[6:10]))
+    probs_out, dscores_out, query_out = refs[10:]
+    cells = stack_ref.shape[0] // 2
+    take = taker(slab, stack_ref)
 
     units = [(c, (2 * c, 2 * c + 1)) for c in range(cells) if c not in (DONE, LATE // 2)]
     units = [(LATE // 2, (place,)) for place in (LATE - 1, LATE)] + units
@@ -356,15 +367,6 @@
             dscores.append((probs * (term - delta[u])).astype(jnp.bfloat16))
         return probs_low, dscores
 
-    def put(n, c, value):
-        low = value.astype(jnp.bfloat16).reshape(2, 128, HEAD_DIM)
-        for place in (2 * c, 2 * c + 1):
-            out = fixed.get(place, out_ref.at[place])
-            out[:, n * HEAD_DIM : (n + 1) * HEAD_DIM] = low[place - 2 * c]
-
-    def joined(blocks, c, axis):
-        return jnp.concatenate([blocks[n] for n in near_cells(c)], axis=axis)
-
     probs_low = [{} for _ in range(cells)]
     dscores = [{} for _ in range(cells)]
 
@@ -382,37 +384,42 @@
             probs_low[n][c] = jnp.concatenate(pair[0][2 * t : 2 * t + 2], axis=0)
             dscores[n][c] = jnp.concatenate(pair[1][2 * t : 2 * t + 2], axis=0)
 
-    def put_value_grad(c):
-        low = joined(probs_low[c], c, 1)
-        put(2, c, jnp.dot(low, joined(g, c, 0), preferred_element_type=jnp.float32))
-
-    def put_key_grad(c):
-        low = joined(dscores[c], c, 1)
-        put(1, c, jnp.dot(low, joined(q, c, 0), preferred_element_type=jnp.float32) * scale)
-
-    def put_query_grad(c):
-        if c == DONE:
-            put(0, c, query_ref[...])
-            return
-        terms = jnp.concatenate([dscores[n][c] for n in near_cells(c)], axis=0)
-        put(0, c, query_grad(joined(k, c, 0), terms))
+    def joined(blocks, c):
+        return jnp.concatenate([blocks[n] for n in near_cells(c)], axis=1)
 
     rows_of(2)
     rows_of(1)
     rows_of(3)
     rows_of(0)
-    put_value_grad(0)
-    put_value_grad(1)
-    put_value_grad(2)
-    put_value_grad(3)
-    put_key_grad(0)
-    put_key_grad(1)
-    put_key_grad(2)
-    put_key_grad(3)
-    put_query_grad(0)
-    put_query_grad(1)
-    put_query_grad(2)
-    put_query_grad(3)
+    for c in (2, 3):
+        places = (2 * c, 2 * c + 1)
+        put_pair_grads(take, c, joined(probs_low[c], c), joined(dscores[c], c), [outs[p] for p in places])
+    for c in (2, 3, 1):
+        terms = jnp.concatenate([dscores[n][c] for n in near_cells(c)], axis=0)
+        dq = query_grad(take(key_places(c), 1), terms)
+        if c == 1:
+            query_out[...] = dq
+        else:
+            for a in range(2):
+                put(outs[2 * c + a], 0, dq[a])
+    for n in (0, 1):
+        probs_out[n] = joined(probs_low[n], n)
+        dscores_out[n] = joined(dscores[n], n)
+
+
+def rest_kernel(distances, slab, stack_ref, probs_ref, dscores_ref, *refs):
+    query_refs, kept, outs, out_ref = refs[:2], refs[2:4], refs[4:-1], refs[-1]
+    here = flat_index(GROUP)
+    fixed = [distance(here) for distance in distances]
+    fixed = {place: out for place, out in zip(fixed, outs) if isinstance(place, int)}
+    take = taker(slab, stack_ref)
+    for c in (0, 1):
+        targets = [fixed.get(place, out_ref.at[place]) for place in (2 * c, 2 * c + 1)]
+        put_pair_grads(take, c, probs_ref[c], dscores_ref[c], targets)
+        for a, target in enumerate(targets):
+            put(target, 0, query_refs[c][a])
+    for place, ref in zip((4, 6), kept):
+        out_ref[place] = ref[...]
     for distance, out in zip(distances, outs):
         if not isinstance(distance(here), int):
             out[...] = out_ref[distance(here)]
@@ -491,16 +498,30 @@
         compiler_params=pltpu.CompilerParams(vmem_limit_bytes=24 * MIB),
         name="early",
     )(block_mask, *[got[n] for n in soon], own)
+    stack, *partial, query_grad_0 = partial
+    slab = got[INWARD.index(FAR)]
+    low = jax.ShapeDtypeStruct((2, 2 * tokens, 6 * tokens), jnp.bfloat16)
+    *beyond, probs_low, dscores, query_grad_1 = pl.pallas_call(
+        late_kernel,
+        out_shape=[slab_shape(tokens, 3)] * len(BEYOND)
+        + [low, low, jax.ShapeDtypeStruct((2, tokens, HEAD_DIM), jnp.bfloat16)],
+        in_specs=[VMEM] * 7,
+        out_specs=[VMEM] * (len(BEYOND) + 3),
+        compiler_params=pltpu.CompilerParams(vmem_limit_bytes=24 * MIB),
+        name="late",
+    )(slab, stack, *partial)
+    beyond = dict(zip(BEYOND, beyond))
     distances = OUTWARD + (STAY,)
-    grads = pl.pallas_call(
-        functools.partial(late_kernel, distances),
-        out_shape=[slab_shape(tokens, 3)] * devices,
+    rest = pl.pallas_call(
+        functools.partial(rest_kernel, distances[2:]),
+        out_shape=[slab_shape(tokens, 3)] * (devices - 2),
         in_specs=[VMEM] * 8,
-        out_specs=[VMEM] * devices,
+        out_specs=[VMEM] * (devices - 2),
         scratch_shapes=[pltpu.VMEM((devices, tokens, 3 * HEAD_DIM), jnp.bfloat16)],
         compiler_params=pltpu.CompilerParams(vmem_limit_bytes=24 * MIB),
-        name="late",
-    )(got[INWARD.index(FAR)], *partial)
+        name="rest",
+    )(slab, stack, probs_low, dscores, query_grad_0, query_grad_1, beyond[4], beyond[6])
+    grads = [beyond[5], beyond[7], *rest]
     back = [exchange(grad, distance) for grad, distance in zip(grads, OUTWARD)] + [grads[-1]]
     whole = jax.ShapeDtypeStruct(queries.shape, queries.dtype)
     grads = unpack(whole, distances[-1:] + distances[:EARLY], back[-1:] + back[:EARLY], "unpack")

time: 33.3 us -> 33 us (level)
  waiting for transfers between devices: 8.57 us -> 8.03 us
    ppermute x14, waiting for transfers between devices: 8.57 us -> 8.03 us  [exchange(): return lax.ppermute(block, GROUP, [(i, i ^ distance(i)) for i in places])]
    pallas_call x1 -> x2, Pallas kernels: 1.89 us -> 2.13 us  [the longest x1 1.48 us: by_heads(): pl.pallas_call(late_kernel, out_shape=[slab_shape(tokens, 3)] * len(BEYON...]
  transfers between devices with their start and end apart: 14 -> 14, of which waited for: 9 -> 9; matrix products, arithmetic and copies ran while one was open for 0% -> 0% of each run, Pallas kernels for 13% -> 15%
where the time goes in v6:
time: 33 us; the launch traced here: 32.7 us
  starting transfers between devices  15.7 us (48%)
  Pallas kernels  8.31 us (25%)
  waiting for transfers between devices  8.03 us (24%)
  between operations  0.68 us (2%)
    ppermute x14, starting transfers between devices, exchange(): return lax.ppermute(block, GROUP, [(i, i ^ distance(i)) for i in places])  15.7 us
    ppermute x14, waiting for transfers between devices, exchange(): return lax.ppermute(block, GROUP, [(i, i ^ distance(i)) for i in places])  8.03 us
    pallas_call x2, Pallas kernels, pack(): pl.pallas_call(functools.partial(pack_kernel, distances), out_shape=outs,...  2.29 us
    pallas_call x1, Pallas kernels, by_heads(): pl.pallas_call(functools.partial(early_kernel, [INWARD[n] for n in soon]...  2.21 us
    pallas_call x2, Pallas kernels, unpack(): pl.pallas_call(functools.partial(unpack_kernel, distances), out_shape=[wh...  1.67 us
    pallas_call x1, Pallas kernels, by_heads(): pl.pallas_call(late_kernel, out_shape=[slab_shape(tokens, 3)] * len(BEYON...  1.48 us
  transfers between devices with their start and end apart: 14, of which 9 were waited for; matrix products, arithmetic and copies ran while one was open for 0% of the time, Pallas kernels for 15%

profile of v6, /device:TPU:0, one launch (start us, length us, event | category | flops | bytes accessed | tf_op | source)
XLA Modules:
  0.0 32.7 jit_solution(9058708418937450461)
XLA Ops:
  0.6 1.0 %pack_first.1 = (bf16[128,512]{1,0:T(8,128)(2,1)S(1)}, bf16[128,512]{1,0:T(8,128)(2,1)S(1)}) custom-call(bf16[128,1024]{1,0:T(8,128)(2,1)} %refs_0_.2, bf16[128,1024]{1,0:T(8,128)(2,1)} %refs_1_.2, bf16[128,1024]{1,0:T(8,128)(2,1)} %refs_2_.2, bf16[128,1024]{1,0:T(8,128)(2,1)} %refs_3_.2), custom_call_target="tpu_custom_call" | custom-call | tf_op jit(solution)/shard_map/pack_first/pallas_call | solution.py:442
  1.6 3.4 %collective-permute-start.1 = (bf16[128,512]{1,0:T(8,128)(2,1)S(1)}, bf16[128,512]{1,0:T(8,128)(2,1)S(1)}, u32[]{:S(2)}, u32[]{:S(2)}) collective-permute-start(bf16[128,512]{1,0:T(8,128)(2,1)S(1)} %get-tuple-element.49), channel_id=1, source_target_pairs={{0,28},{4,24},{8,20},{12,16},{16,12},{20,8},{24,4},{28,0},{1,29},{... | collective-permute-start | bytes 393224 | tf_op jit(solution)/shard_map/ppermute | solution.py:160
  5.0 0.5 %collective-permute-start.2 = (bf16[128,512]{1,0:T(8,128)(2,1)S(1)}, bf16[128,512]{1,0:T(8,128)(2,1)S(1)}, u32[]{:S(2)}, u32[]{:S(2)}) collective-permute-start(bf16[128,512]{1,0:T(8,128)(2,1)S(1)} %get-tuple-element.50), channel_id=1, source_target_pairs={{0,16},{4,20},{8,12},{12,8},{16,0},{20,4},{24,28},{28,24},{1,17},{... | collective-permute-start | bytes 393224 | tf_op jit(solution)/shard_map/ppermute | solution.py:160
  5.5 1.3 %pack_rest.1 = (bf16[128,512]{1,0:T(8,128)(2,1)S(1)}, bf16[128,512]{1,0:T(8,128)(2,1)S(1)}, bf16[128,512]{1,0:T(8,128)(2,1)S(1)}, bf16[128,512]{1,0:T(8,128)(2,1...) custom-call(bf16[128,1024]{1,0:T(8,128)(2,1)} %refs_0_.2, ...), custom_call_target="tpu_custom_call" | custom-call | tf_op jit(solution)/shard_map/pack_rest/pallas_call | solution.py:442
  6.9 0.4 %collective-permute-start.3 = (bf16[128,512]{1,0:T(8,128)(2,1)S(1)}, bf16[128,512]{1,0:T(8,128)(2,1)S(1)}, u32[]{:S(2)}, u32[]{:S(2)}) collective-permute-start(bf16[128,512]{1,0:T(8,128)(2,1)S(1)} %get-tuple-element.51), channel_id=1, source_target_pairs={{0,8},{4,12},{8,0},{12,4},{16,24},{20,28},{24,16},{28,20},{1,9},{5... | collective-permute-start | bytes 393224 | tf_op jit(solution)/shard_map/ppermute | solution.py:160
  7.3 1.5 %collective-permute-start.4 = (bf16[128,512]{1,0:T(8,128)(2,1)S(1)}, bf16[128,512]{1,0:T(8,128)(2,1)S(1)}, u32[]{:S(2)}, u32[]{:S(2)}) collective-permute-start(bf16[128,512]{1,0:T(8,128)(2,1)S(1)} %get-tuple-element.52), channel_id=1, source_target_pairs={{0,4},{4,0},{8,24},{12,28},{16,20},{20,16},{24,8},{28,12},{1,5},{5... | collective-permute-start | bytes 393224 | tf_op jit(solution)/shard_map/ppermute | solution.py:160
  8.8 0.0 collective-permute-start.5
  8.8 0.1 collective-permute-done.1.refs_0_
  8.9 2.1 %collective-permute-start.6 = (bf16[128,512]{1,0:T(8,128)(2,1)S(1)}, bf16[128,512]{1,0:T(8,128)(2,1)S(1)}, u32[]{:S(2)}, u32[]{:S(2)}) collective-permute-start(bf16[128,512]{1,0:T(8,128)(2,1)S(1)} %get-tuple-element.54), channel_id=1, source_target_pairs={{0,12},{4,28},{8,16},{12,0},{16,8},{20,24},{24,20},{28,4},{1,13},{... | collective-permute-start | bytes 393224 | tf_op jit(solution)/shard_map/ppermute | solution.py:160
  11.1 1.4 %collective-permute-done.2.refs_1_ = bf16[128,512]{1,0:T(8,128)(2,1)S(1)} collective-permute-done((bf16[128,512]{1,0:T(8,128)(2,1)S(1)}, bf16[128,512]{1,0:T(8,128)(2,1)S(1)}, u32[]{:S(2)}, u32[]{:S(2)}) %collective-permute-start.2) | collective-permute-done | bytes 131104 | tf_op jit(solution)/shard_map/ppermute | solution.py:160
  12.5 1.4 %collective-permute-start = (bf16[128,512]{1,0:T(8,128)(2,1)S(1)}, bf16[128,512]{1,0:T(8,128)(2,1)S(1)}, u32[]{:S(2)}, u32[]{:S(2)}) collective-permute-start(bf16[128,512]{1,0:T(8,128)(2,1)S(1)} %get-tuple-element.47), channel_id=1, source_target_pairs={{0,20},{4,16},{8,28},{12,24},{16,4},{20,0},{24,12},{28,8},{1,21},{... | collective-permute-start | bytes 393224 | tf_op jit(solution)/shard_map/ppermute | solution.py:160
  13.9 0.0 collective-permute-done.3.refs_2_
  14.0 0.0 collective-permute-done.4.refs_3_
  14.0 1.3 %collective-permute-done.5.refs_4_ = bf16[128,512]{1,0:T(8,128)(2,1)S(1)} collective-permute-done((bf16[128,512]{1,0:T(8,128)(2,1)S(1)}, bf16[128,512]{1,0:T(8,128)(2,1)S(1)}, u32[]{:S(2)}, u32[]{:S(2)}) %collective-permute-start.5) | collective-permute-done | bytes 131104 | tf_op jit(solution)/shard_map/ppermute | solution.py:160
  15.3 2.2 %early.1 = (bf16[8,128,512]{2,1,0:T(8,128)(2,1)S(1)}, f32[4,768,256]{2,1,0:T(8,128)S(1)}, f32[4,768,256]{2,1,0:T(8,128)S(1)}, f32[4,8,256]{2,1,0:T(8,128)S(1)}, ...) custom-call(s32[8,8]{1,0:T(8,128)S(1)} %get-tuple-element.48.mask_ref, ...), custom_call_target="tpu_custom_call" | custom-call | tf_op jit(solution)/shard_map/early/pallas_call | solution.py:485
  17.5 0.9 %collective-permute-done.slab = bf16[128,512]{1,0:T(8,128)(2,1)S(1)} collective-permute-done((bf16[128,512]{1,0:T(8,128)(2,1)S(1)}, bf16[128,512]{1,0:T(8,128)(2,1)S(1)}, u32[]{:S(2)}, u32[]{:S(2)}) %collective-permute-start) | collective-permute-done | bytes 131104 | tf_op jit(solution)/shard_map/ppermute | solution.py:160
  18.4 1.5 %late.1 = (bf16[128,384]{1,0:T(8,128)(2,1)S(1)}, bf16[128,384]{1,0:T(8,128)(2,1)S(1)}, bf16[128,384]{1,0:T(8,128)(2,1)S(1)}, bf16[128,384]{1,0:T(8,128)(2,1)S(1)...) custom-call(bf16[128,512]{1,0:T(8,128)(2,1)S(1)} %collective-permute-done.sla, ...), custom_call_target="tpu_custom_call" | custom-call | tf_op jit(solution)/shard_map/late/pallas_call | solution.py:504
  19.9 2.4 %collective-permute-start.12 = (bf16[128,384]{1,0:T(8,128)(2,1)S(1)}, bf16[128,384]{1,0:T(8,128)(2,1)S(1)}, u32[]{:S(2)}, u32[]{:S(2)}) collective-permute-start(bf16[128,384]{1,0:T(8,128)(2,1)S(1)} %get-tuple-element.74), channel_id=1, source_target_pairs={{0,20},{4,16},{8,28},{12,24},{16,4},{20,0},{24,12},{28,8},{1,21},{... | collective-permute-start | bytes 294920 | tf_op jit(solution)/shard_map/ppermute | solution.py:160
  22.3 0.7 %rest.1 = (bf16[128,384]{1,0:T(8,128)(2,1)S(1)}, bf16[128,384]{1,0:T(8,128)(2,1)S(1)}, bf16[128,384]{1,0:T(8,128)(2,1)S(1)}, bf16[128,384]{1,0:T(8,128)(2,1)S(1)...) custom-call(bf16[128,512]{1,0:T(8,128)(2,1)S(1)} %collective-permute-done.slab, ...), custom_call_target="tpu_custom_call" | custom-call | tf_op jit(solution)/shard_map/rest/pallas_call | solution.py:515
  22.9 0.8 %collective-permute-start.7 = (bf16[128,384]{1,0:T(8,128)(2,1)S(1)}, bf16[128,384]{1,0:T(8,128)(2,1)S(1)}, u32[]{:S(2)}, u32[]{:S(2)}) collective-permute-start(bf16[128,384]{1,0:T(8,128)(2,1)S(1)} %get-tuple-element.68), channel_id=1, source_target_pairs={{0,16},{4,20},{8,12},{12,8},{16,0},{20,4},{24,28},{28,24},{1,17},{... | collective-permute-start | bytes 294920 | tf_op jit(solution)/shard_map/ppermute | solution.py:160
  23.8 1.6 %collective-permute-start.8 = (bf16[128,384]{1,0:T(8,128)(2,1)S(1)}, bf16[128,384]{1,0:T(8,128)(2,1)S(1)}, u32[]{:S(2)}, u32[]{:S(2)}) collective-permute-start(bf16[128,384]{1,0:T(8,128)(2,1)S(1)} %get-tuple-element.69), channel_id=1, source_target_pairs={{0,4},{4,0},{8,24},{12,28},{16,20},{20,16},{24,8},{28,12},{1,5},{5... | collective-permute-start | bytes 294920 | tf_op jit(solution)/shard_map/ppermute | solution.py:160
  25.4 0.8 %collective-permute-start.9 = (bf16[128,384]{1,0:T(8,128)(2,1)S(1)}, bf16[128,384]{1,0:T(8,128)(2,1)S(1)}, u32[]{:S(2)}, u32[]{:S(2)}) collective-permute-start(bf16[128,384]{1,0:T(8,128)(2,1)S(1)} %get-tuple-element.70), channel_id=1, source_target_pairs={{0,24},{4,8},{8,4},{12,20},{16,28},{20,12},{24,0},{28,16},{1,25},{... | collective-permute-start | bytes 294920 | tf_op jit(solution)/shard_map/ppermute | solution.py:160
  26.2 0.0 collective-permute-done.12.refs_1_
  26.2 0.6 %collective-permute-start.10 = (bf16[128,384]{1,0:T(8,128)(2,1)S(1)}, bf16[128,384]{1,0:T(8,128)(2,1)S(1)}, u32[]{:S(2)}, u32[]{:S(2)}) collective-permute-start(bf16[128,384]{1,0:T(8,128)(2,1)S(1)} %get-tuple-element.71), channel_id=1, source_target_pairs={{0,12},{4,28},{8,16},{12,0},{16,8},{20,24},{24,20},{28,4},{1,13},{... | collective-permute-start | bytes 294920 | tf_op jit(solution)/shard_map/ppermute | solution.py:160
  26.8 1.4 %collective-permute-done.13.refs_2_ = bf16[128,384]{1,0:T(8,128)(2,1)S(1)} collective-permute-done((bf16[128,384]{1,0:T(8,128)(2,1)S(1)}, bf16[128,384]{1,0:T(8,128)(2,1)S(1)}, u32[]{:S(2)}, u32[]{:S(2)}) %collective-permute-start.13) | collective-permute-done | bytes 98336 | tf_op jit(solution)/shard_map/ppermute | solution.py:160
  28.2 0.8 %unpack.1 = (bf16[128,1024]{1,0:T(8,128)(2,1)}, bf16[128,1024]{1,0:T(8,128)(2,1)}, bf16[128,1024]{1,0:T(8,128)(2,1)}) custom-call(bf16[128,384]{1,0:T(8,128)(2,1)S(1)} %get-tuple-element.73.refs_0_, bf16[128,384]{1,0:T(8,128)(2,1)S(1)} %collective-permute-done.12.refs_1_, bf16[128,384]{1,0:T(8,128)(2,1)S(1)} %collective-permute-done.13.refs_2_), custom_call_target="tpu_custom_call" | custom-call | tf_op jit(solution)/shard_map/unpack/pallas_call | solution.py:455
  29.0 0.6 %collective-permute-done.7.refs_0_ = bf16[128,384]{1,0:T(8,128)(2,1)S(1)} collective-permute-done((bf16[128,384]{1,0:T(8,128)(2,1)S(1)}, bf16[128,384]{1,0:T(8,128)(2,1)S(1)}, u32[]{:S(2)}, u32[]{:S(2)}) %collective-permute-start.7) | collective-permute-done | bytes 98336 | tf_op jit(solution)/shard_map/ppermute | solution.py:160
  29.6 0.3 collective-permute-done.8.refs_1_
  29.9 1.8 %collective-permute-done.9.refs_2_ = bf16[128,384]{1,0:T(8,128)(2,1)S(1)} collective-permute-done((bf16[128,384]{1,0:T(8,128)(2,1)S(1)}, bf16[128,384]{1,0:T(8,128)(2,1)S(1)}, u32[]{:S(2)}, u32[]{:S(2)}) %collective-permute-start.9) | collective-permute-done | bytes 98336 | tf_op jit(solution)/shard_map/ppermute | solution.py:160
  31.7 0.1 collective-permute-done.10.refs_3_
  31.8 0.0 collective-permute-done.11.refs_4_
  31.8 0.9 %unpack_last.1 = (bf16[128,1024]{1,0:T(8,128)(2,1)}, bf16[128,1024]{1,0:T(8,128)(2,1)}, bf16[128,1024]{1,0:T(8,128)(2,1)}) custom-call(bf16[128,384]{1,0:T(8,128)(2,1)S(1)} %collective-permute-done.7.refs_0_, bf16[128,384]{1,0:T(8,128)(2,1)S(1)} %collective-permute-done.8.refs_1_, ...), custom_call_target="tpu_custom_call", output_to_operand_aliasing={{0}: (5, {}), {1}: (6, {}), {2}: (7, {})} | custom-call | tf_op jit(solution)/shard_map/unpack_last/pallas_call | solution.py:455
  (3 shorter events, 0.0 us)
Async XLA Ops:
  1.6 7.3 %collective-permute-start.1 = (bf16[128,512]{1,0:T(8,128)(2,1)S(1)}, bf16[128,512]{1,0:T(8,128)(2,1)S(1)}, u32[]{:S(2)}, u32[]{:S(2)}) collective-permute-start(bf16[128,512]{1,0:T(8,128)(2,1)S(1)} %get-tuple-element.49), channel_id=1, source_target_pairs={{0,28},{4,24},{8,20},{12,16},{16,12},{20,8},{24,4},{28,0},{1,29},{... | collective-permute-start | bytes 393224 | tf_op jit(solution)/shard_map/ppermute | solution.py:160
  5.0 7.5 %collective-permute-start.2 = (bf16[128,512]{1,0:T(8,128)(2,1)S(1)}, bf16[128,512]{1,0:T(8,128)(2,1)S(1)}, u32[]{:S(2)}, u32[]{:S(2)}) collective-permute-start(bf16[128,512]{1,0:T(8,128)(2,1)S(1)} %get-tuple-element.50), channel_id=1, source_target_pairs={{0,16},{4,20},{8,12},{12,8},{16,0},{20,4},{24,28},{28,24},{1,17},{... | collective-permute-start | bytes 393224 | tf_op jit(solution)/shard_map/ppermute | solution.py:160
  6.9 7.1 %collective-permute-start.3 = (bf16[128,512]{1,0:T(8,128)(2,1)S(1)}, bf16[128,512]{1,0:T(8,128)(2,1)S(1)}, u32[]{:S(2)}, u32[]{:S(2)}) collective-permute-start(bf16[128,512]{1,0:T(8,128)(2,1)S(1)} %get-tuple-element.51), channel_id=1, source_target_pairs={{0,8},{4,12},{8,0},{12,4},{16,24},{20,28},{24,16},{28,20},{1,9},{5... | collective-permute-start | bytes 393224 | tf_op jit(solution)/shard_map/ppermute | solution.py:160
  7.3 6.6 %collective-permute-start.4 = (bf16[128,512]{1,0:T(8,128)(2,1)S(1)}, bf16[128,512]{1,0:T(8,128)(2,1)S(1)}, u32[]{:S(2)}, u32[]{:S(2)}) collective-permute-start(bf16[128,512]{1,0:T(8,128)(2,1)S(1)} %get-tuple-element.52), channel_id=1, source_target_pairs={{0,4},{4,0},{8,24},{12,28},{16,20},{20,16},{24,8},{28,12},{1,5},{5... | collective-permute-start | bytes 393224 | tf_op jit(solution)/shard_map/ppermute | solution.py:160
  8.8 6.4 %collective-permute-start.5 = (bf16[128,512]{1,0:T(8,128)(2,1)S(1)}, bf16[128,512]{1,0:T(8,128)(2,1)S(1)}, u32[]{:S(2)}, u32[]{:S(2)}) collective-permute-start(bf16[128,512]{1,0:T(8,128)(2,1)S(1)} %get-tuple-element.53), channel_id=1, source_target_pairs={{0,24},{4,8},{8,4},{12,20},{16,28},{20,12},{24,0},{28,16},{1,25},{... | collective-permute-start | bytes 393224 | tf_op jit(solution)/shard_map/ppermute | solution.py:160
  8.9 6.3 %collective-permute-start.6 = (bf16[128,512]{1,0:T(8,128)(2,1)S(1)}, bf16[128,512]{1,0:T(8,128)(2,1)S(1)}, u32[]{:S(2)}, u32[]{:S(2)}) collective-permute-start(bf16[128,512]{1,0:T(8,128)(2,1)S(1)} %get-tuple-element.54), channel_id=1, source_target_pairs={{0,12},{4,28},{8,16},{12,0},{16,8},{20,24},{24,20},{28,4},{1,13},{... | collective-permute-start | bytes 393224 | tf_op jit(solution)/shard_map/ppermute | solution.py:160
  12.5 5.9 %collective-permute-start = (bf16[128,512]{1,0:T(8,128)(2,1)S(1)}, bf16[128,512]{1,0:T(8,128)(2,1)S(1)}, u32[]{:S(2)}, u32[]{:S(2)}) collective-permute-start(bf16[128,512]{1,0:T(8,128)(2,1)S(1)} %get-tuple-element.47), channel_id=1, source_target_pairs={{0,20},{4,16},{8,28},{12,24},{16,4},{20,0},{24,12},{28,8},{1,21},{... | collective-permute-start | bytes 393224 | tf_op jit(solution)/shard_map/ppermute | solution.py:160
  19.9 6.3 %collective-permute-start.12 = (bf16[128,384]{1,0:T(8,128)(2,1)S(1)}, bf16[128,384]{1,0:T(8,128)(2,1)S(1)}, u32[]{:S(2)}, u32[]{:S(2)}) collective-permute-start(bf16[128,384]{1,0:T(8,128)(2,1)S(1)} %get-tuple-element.74), channel_id=1, source_target_pairs={{0,20},{4,16},{8,28},{12,24},{16,4},{20,0},{24,12},{28,8},{1,21},{... | collective-permute-start | bytes 294920 | tf_op jit(solution)/shard_map/ppermute | solution.py:160
  22.3 5.9 %collective-permute-start.13 = (bf16[128,384]{1,0:T(8,128)(2,1)S(1)}, bf16[128,384]{1,0:T(8,128)(2,1)S(1)}, u32[]{:S(2)}, u32[]{:S(2)}) collective-permute-start(bf16[128,384]{1,0:T(8,128)(2,1)S(1)} %get-tuple-element.75), channel_id=1, source_target_pairs={{0,28},{4,24},{8,20},{12,16},{16,12},{20,8},{24,4},{28,0},{1,29},{... | collective-permute-start | bytes 294920 | tf_op jit(solution)/shard_map/ppermute | solution.py:160
  22.9 6.7 %collective-permute-start.7 = (bf16[128,384]{1,0:T(8,128)(2,1)S(1)}, bf16[128,384]{1,0:T(8,128)(2,1)S(1)}, u32[]{:S(2)}, u32[]{:S(2)}) collective-permute-start(bf16[128,384]{1,0:T(8,128)(2,1)S(1)} %get-tuple-element.68), channel_id=1, source_target_pairs={{0,16},{4,20},{8,12},{12,8},{16,0},{20,4},{24,28},{28,24},{1,17},{... | collective-permute-start | bytes 294920 | tf_op jit(solution)/shard_map/ppermute | solution.py:160
  23.8 6.1 %collective-permute-start.8 = (bf16[128,384]{1,0:T(8,128)(2,1)S(1)}, bf16[128,384]{1,0:T(8,128)(2,1)S(1)}, u32[]{:S(2)}, u32[]{:S(2)}) collective-permute-start(bf16[128,384]{1,0:T(8,128)(2,1)S(1)} %get-tuple-element.69), channel_id=1, source_target_pairs={{0,4},{4,0},{8,24},{12,28},{16,20},{20,16},{24,8},{28,12},{1,5},{5... | collective-permute-start | bytes 294920 | tf_op jit(solution)/shard_map/ppermute | solution.py:160
  25.4 6.3 %collective-permute-start.9 = (bf16[128,384]{1,0:T(8,128)(2,1)S(1)}, bf16[128,384]{1,0:T(8,128)(2,1)S(1)}, u32[]{:S(2)}, u32[]{:S(2)}) collective-permute-start(bf16[128,384]{1,0:T(8,128)(2,1)S(1)} %get-tuple-element.70), channel_id=1, source_target_pairs={{0,24},{4,8},{8,4},{12,20},{16,28},{20,12},{24,0},{28,16},{1,25},{... | collective-permute-start | bytes 294920 | tf_op jit(solution)/shard_map/ppermute | solution.py:160
  26.2 5.6 %collective-permute-start.10 = (bf16[128,384]{1,0:T(8,128)(2,1)S(1)}, bf16[128,384]{1,0:T(8,128)(2,1)S(1)}, u32[]{:S(2)}, u32[]{:S(2)}) collective-permute-start(bf16[128,384]{1,0:T(8,128)(2,1)S(1)} %get-tuple-element.71), channel_id=1, source_target_pairs={{0,12},{4,28},{8,16},{12,0},{16,8},{20,24},{24,20},{28,4},{1,13},{... | collective-permute-start | bytes 294920 | tf_op jit(solution)/shard_map/ppermute | solution.py:160
  28.2 3.6 %collective-permute-start.11 = (bf16[128,384]{1,0:T(8,128)(2,1)S(1)}, bf16[128,384]{1,0:T(8,128)(2,1)S(1)}, u32[]{:S(2)}, u32[]{:S(2)}) collective-permute-start(bf16[128,384]{1,0:T(8,128)(2,1)S(1)} %get-tuple-element.72), channel_id=1, source_target_pairs={{0,8},{4,12},{8,0},{12,4},{16,24},{20,28},{24,16},{28,20},{1,9},{5... | collective-permute-start | bytes 294920 | tf_op jit(solution)/shard_map/ppermute | solution.py:160

commit v7 on v6

--- a/solution.py
+++ b/solution.py
@@ -144,13 +144,14 @@
 SIDE_CORE = hop(6, 3, even_places)
 OTHER_SIDE_CORE = hop(3, 6, even_places)
 
-INWARD = (FAR_CORE, SIDE, CORE, OTHER_SIDE, SIDE_CORE, FAR, OTHER_SIDE_CORE)
+INWARD = (FAR, SIDE_CORE, CORE, SIDE, OTHER_SIDE, OTHER_SIDE_CORE, FAR_CORE)
 OUTWARD = (FAR, FAR_CORE, SIDE, OTHER_SIDE, SIDE_CORE, OTHER_SIDE_CORE, CORE)
 FIRST = 2
 EARLY = 2
-LATE = 5
+LATE_HOP = FAR_CORE
+LATE = 7
 BEYOND = (4, 5, 6, 7)
-DONE = 0
+DONE = 1
 AFTER = {}
 EXPONENT = math.log2(math.e) / math.sqrt(HEAD_DIM)
 
@@ -239,9 +240,17 @@
     return low.reshape(-1, 128, HEAD_DIM)
 
 
-def early_kernel(distances, mask_ref, *refs):
-    slabs, outs = refs[:-7], refs[-7:]
-    stack_ref, exps_ref, dprobs_ref, stats_ref, seen_ref, done_ref, query_ref = outs
+def seen_kernel(mask_ref, seen_ref):
+    here = flat_index(GROUP)
+    for c in range(seen_ref.shape[0]):
+        for n, key in enumerate(key_places(c)):
+            flags = seen_by(mask_ref, here, key, (2 * c, 2 * c + 1))
+            seen_ref[c, n : n + 1] = flags.astype(jnp.float32)
+
+
+def early_kernel(distances, seen_ref, *refs):
+    slabs, outs = refs[:-6], refs[-6:]
+    stack_ref, exps_ref, dprobs_ref, stats_ref, done_ref, query_ref = outs
     here = flat_index(GROUP)
     for distance, slab in zip(distances, slabs):
         stack_ref[distance(here)] = slab[...]
@@ -258,7 +267,8 @@
         keys = [place for place in key_places(c) if place != LATE]
         scores = [b for n in near_cells(c) for b in blocks_of(times_t(take(present[n], 1), q))]
         dprobs = [b for n in near_cells(c) for b in blocks_of(times_t(take(present[n], 2), g))]
-        seen = [seen_by(mask_ref, here, key, present[c]) for key in keys]
+        rows = [key_places(c).index(key) for key in keys]
+        seen = [seen_ref[c, n : n + 1, :width] > 0 for n in rows]
         top = top_of(scores, seen)
         exps = weights(scores, seen, top)
         total = sum_of(exps)
@@ -281,9 +291,6 @@
         stats_ref[c, 0:1, :width] = top
         stats_ref[c, 1:2, :width] = total
         stats_ref[c, 2:3, :width] = product
-        for n, key in enumerate(key_places(c)):
-            flags = seen_by(mask_ref, here, key, (2 * c, 2 * c + 1))
-            seen_ref[c, n : n + 1] = flags.astype(jnp.float32)
 
 
 def taker(slab, stack_ref):
@@ -309,7 +316,7 @@
 
 
 def late_kernel(slab, *refs):
-    stack_ref, exps_ref, dprobs_ref, stats_ref, seen_ref, done_ref = refs[:6]
+    seen_ref, stack_ref, exps_ref, dprobs_ref, stats_ref, done_ref = refs[:6]
     outs = dict(zip(BEYOND, refs[6:10]))
     probs_out, dscores_out, query_out = refs[10:]
     cells = stack_ref.shape[0] // 2
@@ -387,17 +394,15 @@
     def joined(blocks, c):
         return jnp.concatenate([blocks[n] for n in near_cells(c)], axis=1)
 
-    rows_of(2)
-    rows_of(1)
-    rows_of(3)
-    rows_of(0)
+    for c in (LATE // 2, 1 - DONE, LATE // 2 ^ 1, DONE):
+        rows_of(c)
     for c in (2, 3):
         places = (2 * c, 2 * c + 1)
         put_pair_grads(take, c, joined(probs_low[c], c), joined(dscores[c], c), [outs[p] for p in places])
-    for c in (2, 3, 1):
+    for c in (2, 3, 1 - DONE):
         terms = jnp.concatenate([dscores[n][c] for n in near_cells(c)], axis=0)
         dq = query_grad(take(key_places(c), 1), terms)
-        if c == 1:
+        if c == 1 - DONE:
             query_out[...] = dq
         else:
             for a in range(2):
@@ -480,7 +485,15 @@
         if n in AFTER:
             got[n], got[AFTER[n]] = lax.optimization_barrier((got[n], got[AFTER[n]]))
         got[n] = exchange(got[n], distance)
-    soon = [n for n, distance in enumerate(INWARD) if distance is not FAR]
+    soon = [n for n, distance in enumerate(INWARD) if distance is not LATE_HOP]
+    seen = pl.pallas_call(
+        seen_kernel,
+        out_shape=jax.ShapeDtypeStruct((cells, 8, 2 * tokens), jnp.float32),
+        in_specs=[SMEM],
+        out_specs=VMEM,
+        compiler_params=pltpu.CompilerParams(vmem_limit_bytes=MIB),
+        name="seen",
+    )(block_mask)
     pairs = jax.ShapeDtypeStruct((cells, 6 * tokens, 2 * tokens), jnp.float32)
     partial = pl.pallas_call(
         functools.partial(early_kernel, [INWARD[n] for n in soon] + [STAY]),
@@ -489,19 +502,18 @@
             pairs,
             pairs,
             jax.ShapeDtypeStruct((cells, 8, 2 * tokens), jnp.float32),
-            jax.ShapeDtypeStruct((cells, 8, 2 * tokens), jnp.float32),
             jax.ShapeDtypeStruct((2, 6 * tokens, 2 * tokens), jnp.bfloat16),
             jax.ShapeDtypeStruct((2, tokens, HEAD_DIM), jnp.bfloat16),
         ],
-        in_specs=[SMEM] + [VMEM] * (devices - 1),
-        out_specs=[VMEM] * 7,
+        in_specs=[VMEM] * devices,
+        out_specs=[VMEM] * 6,
         compiler_params=pltpu.CompilerParams(vmem_limit_bytes=24 * MIB),
         name="early",
-    )(block_mask, *[got[n] for n in soon], own)
-    stack, *partial, query_grad_0 = partial
-    slab = got[INWARD.index(FAR)]
+    )(seen, *[got[n] for n in soon], own)
+    stack, *partial, query_grad_done = partial
+    slab = got[INWARD.index(LATE_HOP)]
     low = jax.ShapeDtypeStruct((2, 2 * tokens, 6 * tokens), jnp.bfloat16)
-    *beyond, probs_low, dscores, query_grad_1 = pl.pallas_call(
+    *beyond, probs_low, dscores, query_grad_other = pl.pallas_call(
         late_kernel,
         out_shape=[slab_shape(tokens, 3)] * len(BEYOND)
         + [low, low, jax.ShapeDtypeStruct((2, tokens, HEAD_DIM), jnp.bfloat16)],
@@ -509,8 +521,10 @@
         out_specs=[VMEM] * (len(BEYOND) + 3),
         compiler_params=pltpu.CompilerParams(vmem_limit_bytes=24 * MIB),
         name="late",
-    )(slab, stack, *partial)
+    )(slab, seen, stack, *partial)
     beyond = dict(zip(BEYOND, beyond))
+    query_grads = (query_grad_done, query_grad_other)
+    query_grads = query_grads[::-1] if DONE == 1 else query_grads
     distances = OUTWARD + (STAY,)
     rest = pl.pallas_call(
         functools.partial(rest_kernel, distances[2:]),
@@ -520,7 +534,7 @@
         scratch_shapes=[pltpu.VMEM((devices, tokens, 3 * HEAD_DIM), jnp.bfloat16)],
         compiler_params=pltpu.CompilerParams(vmem_limit_bytes=24 * MIB),
         name="rest",
-    )(slab, stack, probs_low, dscores, query_grad_0, query_grad_1, beyond[4], beyond[6])
+    )(slab, stack, probs_low, dscores, *query_grads, beyond[4], beyond[6])
     grads = [beyond[5], beyond[7], *rest]
     back = [exchange(grad, distance) for grad, distance in zip(grads, OUTWARD)] + [grads[-1]]
     whole = jax.ShapeDtypeStruct(queries.shape, queries.dtype)

time: 33 us -> 32.4 us (0.982)
  waiting for transfers between devices: 8.03 us -> 5.48 us
  starting transfers between devices: 15.7 us -> 17.6 us
    ppermute x14, waiting for transfers between devices: 8.03 us -> 5.48 us  [exchange(): return lax.ppermute(block, GROUP, [(i, i ^ distance(i)) for i in places])]
    ppermute x14, starting transfers between devices: 15.7 us -> 17.6 us  [exchange(): return lax.ppermute(block, GROUP, [(i, i ^ distance(i)) for i in places])]
    pallas_call x0 -> x1, Pallas kernels: none -> 0.68 us  [by_heads(): pl.pallas_call(seen_kernel, out_shape=jax.ShapeDtypeStruct((cells, 8, 2 *...]
    pallas_call x1, Pallas kernels: 2.21 us -> 1.56 us  [by_heads(): pl.pallas_call(functools.partial(early_kernel, [INWARD[n] for n in soon]...]
  transfers between devices with their start and end apart: 14 -> 14, of which waited for: 9 -> 9; matrix products, arithmetic and copies ran while one was open for 0% -> 0% of each run, Pallas kernels for 15% -> 16%
where the time goes in v7:
time: 32.4 us; the launch traced here: 32.1 us
  starting transfers between devices  17.6 us (54%)
  Pallas kernels  8.32 us (26%)
  waiting for transfers between devices  5.48 us (17%)
  between operations  0.7 us (2%)
    ppermute x14, starting transfers between devices, exchange(): return lax.ppermute(block, GROUP, [(i, i ^ distance(i)) for i in places])  17.6 us
    ppermute x14, waiting for transfers between devices, exchange(): return lax.ppermute(block, GROUP, [(i, i ^ distance(i)) for i in places])  5.48 us
    pallas_call x2, Pallas kernels, pack(): pl.pallas_call(functools.partial(pack_kernel, distances), out_shape=outs,...  2.3 us
    pallas_call x2, Pallas kernels, unpack(): pl.pallas_call(functools.partial(unpack_kernel, distances), out_shape=[wh...  1.67 us
    pallas_call x1, Pallas kernels, by_heads(): pl.pallas_call(functools.partial(early_kernel, [INWARD[n] for n in soon]...  1.56 us
    pallas_call x1, Pallas kernels, by_heads(): pl.pallas_call(late_kernel, out_shape=[slab_shape(tokens, 3)] * len(BEYON...  1.45 us
    pallas_call x1, Pallas kernels, by_heads(): pl.pallas_call(seen_kernel, out_shape=jax.ShapeDtypeStruct((cells, 8, 2 *...  0.68 us
    pallas_call x1, Pallas kernels, by_heads(): pl.pallas_call(functools.partial(rest_kernel, distances[2:]), out_shape=[...  0.65 us
  transfers between devices with their start and end apart: 14, of which 9 were waited for; matrix products, arithmetic and copies ran while one was open for 0% of the time, Pallas kernels for 16%

profile of v7, /device:TPU:0, one launch (start us, length us, event | category | flops | bytes accessed | tf_op | source)
XLA Modules:
  0.0 32.1 jit_solution(7773973677333007556)
XLA Ops:
  0.6 1.0 %pack_first.1 = (bf16[128,512]{1,0:T(8,128)(2,1)S(1)}, bf16[128,512]{1,0:T(8,128)(2,1)S(1)}) custom-call(bf16[128,1024]{1,0:T(8,128)(2,1)} %refs_0_.2, bf16[128,1024]{1,0:T(8,128)(2,1)} %refs_1_.2, bf16[128,1024]{1,0:T(8,128)(2,1)} %refs_2_.2, bf16[128,1024]{1,0:T(8,128)(2,1)} %refs_3_.2), custom_call_target="tpu_custom_call" | custom-call | tf_op jit(solution)/shard_map/pack_first/pallas_call | solution.py:447
  1.6 4.0 %collective-permute-start.1 = (bf16[128,512]{1,0:T(8,128)(2,1)S(1)}, bf16[128,512]{1,0:T(8,128)(2,1)S(1)}, u32[]{:S(2)}, u32[]{:S(2)}) collective-permute-start(bf16[128,512]{1,0:T(8,128)(2,1)S(1)} %get-tuple-element.48), channel_id=1, source_target_pairs={{0,20},{4,16},{8,28},{12,24},{16,4},{20,0},{24,12},{28,8},{1,21},{... | collective-permute-start | bytes 393224 | tf_op jit(solution)/shard_map/ppermute | solution.py:161
  5.6 1.3 %pack_rest.1 = (bf16[128,512]{1,0:T(8,128)(2,1)S(1)}, bf16[128,512]{1,0:T(8,128)(2,1)S(1)}, bf16[128,512]{1,0:T(8,128)(2,1)S(1)}, bf16[128,512]{1,0:T(8,128)(2,1...) custom-call(bf16[128,1024]{1,0:T(8,128)(2,1)} %refs_0_.2, ...), custom_call_target="tpu_custom_call" | custom-call | tf_op jit(solution)/shard_map/pack_rest/pallas_call | solution.py:447
  6.9 0.7 %collective-permute-start.3 = (bf16[128,512]{1,0:T(8,128)(2,1)S(1)}, bf16[128,512]{1,0:T(8,128)(2,1)S(1)}, u32[]{:S(2)}, u32[]{:S(2)}) collective-permute-start(bf16[128,512]{1,0:T(8,128)(2,1)S(1)} %get-tuple-element.50), channel_id=1, source_target_pairs={{0,8},{4,12},{8,0},{12,4},{16,24},{20,28},{24,16},{28,20},{1,9},{5... | collective-permute-start | bytes 393224 | tf_op jit(solution)/shard_map/ppermute | solution.py:161
  7.6 1.5 %collective-permute-start.4 = (bf16[128,512]{1,0:T(8,128)(2,1)S(1)}, bf16[128,512]{1,0:T(8,128)(2,1)S(1)}, u32[]{:S(2)}, u32[]{:S(2)}) collective-permute-start(bf16[128,512]{1,0:T(8,128)(2,1)S(1)} %get-tuple-element.51), channel_id=1, source_target_pairs={{0,16},{4,20},{8,12},{12,8},{16,0},{20,4},{24,28},{28,24},{1,17},{... | collective-permute-start | bytes 393224 | tf_op jit(solution)/shard_map/ppermute | solution.py:161
  9.1 0.5 %collective-permute-start.5 = (bf16[128,512]{1,0:T(8,128)(2,1)S(1)}, bf16[128,512]{1,0:T(8,128)(2,1)S(1)}, u32[]{:S(2)}, u32[]{:S(2)}) collective-permute-start(bf16[128,512]{1,0:T(8,128)(2,1)S(1)} %get-tuple-element.52), channel_id=1, source_target_pairs={{0,4},{4,0},{8,24},{12,28},{16,20},{20,16},{24,8},{28,12},{1,5},{5... | collective-permute-start | bytes 393224 | tf_op jit(solution)/shard_map/ppermute | solution.py:161
  9.6 0.0 collective-permute-done.1.refs_0_
  9.6 0.6 %collective-permute-start.6 = (bf16[128,512]{1,0:T(8,128)(2,1)S(1)}, bf16[128,512]{1,0:T(8,128)(2,1)S(1)}, u32[]{:S(2)}, u32[]{:S(2)}) collective-permute-start(bf16[128,512]{1,0:T(8,128)(2,1)S(1)} %get-tuple-element.53), channel_id=1, source_target_pairs={{0,12},{4,28},{8,16},{12,0},{16,8},{20,24},{24,20},{28,4},{1,13},{... | collective-permute-start | bytes 393224 | tf_op jit(solution)/shard_map/ppermute | solution.py:161
  10.3 0.4 %collective-permute-done.2.refs_1_ = bf16[128,512]{1,0:T(8,128)(2,1)S(1)} collective-permute-done((bf16[128,512]{1,0:T(8,128)(2,1)S(1)}, bf16[128,512]{1,0:T(8,128)(2,1)S(1)}, u32[]{:S(2)}, u32[]{:S(2)}) %collective-permute-start.2) | collective-permute-done | bytes 131104 | tf_op jit(solution)/shard_map/ppermute | solution.py:161
  10.7 3.4 %collective-permute-start = (bf16[128,512]{1,0:T(8,128)(2,1)S(1)}, bf16[128,512]{1,0:T(8,128)(2,1)S(1)}, u32[]{:S(2)}, u32[]{:S(2)}) collective-permute-start(bf16[128,512]{1,0:T(8,128)(2,1)S(1)} %get-tuple-element.46), channel_id=1, source_target_pairs={{0,28},{4,24},{8,20},{12,16},{16,12},{20,8},{24,4},{28,0},{1,29},{... | collective-permute-start | bytes 393224 | tf_op jit(solution)/shard_map/ppermute | solution.py:161
  14.1 0.7 %seen.1.seen_ref.refs_0_ = f32[4,8,256]{2,1,0:T(8,128)S(1)} custom-call(s32[8,8]{1,0:T(8,128)S(1)} %get-tuple-element.47.mask_ref), custom_call_target="tpu_custom_call" | custom-call | tf_op jit(solution)/shard_map/seen/pallas_call | solution.py:489
  14.8 0.0 collective-permute-done.3.refs_2_
  14.8 0.6 %collective-permute-done.5.refs_4_ = bf16[128,512]{1,0:T(8,128)(2,1)S(1)} collective-permute-done((bf16[128,512]{1,0:T(8,128)(2,1)S(1)}, bf16[128,512]{1,0:T(8,128)(2,1)S(1)}, u32[]{:S(2)}, u32[]{:S(2)}) %collective-permute-start.5) | collective-permute-done | bytes 131104 | tf_op jit(solution)/shard_map/ppermute | solution.py:161
  15.4 1.6 %early.1 = (bf16[8,128,512]{2,1,0:T(8,128)(2,1)S(1)}, f32[4,768,256]{2,1,0:T(8,128)S(1)}, f32[4,768,256]{2,1,0:T(8,128)S(1)}, f32[4,8,256]{2,1,0:T(8,128)S(1)}, ...) custom-call(f32[4,8,256]{2,1,0:T(8,128)S(1)} %seen.1.seen_ref.refs_0_, ...), custom_call_target="tpu_custom_call" | custom-call | tf_op jit(solution)/shard_map/early/pallas_call | solution.py:498
  17.0 0.5 %collective-permute-done.slab = bf16[128,512]{1,0:T(8,128)(2,1)S(1)} collective-permute-done((bf16[128,512]{1,0:T(8,128)(2,1)S(1)}, bf16[128,512]{1,0:T(8,128)(2,1)S(1)}, u32[]{:S(2)}, u32[]{:S(2)}) %collective-permute-start) | collective-permute-done | bytes 131104 | tf_op jit(solution)/shard_map/ppermute | solution.py:161
  17.6 1.4 %late.1 = (bf16[128,384]{1,0:T(8,128)(2,1)S(1)}, bf16[128,384]{1,0:T(8,128)(2,1)S(1)}, bf16[128,384]{1,0:T(8,128)(2,1)S(1)}, bf16[128,384]{1,0:T(8,128)(2,1)S(1)...) custom-call(bf16[128,512]{1,0:T(8,128)(2,1)S(1)} %collective-permute-done.sla, ...), custom_call_target="tpu_custom_call" | custom-call | tf_op jit(solution)/shard_map/late/pallas_call | solution.py:516
  19.0 1.4 %collective-permute-start.12 = (bf16[128,384]{1,0:T(8,128)(2,1)S(1)}, bf16[128,384]{1,0:T(8,128)(2,1)S(1)}, u32[]{:S(2)}, u32[]{:S(2)}) collective-permute-start(bf16[128,384]{1,0:T(8,128)(2,1)S(1)} %get-tuple-element.72), channel_id=1, source_target_pairs={{0,20},{4,16},{8,28},{12,24},{16,4},{20,0},{24,12},{28,8},{1,21},{... | collective-permute-start | bytes 294920 | tf_op jit(solution)/shard_map/ppermute | solution.py:161
  20.4 1.4 %collective-permute-start.13 = (bf16[128,384]{1,0:T(8,128)(2,1)S(1)}, bf16[128,384]{1,0:T(8,128)(2,1)S(1)}, u32[]{:S(2)}, u32[]{:S(2)}) collective-permute-start(bf16[128,384]{1,0:T(8,128)(2,1)S(1)} %get-tuple-element.73), channel_id=1, source_target_pairs={{0,28},{4,24},{8,20},{12,16},{16,12},{20,8},{24,4},{28,0},{1,29},{... | collective-permute-start | bytes 294920 | tf_op jit(solution)/shard_map/ppermute | solution.py:161
  21.8 0.7 %rest.1 = (bf16[128,384]{1,0:T(8,128)(2,1)S(1)}, bf16[128,384]{1,0:T(8,128)(2,1)S(1)}, bf16[128,384]{1,0:T(8,128)(2,1)S(1)}, bf16[128,384]{1,0:T(8,128)(2,1)S(1)...) custom-call(bf16[128,512]{1,0:T(8,128)(2,1)S(1)} %collective-permute-done.slab, ...), custom_call_target="tpu_custom_call" | custom-call | tf_op jit(solution)/shard_map/rest/pallas_call | solution.py:529
  22.5 1.5 %collective-permute-start.7 = (bf16[128,384]{1,0:T(8,128)(2,1)S(1)}, bf16[128,384]{1,0:T(8,128)(2,1)S(1)}, u32[]{:S(2)}, u32[]{:S(2)}) collective-permute-start(bf16[128,384]{1,0:T(8,128)(2,1)S(1)} %get-tuple-element.66), channel_id=1, source_target_pairs={{0,16},{4,20},{8,12},{12,8},{16,0},{20,4},{24,28},{28,24},{1,17},{... | collective-permute-start | bytes 294920 | tf_op jit(solution)/shard_map/ppermute | solution.py:161
  24.0 1.1 %collective-permute-start.8 = (bf16[128,384]{1,0:T(8,128)(2,1)S(1)}, bf16[128,384]{1,0:T(8,128)(2,1)S(1)}, u32[]{:S(2)}, u32[]{:S(2)}) collective-permute-start(bf16[128,384]{1,0:T(8,128)(2,1)S(1)} %get-tuple-element.67), channel_id=1, source_target_pairs={{0,4},{4,0},{8,24},{12,28},{16,20},{20,16},{24,8},{28,12},{1,5},{5... | collective-permute-start | bytes 294920 | tf_op jit(solution)/shard_map/ppermute | solution.py:161
  25.0 0.2 collective-permute-start.9
  25.3 0.3 collective-permute-done.12.refs_1_
  25.6 0.8 %collective-permute-start.10 = (bf16[128,384]{1,0:T(8,128)(2,1)S(1)}, bf16[128,384]{1,0:T(8,128)(2,1)S(1)}, u32[]{:S(2)}, u32[]{:S(2)}) collective-permute-start(bf16[128,384]{1,0:T(8,128)(2,1)S(1)} %get-tuple-element.69), channel_id=1, source_target_pairs={{0,12},{4,28},{8,16},{12,0},{16,8},{20,24},{24,20},{28,4},{1,13},{... | collective-permute-start | bytes 294920 | tf_op jit(solution)/shard_map/ppermute | solution.py:161
  26.3 0.7 %collective-permute-done.13.refs_2_ = bf16[128,384]{1,0:T(8,128)(2,1)S(1)} collective-permute-done((bf16[128,384]{1,0:T(8,128)(2,1)S(1)}, bf16[128,384]{1,0:T(8,128)(2,1)S(1)}, u32[]{:S(2)}, u32[]{:S(2)}) %collective-permute-start.13) | collective-permute-done | bytes 98336 | tf_op jit(solution)/shard_map/ppermute | solution.py:161
  27.0 0.5 %collective-permute-start.11 = (bf16[128,384]{1,0:T(8,128)(2,1)S(1)}, bf16[128,384]{1,0:T(8,128)(2,1)S(1)}, u32[]{:S(2)}, u32[]{:S(2)}) collective-permute-start(bf16[128,384]{1,0:T(8,128)(2,1)S(1)} %get-tuple-element.70), channel_id=1, source_target_pairs={{0,8},{4,12},{8,0},{12,4},{16,24},{20,28},{24,16},{28,20},{1,9},{5... | collective-permute-start | bytes 294920 | tf_op jit(solution)/shard_map/ppermute | solution.py:161
  27.5 0.8 %unpack.1 = (bf16[128,1024]{1,0:T(8,128)(2,1)}, bf16[128,1024]{1,0:T(8,128)(2,1)}, bf16[128,1024]{1,0:T(8,128)(2,1)}) custom-call(bf16[128,384]{1,0:T(8,128)(2,1)S(1)} %get-tuple-element.71.refs_0_, bf16[128,384]{1,0:T(8,128)(2,1)S(1)} %collective-permute-done.12.refs_1_, bf16[128,384]{1,0:T(8,128)(2,1)S(1)} %collective-permute-done.13.refs_2_), custom_call_target="tpu_custom_call" | custom-call | tf_op jit(solution)/shard_map/unpack/pallas_call | solution.py:460
  28.3 1.1 %collective-permute-done.7.refs_0_ = bf16[128,384]{1,0:T(8,128)(2,1)S(1)} collective-permute-done((bf16[128,384]{1,0:T(8,128)(2,1)S(1)}, bf16[128,384]{1,0:T(8,128)(2,1)S(1)}, u32[]{:S(2)}, u32[]{:S(2)}) %collective-permute-start.7) | collective-permute-done | bytes 98336 | tf_op jit(solution)/shard_map/ppermute | solution.py:161
  29.4 0.3 collective-permute-done.8.refs_1_
  29.7 1.3 %collective-permute-done.9.refs_2_ = bf16[128,384]{1,0:T(8,128)(2,1)S(1)} collective-permute-done((bf16[128,384]{1,0:T(8,128)(2,1)S(1)}, bf16[128,384]{1,0:T(8,128)(2,1)S(1)}, u32[]{:S(2)}, u32[]{:S(2)}) %collective-permute-start.9) | collective-permute-done | bytes 98336 | tf_op jit(solution)/shard_map/ppermute | solution.py:161
  31.0 0.2 collective-permute-done.10.refs_3_
  31.2 0.9 %unpack_last.1 = (bf16[128,1024]{1,0:T(8,128)(2,1)}, bf16[128,1024]{1,0:T(8,128)(2,1)}, bf16[128,1024]{1,0:T(8,128)(2,1)}) custom-call(bf16[128,384]{1,0:T(8,128)(2,1)S(1)} %collective-permute-done.7.refs_0_, bf16[128,384]{1,0:T(8,128)(2,1)S(1)} %collective-permute-done.8.refs_1_, ...), custom_call_target="tpu_custom_call", output_to_operand_aliasing={{0}: (5, {}), {1}: (6, {}), {2}: (7, {})} | custom-call | tf_op jit(solution)/shard_map/unpack_last/pallas_call | solution.py:460
  (4 shorter events, 0.0 us)
Async XLA Ops:
  1.6 8.0 %collective-permute-start.1 = (bf16[128,512]{1,0:T(8,128)(2,1)S(1)}, bf16[128,512]{1,0:T(8,128)(2,1)S(1)}, u32[]{:S(2)}, u32[]{:S(2)}) collective-permute-start(bf16[128,512]{1,0:T(8,128)(2,1)S(1)} %get-tuple-element.48), channel_id=1, source_target_pairs={{0,20},{4,16},{8,28},{12,24},{16,4},{20,0},{24,12},{28,8},{1,21},{... | collective-permute-start | bytes 393224 | tf_op jit(solution)/shard_map/ppermute | solution.py:161
  5.6 5.2 %collective-permute-start.2 = (bf16[128,512]{1,0:T(8,128)(2,1)S(1)}, bf16[128,512]{1,0:T(8,128)(2,1)S(1)}, u32[]{:S(2)}, u32[]{:S(2)}) collective-permute-start(bf16[128,512]{1,0:T(8,128)(2,1)S(1)} %get-tuple-element.49), channel_id=1, source_target_pairs={{0,24},{4,8},{8,4},{12,20},{16,28},{20,12},{24,0},{28,16},{1,25},{... | collective-permute-start | bytes 393224 | tf_op jit(solution)/shard_map/ppermute | solution.py:161
  6.9 7.9 %collective-permute-start.3 = (bf16[128,512]{1,0:T(8,128)(2,1)S(1)}, bf16[128,512]{1,0:T(8,128)(2,1)S(1)}, u32[]{:S(2)}, u32[]{:S(2)}) collective-permute-start(bf16[128,512]{1,0:T(8,128)(2,1)S(1)} %get-tuple-element.50), channel_id=1, source_target_pairs={{0,8},{4,12},{8,0},{12,4},{16,24},{20,28},{24,16},{28,20},{1,9},{5... | collective-permute-start | bytes 393224 | tf_op jit(solution)/shard_map/ppermute | solution.py:161
  7.6 7.2 %collective-permute-start.4 = (bf16[128,512]{1,0:T(8,128)(2,1)S(1)}, bf16[128,512]{1,0:T(8,128)(2,1)S(1)}, u32[]{:S(2)}, u32[]{:S(2)}) collective-permute-start(bf16[128,512]{1,0:T(8,128)(2,1)S(1)} %get-tuple-element.51), channel_id=1, source_target_pairs={{0,16},{4,20},{8,12},{12,8},{16,0},{20,4},{24,28},{28,24},{1,17},{... | collective-permute-start | bytes 393224 | tf_op jit(solution)/shard_map/ppermute | solution.py:161
  9.1 6.3 %collective-permute-start.5 = (bf16[128,512]{1,0:T(8,128)(2,1)S(1)}, bf16[128,512]{1,0:T(8,128)(2,1)S(1)}, u32[]{:S(2)}, u32[]{:S(2)}) collective-permute-start(bf16[128,512]{1,0:T(8,128)(2,1)S(1)} %get-tuple-element.52), channel_id=1, source_target_pairs={{0,4},{4,0},{8,24},{12,28},{16,20},{20,16},{24,8},{28,12},{1,5},{5... | collective-permute-start | bytes 393224 | tf_op jit(solution)/shard_map/ppermute | solution.py:161
  9.6 5.8 %collective-permute-start.6 = (bf16[128,512]{1,0:T(8,128)(2,1)S(1)}, bf16[128,512]{1,0:T(8,128)(2,1)S(1)}, u32[]{:S(2)}, u32[]{:S(2)}) collective-permute-start(bf16[128,512]{1,0:T(8,128)(2,1)S(1)} %get-tuple-element.53), channel_id=1, source_target_pairs={{0,12},{4,28},{8,16},{12,0},{16,8},{20,24},{24,20},{28,4},{1,13},{... | collective-permute-start | bytes 393224 | tf_op jit(solution)/shard_map/ppermute | solution.py:161
  10.7 6.8 %collective-permute-start = (bf16[128,512]{1,0:T(8,128)(2,1)S(1)}, bf16[128,512]{1,0:T(8,128)(2,1)S(1)}, u32[]{:S(2)}, u32[]{:S(2)}) collective-permute-start(bf16[128,512]{1,0:T(8,128)(2,1)S(1)} %get-tuple-element.46), channel_id=1, source_target_pairs={{0,28},{4,24},{8,20},{12,16},{16,12},{20,8},{24,4},{28,0},{1,29},{... | collective-permute-start | bytes 393224 | tf_op jit(solution)/shard_map/ppermute | solution.py:161
  19.0 6.6 %collective-permute-start.12 = (bf16[128,384]{1,0:T(8,128)(2,1)S(1)}, bf16[128,384]{1,0:T(8,128)(2,1)S(1)}, u32[]{:S(2)}, u32[]{:S(2)}) collective-permute-start(bf16[128,384]{1,0:T(8,128)(2,1)S(1)} %get-tuple-element.72), channel_id=1, source_target_pairs={{0,20},{4,16},{8,28},{12,24},{16,4},{20,0},{24,12},{28,8},{1,21},{... | collective-permute-start | bytes 294920 | tf_op jit(solution)/shard_map/ppermute | solution.py:161
  20.4 6.6 %collective-permute-start.13 = (bf16[128,384]{1,0:T(8,128)(2,1)S(1)}, bf16[128,384]{1,0:T(8,128)(2,1)S(1)}, u32[]{:S(2)}, u32[]{:S(2)}) collective-permute-start(bf16[128,384]{1,0:T(8,128)(2,1)S(1)} %get-tuple-element.73), channel_id=1, source_target_pairs={{0,28},{4,24},{8,20},{12,16},{16,12},{20,8},{24,4},{28,0},{1,29},{... | collective-permute-start | bytes 294920 | tf_op jit(solution)/shard_map/ppermute | solution.py:161
  22.5 6.9 %collective-permute-start.7 = (bf16[128,384]{1,0:T(8,128)(2,1)S(1)}, bf16[128,384]{1,0:T(8,128)(2,1)S(1)}, u32[]{:S(2)}, u32[]{:S(2)}) collective-permute-start(bf16[128,384]{1,0:T(8,128)(2,1)S(1)} %get-tuple-element.66), channel_id=1, source_target_pairs={{0,16},{4,20},{8,12},{12,8},{16,0},{20,4},{24,28},{28,24},{1,17},{... | collective-permute-start | bytes 294920 | tf_op jit(solution)/shard_map/ppermute | solution.py:161
  24.0 5.7 %collective-permute-start.8 = (bf16[128,384]{1,0:T(8,128)(2,1)S(1)}, bf16[128,384]{1,0:T(8,128)(2,1)S(1)}, u32[]{:S(2)}, u32[]{:S(2)}) collective-permute-start(bf16[128,384]{1,0:T(8,128)(2,1)S(1)} %get-tuple-element.67), channel_id=1, source_target_pairs={{0,4},{4,0},{8,24},{12,28},{16,20},{20,16},{24,8},{28,12},{1,5},{5... | collective-permute-start | bytes 294920 | tf_op jit(solution)/shard_map/ppermute | solution.py:161
  25.0 6.0 %collective-permute-start.9 = (bf16[128,384]{1,0:T(8,128)(2,1)S(1)}, bf16[128,384]{1,0:T(8,128)(2,1)S(1)}, u32[]{:S(2)}, u32[]{:S(2)}) collective-permute-start(bf16[128,384]{1,0:T(8,128)(2,1)S(1)} %get-tuple-element.68), channel_id=1, source_target_pairs={{0,24},{4,8},{8,4},{12,20},{16,28},{20,12},{24,0},{28,16},{1,25},{... | collective-permute-start | bytes 294920 | tf_op jit(solution)/shard_map/ppermute | solution.py:161
  25.6 5.6 %collective-permute-start.10 = (bf16[128,384]{1,0:T(8,128)(2,1)S(1)}, bf16[128,384]{1,0:T(8,128)(2,1)S(1)}, u32[]{:S(2)}, u32[]{:S(2)}) collective-permute-start(bf16[128,384]{1,0:T(8,128)(2,1)S(1)} %get-tuple-element.69), channel_id=1, source_target_pairs={{0,12},{4,28},{8,16},{12,0},{16,8},{20,24},{24,20},{28,4},{1,13},{... | collective-permute-start | bytes 294920 | tf_op jit(solution)/shard_map/ppermute | solution.py:161
  27.0 4.2 %collective-permute-start.11 = (bf16[128,384]{1,0:T(8,128)(2,1)S(1)}, bf16[128,384]{1,0:T(8,128)(2,1)S(1)}, u32[]{:S(2)}, u32[]{:S(2)}) collective-permute-start(bf16[128,384]{1,0:T(8,128)(2,1)S(1)} %get-tuple-element.70), channel_id=1, source_target_pairs={{0,8},{4,12},{8,0},{12,4},{16,24},{20,28},{24,16},{28,20},{1,9},{5... | collective-permute-start | bytes 294920 | tf_op jit(solution)/shard_map/ppermute | solution.py:161

commit v8 on v7

--- a/solution.py
+++ b/solution.py
@@ -147,7 +147,7 @@
 INWARD = (FAR, SIDE_CORE, CORE, SIDE, OTHER_SIDE, OTHER_SIDE_CORE, FAR_CORE)
 OUTWARD = (FAR, FAR_CORE, SIDE, OTHER_SIDE, SIDE_CORE, OTHER_SIDE_CORE, CORE)
 FIRST = 2
-EARLY = 2
+UNPACKED = ((-1, 0, 1), (2, 3), (4, 5, 6))
 LATE_HOP = FAR_CORE
 LATE = 7
 BEYOND = (4, 5, 6, 7)
@@ -538,8 +538,11 @@
     grads = [beyond[5], beyond[7], *rest]
     back = [exchange(grad, distance) for grad, distance in zip(grads, OUTWARD)] + [grads[-1]]
     whole = jax.ShapeDtypeStruct(queries.shape, queries.dtype)
-    grads = unpack(whole, distances[-1:] + distances[:EARLY], back[-1:] + back[:EARLY], "unpack")
-    return unpack(whole, distances[EARLY:-1], back[EARLY:-1], "unpack_last", *grads)
+    grads = []
+    for number, group in enumerate(UNPACKED):
+        hops = [distances[n] for n in group]
+        grads = unpack(whole, hops, [back[n] for n in group], f"unpack_{number}", *grads)
+    return grads
 
 
 def local(queries, keys, values, out_grad, block_mask):

time: 32.4 us -> 32.3 us (level)
  waiting for transfers between devices: 5.48 us -> 4.76 us
  Pallas kernels: 8.32 us -> 8.92 us
    ppermute x14, waiting for transfers between devices: 5.48 us -> 4.76 us  [exchange(): return lax.ppermute(block, GROUP, [(i, i ^ distance(i)) for i in places])]
    pallas_call x2 -> x3, Pallas kernels: 1.67 us -> 2.28 us  [unpack(): pl.pallas_call(functools.partial(unpack_kernel, distances), out_shape=[wh...]
  transfers between devices with their start and end apart: 14 -> 14, of which waited for: 9 -> 9; matrix products, arithmetic and copies ran while one was open for 0% -> 0% of each run, Pallas kernels for 16% -> 18%
where the time goes in v8:
time: 32.3 us; the launch traced here: 32 us
  starting transfers between devices  17.6 us (54%)
  Pallas kernels  8.92 us (28%)
  waiting for transfers between devices  4.76 us (15%)
  between operations  0.71 us (2%)
    ppermute x14, starting transfers between devices, exchange(): return lax.ppermute(block, GROUP, [(i, i ^ distance(i)) for i in places])  17.6 us
    ppermute x14, waiting for transfers between devices, exchange(): return lax.ppermute(block, GROUP, [(i, i ^ distance(i)) for i in places])  4.76 us
    pallas_call x2, Pallas kernels, pack(): pl.pallas_call(functools.partial(pack_kernel, distances), out_shape=outs,...  2.3 us
    pallas_call x3, Pallas kernels, unpack(): pl.pallas_call(functools.partial(unpack_kernel, distances), out_shape=[wh...  2.28 us
    pallas_call x1, Pallas kernels, by_heads(): pl.pallas_call(functools.partial(early_kernel, [INWARD[n] for n in soon]...  1.56 us
    pallas_call x1, Pallas kernels, by_heads(): pl.pallas_call(late_kernel, out_shape=[slab_shape(tokens, 3)] * len(BEYON...  1.45 us
    pallas_call x1, Pallas kernels, by_heads(): pl.pallas_call(seen_kernel, out_shape=jax.ShapeDtypeStruct((cells, 8, 2 *...  0.68 us
    pallas_call x1, Pallas kernels, by_heads(): pl.pallas_call(functools.partial(rest_kernel, distances[2:]), out_shape=[...  0.65 us
  transfers between devices with their start and end apart: 14, of which 9 were waited for; matrix products, arithmetic and copies ran while one was open for 0% of the time, Pallas kernels for 18%

profile of v8, /device:TPU:0, one launch (start us, length us, event | category | flops | bytes accessed | tf_op | source)
XLA Modules:
  0.0 32.0 jit_solution(16255910075457796254)
XLA Ops:
  0.6 1.0 %pack_first.1 = (bf16[128,512]{1,0:T(8,128)(2,1)S(1)}, bf16[128,512]{1,0:T(8,128)(2,1)S(1)}) custom-call(bf16[128,1024]{1,0:T(8,128)(2,1)} %refs_0_.2, bf16[128,1024]{1,0:T(8,128)(2,1)} %refs_1_.2, bf16[128,1024]{1,0:T(8,128)(2,1)} %refs_2_.2, bf16[128,1024]{1,0:T(8,128)(2,1)} %refs_3_.2), custom_call_target="tpu_custom_call" | custom-call | tf_op jit(solution)/shard_map/pack_first/pallas_call | solution.py:447
  1.6 4.0 %collective-permute-start.1 = (bf16[128,512]{1,0:T(8,128)(2,1)S(1)}, bf16[128,512]{1,0:T(8,128)(2,1)S(1)}, u32[]{:S(2)}, u32[]{:S(2)}) collective-permute-start(bf16[128,512]{1,0:T(8,128)(2,1)S(1)} %get-tuple-element.51), channel_id=1, source_target_pairs={{0,20},{4,16},{8,28},{12,24},{16,4},{20,0},{24,12},{28,8},{1,21},{... | collective-permute-start | bytes 393224 | tf_op jit(solution)/shard_map/ppermute | solution.py:161
  5.6 1.3 %pack_rest.1 = (bf16[128,512]{1,0:T(8,128)(2,1)S(1)}, bf16[128,512]{1,0:T(8,128)(2,1)S(1)}, bf16[128,512]{1,0:T(8,128)(2,1)S(1)}, bf16[128,512]{1,0:T(8,128)(2,1...) custom-call(bf16[128,1024]{1,0:T(8,128)(2,1)} %refs_0_.2, ...), custom_call_target="tpu_custom_call" | custom-call | tf_op jit(solution)/shard_map/pack_rest/pallas_call | solution.py:447
  6.9 0.7 %collective-permute-start.3 = (bf16[128,512]{1,0:T(8,128)(2,1)S(1)}, bf16[128,512]{1,0:T(8,128)(2,1)S(1)}, u32[]{:S(2)}, u32[]{:S(2)}) collective-permute-start(bf16[128,512]{1,0:T(8,128)(2,1)S(1)} %get-tuple-element.53), channel_id=1, source_target_pairs={{0,8},{4,12},{8,0},{12,4},{16,24},{20,28},{24,16},{28,20},{1,9},{5... | collective-permute-start | bytes 393224 | tf_op jit(solution)/shard_map/ppermute | solution.py:161
  7.6 1.5 %collective-permute-start.4 = (bf16[128,512]{1,0:T(8,128)(2,1)S(1)}, bf16[128,512]{1,0:T(8,128)(2,1)S(1)}, u32[]{:S(2)}, u32[]{:S(2)}) collective-permute-start(bf16[128,512]{1,0:T(8,128)(2,1)S(1)} %get-tuple-element.54), channel_id=1, source_target_pairs={{0,16},{4,20},{8,12},{12,8},{16,0},{20,4},{24,28},{28,24},{1,17},{... | collective-permute-start | bytes 393224 | tf_op jit(solution)/shard_map/ppermute | solution.py:161
  9.1 0.5 %collective-permute-start.5 = (bf16[128,512]{1,0:T(8,128)(2,1)S(1)}, bf16[128,512]{1,0:T(8,128)(2,1)S(1)}, u32[]{:S(2)}, u32[]{:S(2)}) collective-permute-start(bf16[128,512]{1,0:T(8,128)(2,1)S(1)} %get-tuple-element.55), channel_id=1, source_target_pairs={{0,4},{4,0},{8,24},{12,28},{16,20},{20,16},{24,8},{28,12},{1,5},{5... | collective-permute-start | bytes 393224 | tf_op jit(solution)/shard_map/ppermute | solution.py:161
  9.6 0.0 collective-permute-done.1.refs_0_
  9.6 0.6 %collective-permute-start.6 = (bf16[128,512]{1,0:T(8,128)(2,1)S(1)}, bf16[128,512]{1,0:T(8,128)(2,1)S(1)}, u32[]{:S(2)}, u32[]{:S(2)}) collective-permute-start(bf16[128,512]{1,0:T(8,128)(2,1)S(1)} %get-tuple-element.56), channel_id=1, source_target_pairs={{0,12},{4,28},{8,16},{12,0},{16,8},{20,24},{24,20},{28,4},{1,13},{... | collective-permute-start | bytes 393224 | tf_op jit(solution)/shard_map/ppermute | solution.py:161
  10.3 0.4 %collective-permute-done.2.refs_1_ = bf16[128,512]{1,0:T(8,128)(2,1)S(1)} collective-permute-done((bf16[128,512]{1,0:T(8,128)(2,1)S(1)}, bf16[128,512]{1,0:T(8,128)(2,1)S(1)}, u32[]{:S(2)}, u32[]{:S(2)}) %collective-permute-start.2) | collective-permute-done | bytes 131104 | tf_op jit(solution)/shard_map/ppermute | solution.py:161
  10.7 3.4 %collective-permute-start = (bf16[128,512]{1,0:T(8,128)(2,1)S(1)}, bf16[128,512]{1,0:T(8,128)(2,1)S(1)}, u32[]{:S(2)}, u32[]{:S(2)}) collective-permute-start(bf16[128,512]{1,0:T(8,128)(2,1)S(1)} %get-tuple-element.49), channel_id=1, source_target_pairs={{0,28},{4,24},{8,20},{12,16},{16,12},{20,8},{24,4},{28,0},{1,29},{... | collective-permute-start | bytes 393224 | tf_op jit(solution)/shard_map/ppermute | solution.py:161
  14.1 0.7 %seen.1.seen_ref.refs_0_ = f32[4,8,256]{2,1,0:T(8,128)S(1)} custom-call(s32[8,8]{1,0:T(8,128)S(1)} %get-tuple-element.50.mask_ref), custom_call_target="tpu_custom_call" | custom-call | tf_op jit(solution)/shard_map/seen/pallas_call | solution.py:489
  14.8 0.6 %collective-permute-done.5.refs_4_ = bf16[128,512]{1,0:T(8,128)(2,1)S(1)} collective-permute-done((bf16[128,512]{1,0:T(8,128)(2,1)S(1)}, bf16[128,512]{1,0:T(8,128)(2,1)S(1)}, u32[]{:S(2)}, u32[]{:S(2)}) %collective-permute-start.5) | collective-permute-done | bytes 131104 | tf_op jit(solution)/shard_map/ppermute | solution.py:161
  15.4 1.6 %early.1 = (bf16[8,128,512]{2,1,0:T(8,128)(2,1)S(1)}, f32[4,768,256]{2,1,0:T(8,128)S(1)}, f32[4,768,256]{2,1,0:T(8,128)S(1)}, f32[4,8,256]{2,1,0:T(8,128)S(1)}, ...) custom-call(f32[4,8,256]{2,1,0:T(8,128)S(1)} %seen.1.seen_ref.refs_0_, ...), custom_call_target="tpu_custom_call" | custom-call | tf_op jit(solution)/shard_map/early/pallas_call | solution.py:498
  17.0 0.5 %collective-permute-done.slab = bf16[128,512]{1,0:T(8,128)(2,1)S(1)} collective-permute-done((bf16[128,512]{1,0:T(8,128)(2,1)S(1)}, bf16[128,512]{1,0:T(8,128)(2,1)S(1)}, u32[]{:S(2)}, u32[]{:S(2)}) %collective-permute-start) | collective-permute-done | bytes 131104 | tf_op jit(solution)/shard_map/ppermute | solution.py:161
  17.6 1.4 %late.1 = (bf16[128,384]{1,0:T(8,128)(2,1)S(1)}, bf16[128,384]{1,0:T(8,128)(2,1)S(1)}, bf16[128,384]{1,0:T(8,128)(2,1)S(1)}, bf16[128,384]{1,0:T(8,128)(2,1)S(1)...) custom-call(bf16[128,512]{1,0:T(8,128)(2,1)S(1)} %collective-permute-done.sla, ...), custom_call_target="tpu_custom_call" | custom-call | tf_op jit(solution)/shard_map/late/pallas_call | solution.py:516
  19.0 1.4 %collective-permute-start.12 = (bf16[128,384]{1,0:T(8,128)(2,1)S(1)}, bf16[128,384]{1,0:T(8,128)(2,1)S(1)}, u32[]{:S(2)}, u32[]{:S(2)}) collective-permute-start(bf16[128,384]{1,0:T(8,128)(2,1)S(1)} %get-tuple-element.75), channel_id=1, source_target_pairs={{0,20},{4,16},{8,28},{12,24},{16,4},{20,0},{24,12},{28,8},{1,21},{... | collective-permute-start | bytes 294920 | tf_op jit(solution)/shard_map/ppermute | solution.py:161
  20.4 1.4 %collective-permute-start.13 = (bf16[128,384]{1,0:T(8,128)(2,1)S(1)}, bf16[128,384]{1,0:T(8,128)(2,1)S(1)}, u32[]{:S(2)}, u32[]{:S(2)}) collective-permute-start(bf16[128,384]{1,0:T(8,128)(2,1)S(1)} %get-tuple-element.76), channel_id=1, source_target_pairs={{0,28},{4,24},{8,20},{12,16},{16,12},{20,8},{24,4},{28,0},{1,29},{... | collective-permute-start | bytes 294920 | tf_op jit(solution)/shard_map/ppermute | solution.py:161
  21.8 0.7 %rest.1 = (bf16[128,384]{1,0:T(8,128)(2,1)S(1)}, bf16[128,384]{1,0:T(8,128)(2,1)S(1)}, bf16[128,384]{1,0:T(8,128)(2,1)S(1)}, bf16[128,384]{1,0:T(8,128)(2,1)S(1)...) custom-call(bf16[128,512]{1,0:T(8,128)(2,1)S(1)} %collective-permute-done.slab, ...), custom_call_target="tpu_custom_call" | custom-call | tf_op jit(solution)/shard_map/rest/pallas_call | solution.py:529
  22.5 1.5 %collective-permute-start.10 = (bf16[128,384]{1,0:T(8,128)(2,1)S(1)}, bf16[128,384]{1,0:T(8,128)(2,1)S(1)}, u32[]{:S(2)}, u32[]{:S(2)}) collective-permute-start(bf16[128,384]{1,0:T(8,128)(2,1)S(1)} %get-tuple-element.72), channel_id=1, source_target_pairs={{0,16},{4,20},{8,12},{12,8},{16,0},{20,4},{24,28},{28,24},{1,17},{... | collective-permute-start | bytes 294920 | tf_op jit(solution)/shard_map/ppermute | solution.py:161
  24.0 1.1 %collective-permute-start.11 = (bf16[128,384]{1,0:T(8,128)(2,1)S(1)}, bf16[128,384]{1,0:T(8,128)(2,1)S(1)}, u32[]{:S(2)}, u32[]{:S(2)}) collective-permute-start(bf16[128,384]{1,0:T(8,128)(2,1)S(1)} %get-tuple-element.73), channel_id=1, source_target_pairs={{0,4},{4,0},{8,24},{12,28},{16,20},{20,16},{24,8},{28,12},{1,5},{5... | collective-permute-start | bytes 294920 | tf_op jit(solution)/shard_map/ppermute | solution.py:161
  25.0 0.2 collective-permute-start.7
  25.3 0.3 collective-permute-done.12.refs_1_
  25.6 0.8 %collective-permute-start.8 = (bf16[128,384]{1,0:T(8,128)(2,1)S(1)}, bf16[128,384]{1,0:T(8,128)(2,1)S(1)}, u32[]{:S(2)}, u32[]{:S(2)}) collective-permute-start(bf16[128,384]{1,0:T(8,128)(2,1)S(1)} %get-tuple-element.70), channel_id=1, source_target_pairs={{0,12},{4,28},{8,16},{12,0},{16,8},{20,24},{24,20},{28,4},{1,13},{... | collective-permute-start | bytes 294920 | tf_op jit(solution)/shard_map/ppermute | solution.py:161
  26.3 0.7 %collective-permute-done.13.refs_2_ = bf16[128,384]{1,0:T(8,128)(2,1)S(1)} collective-permute-done((bf16[128,384]{1,0:T(8,128)(2,1)S(1)}, bf16[128,384]{1,0:T(8,128)(2,1)S(1)}, u32[]{:S(2)}, u32[]{:S(2)}) %collective-permute-start.13) | collective-permute-done | bytes 98336 | tf_op jit(solution)/shard_map/ppermute | solution.py:161
  27.0 0.5 %collective-permute-start.9 = (bf16[128,384]{1,0:T(8,128)(2,1)S(1)}, bf16[128,384]{1,0:T(8,128)(2,1)S(1)}, u32[]{:S(2)}, u32[]{:S(2)}) collective-permute-start(bf16[128,384]{1,0:T(8,128)(2,1)S(1)} %get-tuple-element.71), channel_id=1, source_target_pairs={{0,8},{4,12},{8,0},{12,4},{16,24},{20,28},{24,16},{28,20},{1,9},{5... | collective-permute-start | bytes 294920 | tf_op jit(solution)/shard_map/ppermute | solution.py:161
  27.5 0.8 %unpack_0.1 = (bf16[128,1024]{1,0:T(8,128)(2,1)}, bf16[128,1024]{1,0:T(8,128)(2,1)}, bf16[128,1024]{1,0:T(8,128)(2,1)}) custom-call(bf16[128,384]{1,0:T(8,128)(2,1)S(1)} %get-tuple-element.74.refs_0_, bf16[128,384]{1,0:T(8,128)(2,1)S(1)} %collective-permute-done.12.refs_1_, bf16[128,384]{1,0:T(8,128)(2,1)S(1)} %collective-permute-done.13.refs_2_), custom_call_target="tpu_custom_call" | custom-call | tf_op jit(solution)/shard_map/unpack_0/pallas_call | solution.py:460
  28.3 1.1 %collective-permute-done.10.refs_0_ = bf16[128,384]{1,0:T(8,128)(2,1)S(1)} collective-permute-done((bf16[128,384]{1,0:T(8,128)(2,1)S(1)}, bf16[128,384]{1,0:T(8,128)(2,1)S(1)}, u32[]{:S(2)}, u32[]{:S(2)}) %collective-permute-start.10) | collective-permute-done | bytes 98336 | tf_op jit(solution)/shard_map/ppermute | solution.py:161
  29.4 0.3 collective-permute-done.11.refs_1_
  29.7 0.7 %unpack_1.1 = (bf16[128,1024]{1,0:T(8,128)(2,1)}, bf16[128,1024]{1,0:T(8,128)(2,1)}, bf16[128,1024]{1,0:T(8,128)(2,1)}) custom-call(bf16[128,384]{1,0:T(8,128)(2,1)S(1)} %collective-permute-done.10.refs_0_, bf16[128,384]{1,0:T(8,128)(2,1)S(1)} %collective-permute-done.11.refs_1_, ...), custom_call_target="tpu_custom_call", output_to_operand_aliasing={{0}: (2, {}), {1}: (3, {}), {2}: (4, {})} | custom-call | tf_op jit(solution)/shard_map/unpack_1/pallas_call | solution.py:460
  30.4 0.6 %collective-permute-done.7.refs_0_ = bf16[128,384]{1,0:T(8,128)(2,1)S(1)} collective-permute-done((bf16[128,384]{1,0:T(8,128)(2,1)S(1)}, bf16[128,384]{1,0:T(8,128)(2,1)S(1)}, u32[]{:S(2)}, u32[]{:S(2)}) %collective-permute-start.7) | collective-permute-done | bytes 98336 | tf_op jit(solution)/shard_map/ppermute | solution.py:161
  31.0 0.2 collective-permute-done.8.refs_1_
  31.2 0.8 %unpack_2.1 = (bf16[128,1024]{1,0:T(8,128)(2,1)}, bf16[128,1024]{1,0:T(8,128)(2,1)}, bf16[128,1024]{1,0:T(8,128)(2,1)}) custom-call(bf16[128,384]{1,0:T(8,128)(2,1)S(1)} %collective-permute-done.7.refs_0_, bf16[128,384]{1,0:T(8,128)(2,1)S(1)} %collective-permute-done.8.refs_1_, ...), custom_call_target="tpu_custom_call", output_to_operand_aliasing={{0}: (3, {}), {1}: (4, {}), {2}: (5, {})} | custom-call | tf_op jit(solution)/shard_map/unpack_2/pallas_call | solution.py:460
  (5 shorter events, 0.0 us)
Async XLA Ops:
  1.6 8.0 %collective-permute-start.1 = (bf16[128,512]{1,0:T(8,128)(2,1)S(1)}, bf16[128,512]{1,0:T(8,128)(2,1)S(1)}, u32[]{:S(2)}, u32[]{:S(2)}) collective-permute-start(bf16[128,512]{1,0:T(8,128)(2,1)S(1)} %get-tuple-element.51), channel_id=1, source_target_pairs={{0,20},{4,16},{8,28},{12,24},{16,4},{20,0},{24,12},{28,8},{1,21},{... | collective-permute-start | bytes 393224 | tf_op jit(solution)/shard_map/ppermute | solution.py:161
  5.6 5.2 %collective-permute-start.2 = (bf16[128,512]{1,0:T(8,128)(2,1)S(1)}, bf16[128,512]{1,0:T(8,128)(2,1)S(1)}, u32[]{:S(2)}, u32[]{:S(2)}) collective-permute-start(bf16[128,512]{1,0:T(8,128)(2,1)S(1)} %get-tuple-element.52), channel_id=1, source_target_pairs={{0,24},{4,8},{8,4},{12,20},{16,28},{20,12},{24,0},{28,16},{1,25},{... | collective-permute-start | bytes 393224 | tf_op jit(solution)/shard_map/ppermute | solution.py:161
  6.9 7.9 %collective-permute-start.3 = (bf16[128,512]{1,0:T(8,128)(2,1)S(1)}, bf16[128,512]{1,0:T(8,128)(2,1)S(1)}, u32[]{:S(2)}, u32[]{:S(2)}) collective-permute-start(bf16[128,512]{1,0:T(8,128)(2,1)S(1)} %get-tuple-element.53), channel_id=1, source_target_pairs={{0,8},{4,12},{8,0},{12,4},{16,24},{20,28},{24,16},{28,20},{1,9},{5... | collective-permute-start | bytes 393224 | tf_op jit(solution)/shard_map/ppermute | solution.py:161
  7.6 7.2 %collective-permute-start.4 = (bf16[128,512]{1,0:T(8,128)(2,1)S(1)}, bf16[128,512]{1,0:T(8,128)(2,1)S(1)}, u32[]{:S(2)}, u32[]{:S(2)}) collective-permute-start(bf16[128,512]{1,0:T(8,128)(2,1)S(1)} %get-tuple-element.54), channel_id=1, source_target_pairs={{0,16},{4,20},{8,12},{12,8},{16,0},{20,4},{24,28},{28,24},{1,17},{... | collective-permute-start | bytes 393224 | tf_op jit(solution)/shard_map/ppermute | solution.py:161
  9.1 6.3 %collective-permute-start.5 = (bf16[128,512]{1,0:T(8,128)(2,1)S(1)}, bf16[128,512]{1,0:T(8,128)(2,1)S(1)}, u32[]{:S(2)}, u32[]{:S(2)}) collective-permute-start(bf16[128,512]{1,0:T(8,128)(2,1)S(1)} %get-tuple-element.55), channel_id=1, source_target_pairs={{0,4},{4,0},{8,24},{12,28},{16,20},{20,16},{24,8},{28,12},{1,5},{5... | collective-permute-start | bytes 393224 | tf_op jit(solution)/shard_map/ppermute | solution.py:161
  9.6 5.8 %collective-permute-start.6 = (bf16[128,512]{1,0:T(8,128)(2,1)S(1)}, bf16[128,512]{1,0:T(8,128)(2,1)S(1)}, u32[]{:S(2)}, u32[]{:S(2)}) collective-permute-start(bf16[128,512]{1,0:T(8,128)(2,1)S(1)} %get-tuple-element.56), channel_id=1, source_target_pairs={{0,12},{4,28},{8,16},{12,0},{16,8},{20,24},{24,20},{28,4},{1,13},{... | collective-permute-start | bytes 393224 | tf_op jit(solution)/shard_map/ppermute | solution.py:161
  10.7 6.8 %collective-permute-start = (bf16[128,512]{1,0:T(8,128)(2,1)S(1)}, bf16[128,512]{1,0:T(8,128)(2,1)S(1)}, u32[]{:S(2)}, u32[]{:S(2)}) collective-permute-start(bf16[128,512]{1,0:T(8,128)(2,1)S(1)} %get-tuple-element.49), channel_id=1, source_target_pairs={{0,28},{4,24},{8,20},{12,16},{16,12},{20,8},{24,4},{28,0},{1,29},{... | collective-permute-start | bytes 393224 | tf_op jit(solution)/shard_map/ppermute | solution.py:161
  19.0 6.6 %collective-permute-start.12 = (bf16[128,384]{1,0:T(8,128)(2,1)S(1)}, bf16[128,384]{1,0:T(8,128)(2,1)S(1)}, u32[]{:S(2)}, u32[]{:S(2)}) collective-permute-start(bf16[128,384]{1,0:T(8,128)(2,1)S(1)} %get-tuple-element.75), channel_id=1, source_target_pairs={{0,20},{4,16},{8,28},{12,24},{16,4},{20,0},{24,12},{28,8},{1,21},{... | collective-permute-start | bytes 294920 | tf_op jit(solution)/shard_map/ppermute | solution.py:161
  20.4 6.6 %collective-permute-start.13 = (bf16[128,384]{1,0:T(8,128)(2,1)S(1)}, bf16[128,384]{1,0:T(8,128)(2,1)S(1)}, u32[]{:S(2)}, u32[]{:S(2)}) collective-permute-start(bf16[128,384]{1,0:T(8,128)(2,1)S(1)} %get-tuple-element.76), channel_id=1, source_target_pairs={{0,28},{4,24},{8,20},{12,16},{16,12},{20,8},{24,4},{28,0},{1,29},{... | collective-permute-start | bytes 294920 | tf_op jit(solution)/shard_map/ppermute | solution.py:161
  22.5 6.9 %collective-permute-start.10 = (bf16[128,384]{1,0:T(8,128)(2,1)S(1)}, bf16[128,384]{1,0:T(8,128)(2,1)S(1)}, u32[]{:S(2)}, u32[]{:S(2)}) collective-permute-start(bf16[128,384]{1,0:T(8,128)(2,1)S(1)} %get-tuple-element.72), channel_id=1, source_target_pairs={{0,16},{4,20},{8,12},{12,8},{16,0},{20,4},{24,28},{28,24},{1,17},{... | collective-permute-start | bytes 294920 | tf_op jit(solution)/shard_map/ppermute | solution.py:161
  24.0 5.7 %collective-permute-start.11 = (bf16[128,384]{1,0:T(8,128)(2,1)S(1)}, bf16[128,384]{1,0:T(8,128)(2,1)S(1)}, u32[]{:S(2)}, u32[]{:S(2)}) collective-permute-start(bf16[128,384]{1,0:T(8,128)(2,1)S(1)} %get-tuple-element.73), channel_id=1, source_target_pairs={{0,4},{4,0},{8,24},{12,28},{16,20},{20,16},{24,8},{28,12},{1,5},{5... | collective-permute-start | bytes 294920 | tf_op jit(solution)/shard_map/ppermute | solution.py:161
  25.0 6.0 %collective-permute-start.7 = (bf16[128,384]{1,0:T(8,128)(2,1)S(1)}, bf16[128,384]{1,0:T(8,128)(2,1)S(1)}, u32[]{:S(2)}, u32[]{:S(2)}) collective-permute-start(bf16[128,384]{1,0:T(8,128)(2,1)S(1)} %get-tuple-element.69), channel_id=1, source_target_pairs={{0,24},{4,8},{8,4},{12,20},{16,28},{20,12},{24,0},{28,16},{1,25},{... | collective-permute-start | bytes 294920 | tf_op jit(solution)/shard_map/ppermute | solution.py:161
  25.6 5.6 %collective-permute-start.8 = (bf16[128,384]{1,0:T(8,128)(2,1)S(1)}, bf16[128,384]{1,0:T(8,128)(2,1)S(1)}, u32[]{:S(2)}, u32[]{:S(2)}) collective-permute-start(bf16[128,384]{1,0:T(8,128)(2,1)S(1)} %get-tuple-element.70), channel_id=1, source_target_pairs={{0,12},{4,28},{8,16},{12,0},{16,8},{20,24},{24,20},{28,4},{1,13},{... | collective-permute-start | bytes 294920 | tf_op jit(solution)/shard_map/ppermute | solution.py:161
  27.0 4.2 %collective-permute-start.9 = (bf16[128,384]{1,0:T(8,128)(2,1)S(1)}, bf16[128,384]{1,0:T(8,128)(2,1)S(1)}, u32[]{:S(2)}, u32[]{:S(2)}) collective-permute-start(bf16[128,384]{1,0:T(8,128)(2,1)S(1)} %get-tuple-element.71), channel_id=1, source_target_pairs={{0,8},{4,12},{8,0},{12,4},{16,24},{20,28},{24,16},{28,20},{1,9},{5... | collective-permute-start | bytes 294920 | tf_op jit(solution)/shard_map/ppermute | solution.py:161

commit v9 on v8

--- a/solution.py
+++ b/solution.py
@@ -152,6 +152,7 @@
 LATE = 7
 BEYOND = (4, 5, 6, 7)
 DONE = 1
+OTHER = 0
 AFTER = {}
 EXPONENT = math.log2(math.e) / math.sqrt(HEAD_DIM)
 
@@ -318,7 +319,7 @@
 def late_kernel(slab, *refs):
     seen_ref, stack_ref, exps_ref, dprobs_ref, stats_ref, done_ref = refs[:6]
     outs = dict(zip(BEYOND, refs[6:10]))
-    probs_out, dscores_out, query_out = refs[10:]
+    tiles_out, rows_out = refs[10:]
     cells = stack_ref.shape[0] // 2
     take = taker(slab, stack_ref)
 
@@ -360,69 +361,72 @@
         delta[u] = product * inverse[u]
         early_inverse[u] = inverse[u] if shrink is None else inverse[u] * shrink
 
-    def finished(u):
+    def finished(u, n):
         c, queries = units[u]
-        probs_low, dscores = [], []
-        for n, key in enumerate(key_places(c)):
+        low, terms = [], []
+        for key in (2 * n, 2 * n + 1):
             if key in fresh[u]:
                 index = fresh[u].index(key)
-                probs, term = exps[u][index] * inverse[u], dprobs[u][index]
+                probs, dprob = exps[u][index] * inverse[u], dprobs[u][index]
             else:
-                place = (c, slice(128 * n, 128 * (n + 1)), slice(0, 128 * len(queries)))
-                probs, term = exps_ref[place] * early_inverse[u], dprobs_ref[place]
-            probs_low.append(probs.astype(jnp.bfloat16))
-            dscores.append((probs * (term - delta[u])).astype(jnp.bfloat16))
-        return probs_low, dscores
-
-    probs_low = [{} for _ in range(cells)]
-    dscores = [{} for _ in range(cells)]
-
-    def rows_of(c):
-        if c == DONE:
-            pair = [blocks_of(done_ref[n]) for n in range(2)]
-        elif LATE // 2 == c:
-            sides = zip(finished(0), finished(1))
-            pair = [
-                [jnp.concatenate(both, axis=1) for both in zip(left, right)] for left, right in sides
-            ]
-        else:
-            pair = finished(units.index((c, (2 * c, 2 * c + 1))))
+                row = 128 * key_places(c).index(key)
+                place = (c, slice(row, row + 128), slice(0, 128 * len(queries)))
+                probs, dprob = exps_ref[place] * early_inverse[u], dprobs_ref[place]
+            low.append(probs.astype(jnp.bfloat16))
+            terms.append((probs * (dprob - delta[u])).astype(jnp.bfloat16))
+        return jnp.concatenate(low, axis=0), jnp.concatenate(terms, axis=0)
+
+    tiles = {}
+    for c in (LATE // 2, OTHER, LATE // 2 ^ 1, DONE):
         for t, n in enumerate(near_cells(c)):
-            probs_low[n][c] = jnp.concatenate(pair[0][2 * t : 2 * t + 2], axis=0)
-            dscores[n][c] = jnp.concatenate(pair[1][2 * t : 2 * t + 2], axis=0)
-
-    def joined(blocks, c):
-        return jnp.concatenate([blocks[n] for n in near_cells(c)], axis=1)
-
-    for c in (LATE // 2, 1 - DONE, LATE // 2 ^ 1, DONE):
-        rows_of(c)
+            if c < 2 and n < 2:
+                continue
+            if c == DONE:
+                tiles[n, c] = [done_ref[i, 256 * t : 256 * (t + 1)] for i in range(2)]
+            elif c == LATE // 2:
+                sides = zip(finished(0, n), finished(1, n))
+                tiles[n, c] = [jnp.concatenate(both, axis=1) for both in sides]
+            else:
+                tiles[n, c] = finished(units.index((c, (2 * c, 2 * c + 1))), n)
     for c in (2, 3):
-        places = (2 * c, 2 * c + 1)
-        put_pair_grads(take, c, joined(probs_low[c], c), joined(dscores[c], c), [outs[p] for p in places])
-    for c in (2, 3, 1 - DONE):
-        terms = jnp.concatenate([dscores[n][c] for n in near_cells(c)], axis=0)
+        pair = [jnp.concatenate([tiles[c, m][i] for m in near_cells(c)], axis=1) for i in range(2)]
+        put_pair_grads(take, c, *pair, [outs[2 * c], outs[2 * c + 1]])
+    for c in (2, 3):
+        terms = jnp.concatenate([tiles[n, c][1] for n in near_cells(c)], axis=0)
         dq = query_grad(take(key_places(c), 1), terms)
-        if c == 1 - DONE:
-            query_out[...] = dq
-        else:
-            for a in range(2):
-                put(outs[2 * c + a], 0, dq[a])
-    for n in (0, 1):
-        probs_out[n] = joined(probs_low[n], n)
-        dscores_out[n] = joined(dscores[n], n)
-
-
-def rest_kernel(distances, slab, stack_ref, probs_ref, dscores_ref, *refs):
-    query_refs, kept, outs, out_ref = refs[:2], refs[2:4], refs[4:-1], refs[-1]
+        for a in range(2):
+            put(outs[2 * c + a], 0, dq[a])
+    for i in range(2):
+        for n in (0, 1):
+            tiles_out[i, n] = tiles[n, n ^ 3][i]
+    tiles_out[1, 2] = tiles[OTHER ^ 3, OTHER][1]
+    u = units.index((OTHER, (2 * OTHER, 2 * OTHER + 1)))
+    rows_out[0:1] = early_inverse[u]
+    rows_out[1:2] = delta[u]
+
+
+def rest_kernel(distances, slab, *refs):
+    stack_ref, exps_ref, dprobs_ref, done_ref, query_ref, tiles_ref, rows_ref = refs[:7]
+    kept, outs, out_ref = refs[7:9], refs[9:-1], refs[-1]
     here = flat_index(GROUP)
     fixed = [distance(here) for distance in distances]
     fixed = {place: out for place, out in zip(fixed, outs) if isinstance(place, int)}
     take = taker(slab, stack_ref)
+    tiles = {(n, n ^ 3): [tiles_ref[i, n] for i in range(2)] for n in (0, 1)}
+    for n in (0, 1):
+        rows = [slice(256 * near_cells(c).index(n), 256 * (near_cells(c).index(n) + 1)) for c in (DONE, OTHER)]
+        tiles[n, DONE] = [done_ref[i, rows[0]] for i in range(2)]
+        probs = exps_ref[OTHER, rows[1]] * rows_ref[0:1]
+        terms = probs * (dprobs_ref[OTHER, rows[1]] - rows_ref[1:2])
+        tiles[n, OTHER] = [probs.astype(jnp.bfloat16), terms.astype(jnp.bfloat16)]
+    terms = [tiles_ref[1, 2] if n > 1 else tiles[n, OTHER][1] for n in near_cells(OTHER)]
+    other_query = query_grad(take(key_places(OTHER), 1), jnp.concatenate(terms, axis=0))
     for c in (0, 1):
         targets = [fixed.get(place, out_ref.at[place]) for place in (2 * c, 2 * c + 1)]
-        put_pair_grads(take, c, probs_ref[c], dscores_ref[c], targets)
+        pair = [jnp.concatenate([tiles[c, m][i] for m in near_cells(c)], axis=1) for i in range(2)]
+        put_pair_grads(take, c, *pair, targets)
         for a, target in enumerate(targets):
-            put(target, 0, query_refs[c][a])
+            put(target, 0, query_ref[a] if c == DONE else other_query[a])
     for place, ref in zip((4, 6), kept):
         out_ref[place] = ref[...]
     for distance, out in zip(distances, outs):
@@ -510,31 +514,31 @@
         compiler_params=pltpu.CompilerParams(vmem_limit_bytes=24 * MIB),
         name="early",
     )(seen, *[got[n] for n in soon], own)
-    stack, *partial, query_grad_done = partial
+    stack, exps, dprobs, stats, done, done_query = partial
     slab = got[INWARD.index(LATE_HOP)]
-    low = jax.ShapeDtypeStruct((2, 2 * tokens, 6 * tokens), jnp.bfloat16)
-    *beyond, probs_low, dscores, query_grad_other = pl.pallas_call(
+    *beyond, tiles, rows = pl.pallas_call(
         late_kernel,
         out_shape=[slab_shape(tokens, 3)] * len(BEYOND)
-        + [low, low, jax.ShapeDtypeStruct((2, tokens, HEAD_DIM), jnp.bfloat16)],
+        + [
+            jax.ShapeDtypeStruct((2, 3, 2 * tokens, 2 * tokens), jnp.bfloat16),
+            jax.ShapeDtypeStruct((8, 2 * tokens), jnp.float32),
+        ],
         in_specs=[VMEM] * 7,
-        out_specs=[VMEM] * (len(BEYOND) + 3),
+        out_specs=[VMEM] * (len(BEYOND) + 2),
         compiler_params=pltpu.CompilerParams(vmem_limit_bytes=24 * MIB),
         name="late",
-    )(slab, seen, stack, *partial)
+    )(slab, seen, stack, exps, dprobs, stats, done)
     beyond = dict(zip(BEYOND, beyond))
-    query_grads = (query_grad_done, query_grad_other)
-    query_grads = query_grads[::-1] if DONE == 1 else query_grads
     distances = OUTWARD + (STAY,)
     rest = pl.pallas_call(
         functools.partial(rest_kernel, distances[2:]),
         out_shape=[slab_shape(tokens, 3)] * (devices - 2),
-        in_specs=[VMEM] * 8,
+        in_specs=[VMEM] * 10,
         out_specs=[VMEM] * (devices - 2),
         scratch_shapes=[pltpu.VMEM((devices, tokens, 3 * HEAD_DIM), jnp.bfloat16)],
         compiler_params=pltpu.CompilerParams(vmem_limit_bytes=24 * MIB),
         name="rest",
-    )(slab, stack, probs_low, dscores, *query_grads, beyond[4], beyond[6])
+    )(slab, stack, exps, dprobs, done, done_query, tiles, rows, beyond[4], beyond[6])
     grads = [beyond[5], beyond[7], *rest]
     back = [exchange(grad, distance) for grad, distance in zip(grads, OUTWARD)] + [grads[-1]]
     whole = jax.ShapeDtypeStruct(queries.shape, queries.dtype)

time: 32.3 us -> 32.1 us (level)
  no operation moved by 1% of the time
where the time goes in v9:
time: 32.1 us; the launch traced here: 31.8 us
  starting transfers between devices  17.7 us (55%)
  Pallas kernels  8.9 us (28%)
  waiting for transfers between devices  4.57 us (14%)
  between operations  0.71 us (2%)
    ppermute x14, starting transfers between devices, exchange(): return lax.ppermute(block, GROUP, [(i, i ^ distance(i)) for i in places])  17.7 us
    ppermute x14, waiting for transfers between devices, exchange(): return lax.ppermute(block, GROUP, [(i, i ^ distance(i)) for i in places])  4.57 us
    pallas_call x2, Pallas kernels, pack(): pl.pallas_call(functools.partial(pack_kernel, distances), out_shape=outs,...  2.3 us
    pallas_call x3, Pallas kernels, unpack(): pl.pallas_call(functools.partial(unpack_kernel, distances), out_shape=[wh...  2.28 us
    pallas_call x1, Pallas kernels, by_heads(): pl.pallas_call(functools.partial(early_kernel, [INWARD[n] for n in soon]...  1.6 us
    pallas_call x1, Pallas kernels, by_heads(): pl.pallas_call(late_kernel, out_shape=[slab_shape(tokens, 3)] * len(BEYON...  1.33 us
    pallas_call x1, Pallas kernels, by_heads(): pl.pallas_call(functools.partial(rest_kernel, distances[2:]), out_shape=[...  0.71 us
    pallas_call x1, Pallas kernels, by_heads(): pl.pallas_call(seen_kernel, out_shape=jax.ShapeDtypeStruct((cells, 8, 2 *...  0.68 us
  transfers between devices with their start and end apart: 14, of which 9 were waited for; matrix products, arithmetic and copies ran while one was open for 0% of the time, Pallas kernels for 18%

profile of v9, /device:TPU:0, one launch (start us, length us, event | category | flops | bytes accessed | tf_op | source)
XLA Modules:
  0.0 31.8 jit_solution(2505331633295543451)
XLA Ops:
  0.6 1.0 %pack_first.1 = (bf16[128,512]{1,0:T(8,128)(2,1)S(1)}, bf16[128,512]{1,0:T(8,128)(2,1)S(1)}) custom-call(bf16[128,1024]{1,0:T(8,128)(2,1)} %refs_0_.2, bf16[128,1024]{1,0:T(8,128)(2,1)} %refs_1_.2, bf16[128,1024]{1,0:T(8,128)(2,1)} %refs_2_.2, bf16[128,1024]{1,0:T(8,128)(2,1)} %refs_3_.2), custom_call_target="tpu_custom_call" | custom-call | tf_op jit(solution)/shard_map/pack_first/pallas_call | solution.py:451
  1.6 4.0 %collective-permute-start.1 = (bf16[128,512]{1,0:T(8,128)(2,1)S(1)}, bf16[128,512]{1,0:T(8,128)(2,1)S(1)}, u32[]{:S(2)}, u32[]{:S(2)}) collective-permute-start(bf16[128,512]{1,0:T(8,128)(2,1)S(1)} %get-tuple-element.50), channel_id=1, source_target_pairs={{0,20},{4,16},{8,28},{12,24},{16,4},{20,0},{24,12},{28,8},{1,21},{... | collective-permute-start | bytes 393224 | tf_op jit(solution)/shard_map/ppermute | solution.py:162
  5.6 0.0 collective-permute-start.2
  5.6 1.3 %pack_rest.1 = (bf16[128,512]{1,0:T(8,128)(2,1)S(1)}, bf16[128,512]{1,0:T(8,128)(2,1)S(1)}, bf16[128,512]{1,0:T(8,128)(2,1)S(1)}, bf16[128,512]{1,0:T(8,128)(2,1...) custom-call(bf16[128,1024]{1,0:T(8,128)(2,1)} %refs_0_.2, ...), custom_call_target="tpu_custom_call" | custom-call | tf_op jit(solution)/shard_map/pack_rest/pallas_call | solution.py:451
  6.9 0.7 %collective-permute-start.3 = (bf16[128,512]{1,0:T(8,128)(2,1)S(1)}, bf16[128,512]{1,0:T(8,128)(2,1)S(1)}, u32[]{:S(2)}, u32[]{:S(2)}) collective-permute-start(bf16[128,512]{1,0:T(8,128)(2,1)S(1)} %get-tuple-element.52), channel_id=1, source_target_pairs={{0,8},{4,12},{8,0},{12,4},{16,24},{20,28},{24,16},{28,20},{1,9},{5... | collective-permute-start | bytes 393224 | tf_op jit(solution)/shard_map/ppermute | solution.py:162
  7.6 1.5 %collective-permute-start.4 = (bf16[128,512]{1,0:T(8,128)(2,1)S(1)}, bf16[128,512]{1,0:T(8,128)(2,1)S(1)}, u32[]{:S(2)}, u32[]{:S(2)}) collective-permute-start(bf16[128,512]{1,0:T(8,128)(2,1)S(1)} %get-tuple-element.53), channel_id=1, source_target_pairs={{0,16},{4,20},{8,12},{12,8},{16,0},{20,4},{24,28},{28,24},{1,17},{... | collective-permute-start | bytes 393224 | tf_op jit(solution)/shard_map/ppermute | solution.py:162
  9.1 0.5 %collective-permute-start.5 = (bf16[128,512]{1,0:T(8,128)(2,1)S(1)}, bf16[128,512]{1,0:T(8,128)(2,1)S(1)}, u32[]{:S(2)}, u32[]{:S(2)}) collective-permute-start(bf16[128,512]{1,0:T(8,128)(2,1)S(1)} %get-tuple-element.54), channel_id=1, source_target_pairs={{0,4},{4,0},{8,24},{12,28},{16,20},{20,16},{24,8},{28,12},{1,5},{5... | collective-permute-start | bytes 393224 | tf_op jit(solution)/shard_map/ppermute | solution.py:162
  9.6 0.6 %collective-permute-start.6 = (bf16[128,512]{1,0:T(8,128)(2,1)S(1)}, bf16[128,512]{1,0:T(8,128)(2,1)S(1)}, u32[]{:S(2)}, u32[]{:S(2)}) collective-permute-start(bf16[128,512]{1,0:T(8,128)(2,1)S(1)} %get-tuple-element.55), channel_id=1, source_target_pairs={{0,12},{4,28},{8,16},{12,0},{16,8},{20,24},{24,20},{28,4},{1,13},{... | collective-permute-start | bytes 393224 | tf_op jit(solution)/shard_map/ppermute | solution.py:162
  10.3 0.4 %collective-permute-done.2.refs_1_ = bf16[128,512]{1,0:T(8,128)(2,1)S(1)} collective-permute-done((bf16[128,512]{1,0:T(8,128)(2,1)S(1)}, bf16[128,512]{1,0:T(8,128)(2,1)S(1)}, u32[]{:S(2)}, u32[]{:S(2)}) %collective-permute-start.2) | collective-permute-done | bytes 131104 | tf_op jit(solution)/shard_map/ppermute | solution.py:162
  10.7 3.4 %collective-permute-start = (bf16[128,512]{1,0:T(8,128)(2,1)S(1)}, bf16[128,512]{1,0:T(8,128)(2,1)S(1)}, u32[]{:S(2)}, u32[]{:S(2)}) collective-permute-start(bf16[128,512]{1,0:T(8,128)(2,1)S(1)} %get-tuple-element.48), channel_id=1, source_target_pairs={{0,28},{4,24},{8,20},{12,16},{16,12},{20,8},{24,4},{28,0},{1,29},{... | collective-permute-start | bytes 393224 | tf_op jit(solution)/shard_map/ppermute | solution.py:162
  14.1 0.7 %seen.1.seen_ref.refs_0_ = f32[4,8,256]{2,1,0:T(8,128)S(1)} custom-call(s32[8,8]{1,0:T(8,128)S(1)} %get-tuple-element.49.mask_ref), custom_call_target="tpu_custom_call" | custom-call | tf_op jit(solution)/shard_map/seen/pallas_call | solution.py:493
  14.8 0.6 %collective-permute-done.5.refs_4_ = bf16[128,512]{1,0:T(8,128)(2,1)S(1)} collective-permute-done((bf16[128,512]{1,0:T(8,128)(2,1)S(1)}, bf16[128,512]{1,0:T(8,128)(2,1)S(1)}, u32[]{:S(2)}, u32[]{:S(2)}) %collective-permute-start.5) | collective-permute-done | bytes 131104 | tf_op jit(solution)/shard_map/ppermute | solution.py:162
  15.4 1.6 %early.1 = (bf16[8,128,512]{2,1,0:T(8,128)(2,1)S(1)}, f32[4,768,256]{2,1,0:T(8,128)S(1)}, f32[4,768,256]{2,1,0:T(8,128)S(1)}, f32[4,8,256]{2,1,0:T(8,128)S(1)}, ...) custom-call(f32[4,8,256]{2,1,0:T(8,128)S(1)} %seen.1.seen_ref.refs_0_, ...), custom_call_target="tpu_custom_call" | custom-call | tf_op jit(solution)/shard_map/early/pallas_call | solution.py:502
  17.1 0.5 %collective-permute-done.slab = bf16[128,512]{1,0:T(8,128)(2,1)S(1)} collective-permute-done((bf16[128,512]{1,0:T(8,128)(2,1)S(1)}, bf16[128,512]{1,0:T(8,128)(2,1)S(1)}, u32[]{:S(2)}, u32[]{:S(2)}) %collective-permute-start) | collective-permute-done | bytes 131104 | tf_op jit(solution)/shard_map/ppermute | solution.py:162
  17.6 1.3 %late.1 = (bf16[128,384]{1,0:T(8,128)(2,1)S(1)}, bf16[128,384]{1,0:T(8,128)(2,1)S(1)}, bf16[128,384]{1,0:T(8,128)(2,1)S(1)}, bf16[128,384]{1,0:T(8,128)(2,1)S(1)...) custom-call(bf16[128,512]{1,0:T(8,128)(2,1)S(1)} %collective-permute-done.slab, ...), custom_call_target="tpu_custom_call" | custom-call | tf_op jit(solution)/shard_map/late/pallas_call | solution.py:519
  18.9 1.4 %collective-permute-start.12 = (bf16[128,384]{1,0:T(8,128)(2,1)S(1)}, bf16[128,384]{1,0:T(8,128)(2,1)S(1)}, u32[]{:S(2)}, u32[]{:S(2)}) collective-permute-start(bf16[128,384]{1,0:T(8,128)(2,1)S(1)} %get-tuple-element.73), channel_id=1, source_target_pairs={{0,20},{4,16},{8,28},{12,24},{16,4},{20,0},{24,12},{28,8},{1,21},{... | collective-permute-start | bytes 294920 | tf_op jit(solution)/shard_map/ppermute | solution.py:162
  20.3 1.4 %collective-permute-start.13 = (bf16[128,384]{1,0:T(8,128)(2,1)S(1)}, bf16[128,384]{1,0:T(8,128)(2,1)S(1)}, u32[]{:S(2)}, u32[]{:S(2)}) collective-permute-start(bf16[128,384]{1,0:T(8,128)(2,1)S(1)} %get-tuple-element.74), channel_id=1, source_target_pairs={{0,28},{4,24},{8,20},{12,16},{16,12},{20,8},{24,4},{28,0},{1,29},{... | collective-permute-start | bytes 294920 | tf_op jit(solution)/shard_map/ppermute | solution.py:162
  21.7 0.7 %rest.1 = (bf16[128,384]{1,0:T(8,128)(2,1)S(1)}, bf16[128,384]{1,0:T(8,128)(2,1)S(1)}, bf16[128,384]{1,0:T(8,128)(2,1)S(1)}, bf16[128,384]{1,0:T(8,128)(2,1)S(1)...) custom-call(bf16[128,512]{1,0:T(8,128)(2,1)S(1)} %collective-permute-done.slab, ...), custom_call_target="tpu_custom_call" | custom-call | tf_op jit(solution)/shard_map/rest/pallas_call | solution.py:533
  22.4 1.5 %collective-permute-start.10 = (bf16[128,384]{1,0:T(8,128)(2,1)S(1)}, bf16[128,384]{1,0:T(8,128)(2,1)S(1)}, u32[]{:S(2)}, u32[]{:S(2)}) collective-permute-start(bf16[128,384]{1,0:T(8,128)(2,1)S(1)} %get-tuple-element.70), channel_id=1, source_target_pairs={{0,16},{4,20},{8,12},{12,8},{16,0},{20,4},{24,28},{28,24},{1,17},{... | collective-permute-start | bytes 294920 | tf_op jit(solution)/shard_map/ppermute | solution.py:162
  23.9 1.1 %collective-permute-start.11 = (bf16[128,384]{1,0:T(8,128)(2,1)S(1)}, bf16[128,384]{1,0:T(8,128)(2,1)S(1)}, u32[]{:S(2)}, u32[]{:S(2)}) collective-permute-start(bf16[128,384]{1,0:T(8,128)(2,1)S(1)} %get-tuple-element.71), channel_id=1, source_target_pairs={{0,4},{4,0},{8,24},{12,28},{16,20},{20,16},{24,8},{28,12},{1,5},{5... | collective-permute-start | bytes 294920 | tf_op jit(solution)/shard_map/ppermute | solution.py:162
  25.0 0.2 collective-permute-start.7
  25.2 0.2 collective-permute-done.12.refs_1_
  25.4 0.8 %collective-permute-start.8 = (bf16[128,384]{1,0:T(8,128)(2,1)S(1)}, bf16[128,384]{1,0:T(8,128)(2,1)S(1)}, u32[]{:S(2)}, u32[]{:S(2)}) collective-permute-start(bf16[128,384]{1,0:T(8,128)(2,1)S(1)} %get-tuple-element.68), channel_id=1, source_target_pairs={{0,12},{4,28},{8,16},{12,0},{16,8},{20,24},{24,20},{28,4},{1,13},{... | collective-permute-start | bytes 294920 | tf_op jit(solution)/shard_map/ppermute | solution.py:162
  26.3 0.6 %collective-permute-done.13.refs_2_ = bf16[128,384]{1,0:T(8,128)(2,1)S(1)} collective-permute-done((bf16[128,384]{1,0:T(8,128)(2,1)S(1)}, bf16[128,384]{1,0:T(8,128)(2,1)S(1)}, u32[]{:S(2)}, u32[]{:S(2)}) %collective-permute-start.13) | collective-permute-done | bytes 98336 | tf_op jit(solution)/shard_map/ppermute | solution.py:162
  26.9 0.5 %collective-permute-start.9 = (bf16[128,384]{1,0:T(8,128)(2,1)S(1)}, bf16[128,384]{1,0:T(8,128)(2,1)S(1)}, u32[]{:S(2)}, u32[]{:S(2)}) collective-permute-start(bf16[128,384]{1,0:T(8,128)(2,1)S(1)} %get-tuple-element.69), channel_id=1, source_target_pairs={{0,8},{4,12},{8,0},{12,4},{16,24},{20,28},{24,16},{28,20},{1,9},{5... | collective-permute-start | bytes 294920 | tf_op jit(solution)/shard_map/ppermute | solution.py:162
  27.4 0.8 %unpack_0.1 = (bf16[128,1024]{1,0:T(8,128)(2,1)}, bf16[128,1024]{1,0:T(8,128)(2,1)}, bf16[128,1024]{1,0:T(8,128)(2,1)}) custom-call(bf16[128,384]{1,0:T(8,128)(2,1)S(1)} %get-tuple-element.72.refs_0_, bf16[128,384]{1,0:T(8,128)(2,1)S(1)} %collective-permute-done.12.refs_1_, bf16[128,384]{1,0:T(8,128)(2,1)S(1)} %collective-permute-done.13.refs_2_), custom_call_target="tpu_custom_call" | custom-call | tf_op jit(solution)/shard_map/unpack_0/pallas_call | solution.py:464
  28.2 1.1 %collective-permute-done.10.refs_0_ = bf16[128,384]{1,0:T(8,128)(2,1)S(1)} collective-permute-done((bf16[128,384]{1,0:T(8,128)(2,1)S(1)}, bf16[128,384]{1,0:T(8,128)(2,1)S(1)}, u32[]{:S(2)}, u32[]{:S(2)}) %collective-permute-start.10) | collective-permute-done | bytes 98336 | tf_op jit(solution)/shard_map/ppermute | solution.py:162
  29.3 0.3 %collective-permute-done.11.refs_1_ = bf16[128,384]{1,0:T(8,128)(2,1)S(1)} collective-permute-done((bf16[128,384]{1,0:T(8,128)(2,1)S(1)}, bf16[128,384]{1,0:T(8,128)(2,1)S(1)}, u32[]{:S(2)}, u32[]{:S(2)}) %collective-permute-start.11) | collective-permute-done | bytes 98336 | tf_op jit(solution)/shard_map/ppermute | solution.py:162
  29.6 0.7 %unpack_1.1 = (bf16[128,1024]{1,0:T(8,128)(2,1)}, bf16[128,1024]{1,0:T(8,128)(2,1)}, bf16[128,1024]{1,0:T(8,128)(2,1)}) custom-call(bf16[128,384]{1,0:T(8,128)(2,1)S(1)} %collective-permute-done.10.refs_0_, bf16[128,384]{1,0:T(8,128)(2,1)S(1)} %collective-permute-done.11.refs_1_, ...), custom_call_target="tpu_custom_call", output_to_operand_aliasing={{0}: (2, {}), {1}: (3, {}), {2}: (4, {})} | custom-call | tf_op jit(solution)/shard_map/unpack_1/pallas_call | solution.py:464
  30.4 0.5 %collective-permute-done.7.refs_0_ = bf16[128,384]{1,0:T(8,128)(2,1)S(1)} collective-permute-done((bf16[128,384]{1,0:T(8,128)(2,1)S(1)}, bf16[128,384]{1,0:T(8,128)(2,1)S(1)}, u32[]{:S(2)}, u32[]{:S(2)}) %collective-permute-start.7) | collective-permute-done | bytes 98336 | tf_op jit(solution)/shard_map/ppermute | solution.py:162
  30.9 0.2 collective-permute-done.8.refs_1_
  31.0 0.8 %unpack_2.1 = (bf16[128,1024]{1,0:T(8,128)(2,1)}, bf16[128,1024]{1,0:T(8,128)(2,1)}, bf16[128,1024]{1,0:T(8,128)(2,1)}) custom-call(bf16[128,384]{1,0:T(8,128)(2,1)S(1)} %collective-permute-done.7.refs_0_, bf16[128,384]{1,0:T(8,128)(2,1)S(1)} %collective-permute-done.8.refs_1_, ...), custom_call_target="tpu_custom_call", output_to_operand_aliasing={{0}: (3, {}), {1}: (4, {}), {2}: (5, {})} | custom-call | tf_op jit(solution)/shard_map/unpack_2/pallas_call | solution.py:464
  (5 shorter events, 0.0 us)
Async XLA Ops:
  1.6 8.0 %collective-permute-start.1 = (bf16[128,512]{1,0:T(8,128)(2,1)S(1)}, bf16[128,512]{1,0:T(8,128)(2,1)S(1)}, u32[]{:S(2)}, u32[]{:S(2)}) collective-permute-start(bf16[128,512]{1,0:T(8,128)(2,1)S(1)} %get-tuple-element.50), channel_id=1, source_target_pairs={{0,20},{4,16},{8,28},{12,24},{16,4},{20,0},{24,12},{28,8},{1,21},{... | collective-permute-start | bytes 393224 | tf_op jit(solution)/shard_map/ppermute | solution.py:162
  5.6 5.2 %collective-permute-start.2 = (bf16[128,512]{1,0:T(8,128)(2,1)S(1)}, bf16[128,512]{1,0:T(8,128)(2,1)S(1)}, u32[]{:S(2)}, u32[]{:S(2)}) collective-permute-start(bf16[128,512]{1,0:T(8,128)(2,1)S(1)} %get-tuple-element.51), channel_id=1, source_target_pairs={{0,24},{4,8},{8,4},{12,20},{16,28},{20,12},{24,0},{28,16},{1,25},{... | collective-permute-start | bytes 393224 | tf_op jit(solution)/shard_map/ppermute | solution.py:162
  6.9 7.9 %collective-permute-start.3 = (bf16[128,512]{1,0:T(8,128)(2,1)S(1)}, bf16[128,512]{1,0:T(8,128)(2,1)S(1)}, u32[]{:S(2)}, u32[]{:S(2)}) collective-permute-start(bf16[128,512]{1,0:T(8,128)(2,1)S(1)} %get-tuple-element.52), channel_id=1, source_target_pairs={{0,8},{4,12},{8,0},{12,4},{16,24},{20,28},{24,16},{28,20},{1,9},{5... | collective-permute-start | bytes 393224 | tf_op jit(solution)/shard_map/ppermute | solution.py:162
  7.6 7.2 %collective-permute-start.4 = (bf16[128,512]{1,0:T(8,128)(2,1)S(1)}, bf16[128,512]{1,0:T(8,128)(2,1)S(1)}, u32[]{:S(2)}, u32[]{:S(2)}) collective-permute-start(bf16[128,512]{1,0:T(8,128)(2,1)S(1)} %get-tuple-element.53), channel_id=1, source_target_pairs={{0,16},{4,20},{8,12},{12,8},{16,0},{20,4},{24,28},{28,24},{1,17},{... | collective-permute-start | bytes 393224 | tf_op jit(solution)/shard_map/ppermute | solution.py:162
  9.1 6.3 %collective-permute-start.5 = (bf16[128,512]{1,0:T(8,128)(2,1)S(1)}, bf16[128,512]{1,0:T(8,128)(2,1)S(1)}, u32[]{:S(2)}, u32[]{:S(2)}) collective-permute-start(bf16[128,512]{1,0:T(8,128)(2,1)S(1)} %get-tuple-element.54), channel_id=1, source_target_pairs={{0,4},{4,0},{8,24},{12,28},{16,20},{20,16},{24,8},{28,12},{1,5},{5... | collective-permute-start | bytes 393224 | tf_op jit(solution)/shard_map/ppermute | solution.py:162
  9.6 5.8 %collective-permute-start.6 = (bf16[128,512]{1,0:T(8,128)(2,1)S(1)}, bf16[128,512]{1,0:T(8,128)(2,1)S(1)}, u32[]{:S(2)}, u32[]{:S(2)}) collective-permute-start(bf16[128,512]{1,0:T(8,128)(2,1)S(1)} %get-tuple-element.55), channel_id=1, source_target_pairs={{0,12},{4,28},{8,16},{12,0},{16,8},{20,24},{24,20},{28,4},{1,13},{... | collective-permute-start | bytes 393224 | tf_op jit(solution)/shard_map/ppermute | solution.py:162
  10.7 6.8 %collective-permute-start = (bf16[128,512]{1,0:T(8,128)(2,1)S(1)}, bf16[128,512]{1,0:T(8,128)(2,1)S(1)}, u32[]{:S(2)}, u32[]{:S(2)}) collective-permute-start(bf16[128,512]{1,0:T(8,128)(2,1)S(1)} %get-tuple-element.48), channel_id=1, source_target_pairs={{0,28},{4,24},{8,20},{12,16},{16,12},{20,8},{24,4},{28,0},{1,29},{... | collective-permute-start | bytes 393224 | tf_op jit(solution)/shard_map/ppermute | solution.py:162
  18.9 6.6 %collective-permute-start.12 = (bf16[128,384]{1,0:T(8,128)(2,1)S(1)}, bf16[128,384]{1,0:T(8,128)(2,1)S(1)}, u32[]{:S(2)}, u32[]{:S(2)}) collective-permute-start(bf16[128,384]{1,0:T(8,128)(2,1)S(1)} %get-tuple-element.73), channel_id=1, source_target_pairs={{0,20},{4,16},{8,28},{12,24},{16,4},{20,0},{24,12},{28,8},{1,21},{... | collective-permute-start | bytes 294920 | tf_op jit(solution)/shard_map/ppermute | solution.py:162
  20.3 6.6 %collective-permute-start.13 = (bf16[128,384]{1,0:T(8,128)(2,1)S(1)}, bf16[128,384]{1,0:T(8,128)(2,1)S(1)}, u32[]{:S(2)}, u32[]{:S(2)}) collective-permute-start(bf16[128,384]{1,0:T(8,128)(2,1)S(1)} %get-tuple-element.74), channel_id=1, source_target_pairs={{0,28},{4,24},{8,20},{12,16},{16,12},{20,8},{24,4},{28,0},{1,29},{... | collective-permute-start | bytes 294920 | tf_op jit(solution)/shard_map/ppermute | solution.py:162
  22.4 6.8 %collective-permute-start.10 = (bf16[128,384]{1,0:T(8,128)(2,1)S(1)}, bf16[128,384]{1,0:T(8,128)(2,1)S(1)}, u32[]{:S(2)}, u32[]{:S(2)}) collective-permute-start(bf16[128,384]{1,0:T(8,128)(2,1)S(1)} %get-tuple-element.70), channel_id=1, source_target_pairs={{0,16},{4,20},{8,12},{12,8},{16,0},{20,4},{24,28},{28,24},{1,17},{... | collective-permute-start | bytes 294920 | tf_op jit(solution)/shard_map/ppermute | solution.py:162
  23.9 5.7 %collective-permute-start.11 = (bf16[128,384]{1,0:T(8,128)(2,1)S(1)}, bf16[128,384]{1,0:T(8,128)(2,1)S(1)}, u32[]{:S(2)}, u32[]{:S(2)}) collective-permute-start(bf16[128,384]{1,0:T(8,128)(2,1)S(1)} %get-tuple-element.71), channel_id=1, source_target_pairs={{0,4},{4,0},{8,24},{12,28},{16,20},{20,16},{24,8},{28,12},{1,5},{5... | collective-permute-start | bytes 294920 | tf_op jit(solution)/shard_map/ppermute | solution.py:162
  25.0 5.9 %collective-permute-start.7 = (bf16[128,384]{1,0:T(8,128)(2,1)S(1)}, bf16[128,384]{1,0:T(8,128)(2,1)S(1)}, u32[]{:S(2)}, u32[]{:S(2)}) collective-permute-start(bf16[128,384]{1,0:T(8,128)(2,1)S(1)} %get-tuple-element.67), channel_id=1, source_target_pairs={{0,24},{4,8},{8,4},{12,20},{16,28},{20,12},{24,0},{28,16},{1,25},{... | collective-permute-start | bytes 294920 | tf_op jit(solution)/shard_map/ppermute | solution.py:162
  25.4 5.6 %collective-permute-start.8 = (bf16[128,384]{1,0:T(8,128)(2,1)S(1)}, bf16[128,384]{1,0:T(8,128)(2,1)S(1)}, u32[]{:S(2)}, u32[]{:S(2)}) collective-permute-start(bf16[128,384]{1,0:T(8,128)(2,1)S(1)} %get-tuple-element.68), channel_id=1, source_target_pairs={{0,12},{4,28},{8,16},{12,0},{16,8},{20,24},{24,20},{28,4},{1,13},{... | collective-permute-start | bytes 294920 | tf_op jit(solution)/shard_map/ppermute | solution.py:162
  26.9 4.2 %collective-permute-start.9 = (bf16[128,384]{1,0:T(8,128)(2,1)S(1)}, bf16[128,384]{1,0:T(8,128)(2,1)S(1)}, u32[]{:S(2)}, u32[]{:S(2)}) collective-permute-start(bf16[128,384]{1,0:T(8,128)(2,1)S(1)} %get-tuple-element.69), channel_id=1, source_target_pairs={{0,8},{4,12},{8,0},{12,4},{16,24},{20,28},{24,16},{28,20},{1,9},{5... | collective-permute-start | bytes 294920 | tf_op jit(solution)/shard_map/ppermute | solution.py:162

commit v10 on v9

--- a/solution.py
+++ b/solution.py
@@ -250,8 +250,8 @@
 
 
 def early_kernel(distances, seen_ref, *refs):
-    slabs, outs = refs[:-6], refs[-6:]
-    stack_ref, exps_ref, dprobs_ref, stats_ref, done_ref, query_ref = outs
+    slabs, outs = refs[:-7], refs[-7:]
+    stack_ref, exps_ref, dprobs_ref, stats_ref, done_ref, query_ref, partial_ref = outs
     here = flat_index(GROUP)
     for distance, slab in zip(distances, slabs):
         stack_ref[distance(here)] = slab[...]
@@ -284,6 +284,9 @@
                 done_ref[0, 128 * n : 128 * (n + 1)] = probs.astype(jnp.bfloat16)
                 done_ref[1, 128 * n : 128 * (n + 1)] = terms[n]
             query_ref[...] = query_grad(take(key_places(c), 1), jnp.concatenate(terms, axis=0))
+            rows = slice(256 * near_cells(c).index(c ^ 3), 256 * near_cells(c).index(c ^ 3) + 256)
+            partial_ref[0] = jnp.dot(done_ref[0, rows], g, preferred_element_type=jnp.float32)
+            partial_ref[1] = jnp.dot(done_ref[1, rows], q, preferred_element_type=jnp.float32)
             continue
         for key, weight, term in zip(keys, exps, dprobs):
             row = 128 * key_places(c).index(key)
@@ -307,17 +310,20 @@
     out[:, n * HEAD_DIM : (n + 1) * HEAD_DIM] = value.astype(jnp.bfloat16)
 
 
-def put_pair_grads(take, c, probs_low, dscores, outs):
-    q, g = take(key_places(c), 0), take(key_places(c), 3)
-    dk = jnp.dot(dscores, q, preferred_element_type=jnp.float32) * (1.0 / math.sqrt(HEAD_DIM))
-    dv = jnp.dot(probs_low, g, preferred_element_type=jnp.float32)
+def put_pair_grads(take, c, probs_low, dscores, outs, partial=None):
+    places = key_places(c)[: dscores.shape[1] // 128]
+    dk = jnp.dot(dscores, take(places, 0), preferred_element_type=jnp.float32)
+    dv = jnp.dot(probs_low, take(places, 3), preferred_element_type=jnp.float32)
+    if partial is not None:
+        dv, dk = dv + partial[0], dk + partial[1]
+    dk = dk * (1.0 / math.sqrt(HEAD_DIM))
     for a, out in enumerate(outs):
         put(out, 1, dk[128 * a : 128 * (a + 1)])
         put(out, 2, dv[128 * a : 128 * (a + 1)])
 
 
 def late_kernel(slab, *refs):
-    seen_ref, stack_ref, exps_ref, dprobs_ref, stats_ref, done_ref = refs[:6]
+    seen_ref, stack_ref, exps_ref, dprobs_ref, stats_ref, partial_ref = refs[:6]
     outs = dict(zip(BEYOND, refs[6:10]))
     tiles_out, rows_out = refs[10:]
     cells = stack_ref.shape[0] // 2
@@ -377,20 +383,20 @@
         return jnp.concatenate(low, axis=0), jnp.concatenate(terms, axis=0)
 
     tiles = {}
-    for c in (LATE // 2, OTHER, LATE // 2 ^ 1, DONE):
-        for t, n in enumerate(near_cells(c)):
+    for c in (LATE // 2, OTHER, LATE // 2 ^ 1):
+        for n in near_cells(c):
             if c < 2 and n < 2:
                 continue
-            if c == DONE:
-                tiles[n, c] = [done_ref[i, 256 * t : 256 * (t + 1)] for i in range(2)]
-            elif c == LATE // 2:
+            if c == LATE // 2:
                 sides = zip(finished(0, n), finished(1, n))
                 tiles[n, c] = [jnp.concatenate(both, axis=1) for both in sides]
             else:
                 tiles[n, c] = finished(units.index((c, (2 * c, 2 * c + 1))), n)
     for c in (2, 3):
-        pair = [jnp.concatenate([tiles[c, m][i] for m in near_cells(c)], axis=1) for i in range(2)]
-        put_pair_grads(take, c, *pair, [outs[2 * c], outs[2 * c + 1]])
+        near = [m for m in near_cells(c) if m != DONE]
+        pair = [jnp.concatenate([tiles[c, m][i] for m in near], axis=1) for i in range(2)]
+        partial = partial_ref if len(near) < 3 else None
+        put_pair_grads(take, c, *pair, [outs[2 * c], outs[2 * c + 1]], partial)
     for c in (2, 3):
         terms = jnp.concatenate([tiles[n, c][1] for n in near_cells(c)], axis=0)
         dq = query_grad(take(key_places(c), 1), terms)
@@ -508,13 +514,14 @@
             jax.ShapeDtypeStruct((cells, 8, 2 * tokens), jnp.float32),
             jax.ShapeDtypeStruct((2, 6 * tokens, 2 * tokens), jnp.bfloat16),
             jax.ShapeDtypeStruct((2, tokens, HEAD_DIM), jnp.bfloat16),
+            jax.ShapeDtypeStruct((2, 2 * tokens, HEAD_DIM), jnp.float32),
         ],
         in_specs=[VMEM] * devices,
-        out_specs=[VMEM] * 6,
+        out_specs=[VMEM] * 7,
         compiler_params=pltpu.CompilerParams(vmem_limit_bytes=24 * MIB),
         name="early",
     )(seen, *[got[n] for n in soon], own)
-    stack, exps, dprobs, stats, done, done_query = partial
+    stack, exps, dprobs, stats, done, done_query, done_part = partial
     slab = got[INWARD.index(LATE_HOP)]
     *beyond, tiles, rows = pl.pallas_call(
         late_kernel,
@@ -527,7 +534,7 @@
         out_specs=[VMEM] * (len(BEYOND) + 2),
         compiler_params=pltpu.CompilerParams(vmem_limit_bytes=24 * MIB),
         name="late",
-    )(slab, seen, stack, exps, dprobs, stats, done)
+    )(slab, seen, stack, exps, dprobs, stats, done_part)
     beyond = dict(zip(BEYOND, beyond))
     distances = OUTWARD + (STAY,)
     rest = pl.pallas_call(

time: 32.1 us -> 32.1 us (level)
  no operation moved by 1% of the time
where the time goes in v10:
time: 32.1 us; the launch traced here: 31.8 us
  starting transfers between devices  17.7 us (55%)
  Pallas kernels  8.85 us (28%)
  waiting for transfers between devices  4.55 us (14%)
  between operations  0.71 us (2%)
    ppermute x14, starting transfers between devices, exchange(): return lax.ppermute(block, GROUP, [(i, i ^ distance(i)) for i in places])  17.7 us
    ppermute x14, waiting for transfers between devices, exchange(): return lax.ppermute(block, GROUP, [(i, i ^ distance(i)) for i in places])  4.55 us
    pallas_call x2, Pallas kernels, pack(): pl.pallas_call(functools.partial(pack_kernel, distances), out_shape=outs,...  2.3 us
    pallas_call x3, Pallas kernels, unpack(): pl.pallas_call(functools.partial(unpack_kernel, distances), out_shape=[wh...  2.28 us
    pallas_call x1, Pallas kernels, by_heads(): pl.pallas_call(functools.partial(early_kernel, [INWARD[n] for n in soon]...  1.62 us
    pallas_call x1, Pallas kernels, by_heads(): pl.pallas_call(late_kernel, out_shape=[slab_shape(tokens, 3)] * len(BEYON...  1.27 us
    pallas_call x1, Pallas kernels, by_heads(): pl.pallas_call(functools.partial(rest_kernel, distances[2:]), out_shape=[...  0.71 us
    pallas_call x1, Pallas kernels, by_heads(): pl.pallas_call(seen_kernel, out_shape=jax.ShapeDtypeStruct((cells, 8, 2 *...  0.68 us
  transfers between devices with their start and end apart: 14, of which 9 were waited for; matrix products, arithmetic and copies ran while one was open for 0% of the time, Pallas kernels for 18%

profile of v10, /device:TPU:0, one launch (start us, length us, event | category | flops | bytes accessed | tf_op | source)
XLA Modules:
  0.0 31.8 jit_solution(7455009596671748514)
XLA Ops:
  0.6 1.0 %pack_first.1 = (bf16[128,512]{1,0:T(8,128)(2,1)S(1)}, bf16[128,512]{1,0:T(8,128)(2,1)S(1)}) custom-call(bf16[128,1024]{1,0:T(8,128)(2,1)} %refs_0_.2, bf16[128,1024]{1,0:T(8,128)(2,1)} %refs_1_.2, bf16[128,1024]{1,0:T(8,128)(2,1)} %refs_2_.2, bf16[128,1024]{1,0:T(8,128)(2,1)} %refs_3_.2), custom_call_target="tpu_custom_call" | custom-call | tf_op jit(solution)/shard_map/pack_first/pallas_call | solution.py:457
  1.6 4.0 %collective-permute-start.1 = (bf16[128,512]{1,0:T(8,128)(2,1)S(1)}, bf16[128,512]{1,0:T(8,128)(2,1)S(1)}, u32[]{:S(2)}, u32[]{:S(2)}) collective-permute-start(bf16[128,512]{1,0:T(8,128)(2,1)S(1)} %get-tuple-element.51), channel_id=1, source_target_pairs={{0,20},{4,16},{8,28},{12,24},{16,4},{20,0},{24,12},{28,8},{1,21},{... | collective-permute-start | bytes 393224 | tf_op jit(solution)/shard_map/ppermute | solution.py:162
  5.6 1.3 %pack_rest.1 = (bf16[128,512]{1,0:T(8,128)(2,1)S(1)}, bf16[128,512]{1,0:T(8,128)(2,1)S(1)}, bf16[128,512]{1,0:T(8,128)(2,1)S(1)}, bf16[128,512]{1,0:T(8,128)(2,1...) custom-call(bf16[128,1024]{1,0:T(8,128)(2,1)} %refs_0_.2, ...), custom_call_target="tpu_custom_call" | custom-call | tf_op jit(solution)/shard_map/pack_rest/pallas_call | solution.py:457
  6.9 0.7 %collective-permute-start.3 = (bf16[128,512]{1,0:T(8,128)(2,1)S(1)}, bf16[128,512]{1,0:T(8,128)(2,1)S(1)}, u32[]{:S(2)}, u32[]{:S(2)}) collective-permute-start(bf16[128,512]{1,0:T(8,128)(2,1)S(1)} %get-tuple-element.53), channel_id=1, source_target_pairs={{0,8},{4,12},{8,0},{12,4},{16,24},{20,28},{24,16},{28,20},{1,9},{5... | collective-permute-start | bytes 393224 | tf_op jit(solution)/shard_map/ppermute | solution.py:162
  7.6 1.5 %collective-permute-start.4 = (bf16[128,512]{1,0:T(8,128)(2,1)S(1)}, bf16[128,512]{1,0:T(8,128)(2,1)S(1)}, u32[]{:S(2)}, u32[]{:S(2)}) collective-permute-start(bf16[128,512]{1,0:T(8,128)(2,1)S(1)} %get-tuple-element.54), channel_id=1, source_target_pairs={{0,16},{4,20},{8,12},{12,8},{16,0},{20,4},{24,28},{28,24},{1,17},{... | collective-permute-start | bytes 393224 | tf_op jit(solution)/shard_map/ppermute | solution.py:162
  9.1 0.5 %collective-permute-start.5 = (bf16[128,512]{1,0:T(8,128)(2,1)S(1)}, bf16[128,512]{1,0:T(8,128)(2,1)S(1)}, u32[]{:S(2)}, u32[]{:S(2)}) collective-permute-start(bf16[128,512]{1,0:T(8,128)(2,1)S(1)} %get-tuple-element.55), channel_id=1, source_target_pairs={{0,4},{4,0},{8,24},{12,28},{16,20},{20,16},{24,8},{28,12},{1,5},{5... | collective-permute-start | bytes 393224 | tf_op jit(solution)/shard_map/ppermute | solution.py:162
  9.6 0.6 %collective-permute-start.6 = (bf16[128,512]{1,0:T(8,128)(2,1)S(1)}, bf16[128,512]{1,0:T(8,128)(2,1)S(1)}, u32[]{:S(2)}, u32[]{:S(2)}) collective-permute-start(bf16[128,512]{1,0:T(8,128)(2,1)S(1)} %get-tuple-element.56), channel_id=1, source_target_pairs={{0,12},{4,28},{8,16},{12,0},{16,8},{20,24},{24,20},{28,4},{1,13},{... | collective-permute-start | bytes 393224 | tf_op jit(solution)/shard_map/ppermute | solution.py:162
  10.3 0.4 %collective-permute-done.2.refs_1_ = bf16[128,512]{1,0:T(8,128)(2,1)S(1)} collective-permute-done((bf16[128,512]{1,0:T(8,128)(2,1)S(1)}, bf16[128,512]{1,0:T(8,128)(2,1)S(1)}, u32[]{:S(2)}, u32[]{:S(2)}) %collective-permute-start.2) | collective-permute-done | bytes 131104 | tf_op jit(solution)/shard_map/ppermute | solution.py:162
  10.7 3.4 %collective-permute-start = (bf16[128,512]{1,0:T(8,128)(2,1)S(1)}, bf16[128,512]{1,0:T(8,128)(2,1)S(1)}, u32[]{:S(2)}, u32[]{:S(2)}) collective-permute-start(bf16[128,512]{1,0:T(8,128)(2,1)S(1)} %get-tuple-element.49), channel_id=1, source_target_pairs={{0,28},{4,24},{8,20},{12,16},{16,12},{20,8},{24,4},{28,0},{1,29},{... | collective-permute-start | bytes 393224 | tf_op jit(solution)/shard_map/ppermute | solution.py:162
  14.1 0.7 %seen.1.seen_ref.refs_0_ = f32[4,8,256]{2,1,0:T(8,128)S(1)} custom-call(s32[8,8]{1,0:T(8,128)S(1)} %get-tuple-element.50.mask_ref), custom_call_target="tpu_custom_call" | custom-call | tf_op jit(solution)/shard_map/seen/pallas_call | solution.py:499
  14.8 0.0 collective-permute-done.3.refs_2_
  14.8 0.6 %collective-permute-done.5.refs_4_ = bf16[128,512]{1,0:T(8,128)(2,1)S(1)} collective-permute-done((bf16[128,512]{1,0:T(8,128)(2,1)S(1)}, bf16[128,512]{1,0:T(8,128)(2,1)S(1)}, u32[]{:S(2)}, u32[]{:S(2)}) %collective-permute-start.5) | collective-permute-done | bytes 131104 | tf_op jit(solution)/shard_map/ppermute | solution.py:162
  15.4 1.6 %early.1 = (bf16[8,128,512]{2,1,0:T(8,128)(2,1)S(1)}, f32[4,768,256]{2,1,0:T(8,128)S(1)}, f32[4,768,256]{2,1,0:T(8,128)S(1)}, f32[4,8,256]{2,1,0:T(8,128)S(1)}, ...) custom-call(f32[4,8,256]{2,1,0:T(8,128)S(1)} %seen.1.seen_ref.refs_0_, ...), custom_call_target="tpu_custom_call" | custom-call | tf_op jit(solution)/shard_map/early/pallas_call | solution.py:508
  17.1 0.5 %collective-permute-done.slab = bf16[128,512]{1,0:T(8,128)(2,1)S(1)} collective-permute-done((bf16[128,512]{1,0:T(8,128)(2,1)S(1)}, bf16[128,512]{1,0:T(8,128)(2,1)S(1)}, u32[]{:S(2)}, u32[]{:S(2)}) %collective-permute-start) | collective-permute-done | bytes 131104 | tf_op jit(solution)/shard_map/ppermute | solution.py:162
  17.6 1.3 %late.1 = (bf16[128,384]{1,0:T(8,128)(2,1)S(1)}, bf16[128,384]{1,0:T(8,128)(2,1)S(1)}, bf16[128,384]{1,0:T(8,128)(2,1)S(1)}, bf16[128,384]{1,0:T(8,128)(2,1)S(1)...) custom-call(bf16[128,512]{1,0:T(8,128)(2,1)S(1)} %collective-permute-done.slab, ...), custom_call_target="tpu_custom_call" | custom-call | tf_op jit(solution)/shard_map/late/pallas_call | solution.py:526
  18.8 1.5 %collective-permute-start.12 = (bf16[128,384]{1,0:T(8,128)(2,1)S(1)}, bf16[128,384]{1,0:T(8,128)(2,1)S(1)}, u32[]{:S(2)}, u32[]{:S(2)}) collective-permute-start(bf16[128,384]{1,0:T(8,128)(2,1)S(1)} %get-tuple-element.75), channel_id=1, source_target_pairs={{0,20},{4,16},{8,28},{12,24},{16,4},{20,0},{24,12},{28,8},{1,21},{... | collective-permute-start | bytes 294920 | tf_op jit(solution)/shard_map/ppermute | solution.py:162
  20.3 1.4 %collective-permute-start.13 = (bf16[128,384]{1,0:T(8,128)(2,1)S(1)}, bf16[128,384]{1,0:T(8,128)(2,1)S(1)}, u32[]{:S(2)}, u32[]{:S(2)}) collective-permute-start(bf16[128,384]{1,0:T(8,128)(2,1)S(1)} %get-tuple-element.76), channel_id=1, source_target_pairs={{0,28},{4,24},{8,20},{12,16},{16,12},{20,8},{24,4},{28,0},{1,29},{... | collective-permute-start | bytes 294920 | tf_op jit(solution)/shard_map/ppermute | solution.py:162
  21.7 0.7 %rest.1 = (bf16[128,384]{1,0:T(8,128)(2,1)S(1)}, bf16[128,384]{1,0:T(8,128)(2,1)S(1)}, bf16[128,384]{1,0:T(8,128)(2,1)S(1)}, bf16[128,384]{1,0:T(8,128)(2,1)S(1)...) custom-call(bf16[128,512]{1,0:T(8,128)(2,1)S(1)} %collective-permute-done.slab, ...), custom_call_target="tpu_custom_call" | custom-call | tf_op jit(solution)/shard_map/rest/pallas_call | solution.py:540
  22.4 1.5 %collective-permute-start.10 = (bf16[128,384]{1,0:T(8,128)(2,1)S(1)}, bf16[128,384]{1,0:T(8,128)(2,1)S(1)}, u32[]{:S(2)}, u32[]{:S(2)}) collective-permute-start(bf16[128,384]{1,0:T(8,128)(2,1)S(1)} %get-tuple-element.72), channel_id=1, source_target_pairs={{0,16},{4,20},{8,12},{12,8},{16,0},{20,4},{24,28},{28,24},{1,17},{... | collective-permute-start | bytes 294920 | tf_op jit(solution)/shard_map/ppermute | solution.py:162
  23.9 1.1 %collective-permute-start.11 = (bf16[128,384]{1,0:T(8,128)(2,1)S(1)}, bf16[128,384]{1,0:T(8,128)(2,1)S(1)}, u32[]{:S(2)}, u32[]{:S(2)}) collective-permute-start(bf16[128,384]{1,0:T(8,128)(2,1)S(1)} %get-tuple-element.73), channel_id=1, source_target_pairs={{0,4},{4,0},{8,24},{12,28},{16,20},{20,16},{24,8},{28,12},{1,5},{5... | collective-permute-start | bytes 294920 | tf_op jit(solution)/shard_map/ppermute | solution.py:162
  24.9 0.2 collective-permute-start.7
  25.2 0.2 collective-permute-done.12.refs_1_
  25.4 0.8 %collective-permute-start.8 = (bf16[128,384]{1,0:T(8,128)(2,1)S(1)}, bf16[128,384]{1,0:T(8,128)(2,1)S(1)}, u32[]{:S(2)}, u32[]{:S(2)}) collective-permute-start(bf16[128,384]{1,0:T(8,128)(2,1)S(1)} %get-tuple-element.70), channel_id=1, source_target_pairs={{0,12},{4,28},{8,16},{12,0},{16,8},{20,24},{24,20},{28,4},{1,13},{... | collective-permute-start | bytes 294920 | tf_op jit(solution)/shard_map/ppermute | solution.py:162
  26.2 0.6 %collective-permute-done.13.refs_2_ = bf16[128,384]{1,0:T(8,128)(2,1)S(1)} collective-permute-done((bf16[128,384]{1,0:T(8,128)(2,1)S(1)}, bf16[128,384]{1,0:T(8,128)(2,1)S(1)}, u32[]{:S(2)}, u32[]{:S(2)}) %collective-permute-start.13) | collective-permute-done | bytes 98336 | tf_op jit(solution)/shard_map/ppermute | solution.py:162
  26.8 0.5 %collective-permute-start.9 = (bf16[128,384]{1,0:T(8,128)(2,1)S(1)}, bf16[128,384]{1,0:T(8,128)(2,1)S(1)}, u32[]{:S(2)}, u32[]{:S(2)}) collective-permute-start(bf16[128,384]{1,0:T(8,128)(2,1)S(1)} %get-tuple-element.71), channel_id=1, source_target_pairs={{0,8},{4,12},{8,0},{12,4},{16,24},{20,28},{24,16},{28,20},{1,9},{5... | collective-permute-start | bytes 294920 | tf_op jit(solution)/shard_map/ppermute | solution.py:162
  27.3 0.8 %unpack_0.1 = (bf16[128,1024]{1,0:T(8,128)(2,1)}, bf16[128,1024]{1,0:T(8,128)(2,1)}, bf16[128,1024]{1,0:T(8,128)(2,1)}) custom-call(bf16[128,384]{1,0:T(8,128)(2,1)S(1)} %get-tuple-element.74.refs_0_, bf16[128,384]{1,0:T(8,128)(2,1)S(1)} %collective-permute-done.12.refs_1_, bf16[128,384]{1,0:T(8,128)(2,1)S(1)} %collective-permute-done.13.refs_2_), custom_call_target="tpu_custom_call" | custom-call | tf_op jit(solution)/shard_map/unpack_0/pallas_call | solution.py:470
  28.1 1.1 %collective-permute-done.10.refs_0_ = bf16[128,384]{1,0:T(8,128)(2,1)S(1)} collective-permute-done((bf16[128,384]{1,0:T(8,128)(2,1)S(1)}, bf16[128,384]{1,0:T(8,128)(2,1)S(1)}, u32[]{:S(2)}, u32[]{:S(2)}) %collective-permute-start.10) | collective-permute-done | bytes 98336 | tf_op jit(solution)/shard_map/ppermute | solution.py:162
  29.2 0.3 %collective-permute-done.11.refs_1_ = bf16[128,384]{1,0:T(8,128)(2,1)S(1)} collective-permute-done((bf16[128,384]{1,0:T(8,128)(2,1)S(1)}, bf16[128,384]{1,0:T(8,128)(2,1)S(1)}, u32[]{:S(2)}, u32[]{:S(2)}) %collective-permute-start.11) | collective-permute-done | bytes 98336 | tf_op jit(solution)/shard_map/ppermute | solution.py:162
  29.6 0.7 %unpack_1.1 = (bf16[128,1024]{1,0:T(8,128)(2,1)}, bf16[128,1024]{1,0:T(8,128)(2,1)}, bf16[128,1024]{1,0:T(8,128)(2,1)}) custom-call(bf16[128,384]{1,0:T(8,128)(2,1)S(1)} %collective-permute-done.10.refs_0_, bf16[128,384]{1,0:T(8,128)(2,1)S(1)} %collective-permute-done.11.refs_1_, ...), custom_call_target="tpu_custom_call", output_to_operand_aliasing={{0}: (2, {}), {1}: (3, {}), {2}: (4, {})} | custom-call | tf_op jit(solution)/shard_map/unpack_1/pallas_call | solution.py:470
  30.3 0.5 %collective-permute-done.7.refs_0_ = bf16[128,384]{1,0:T(8,128)(2,1)S(1)} collective-permute-done((bf16[128,384]{1,0:T(8,128)(2,1)S(1)}, bf16[128,384]{1,0:T(8,128)(2,1)S(1)}, u32[]{:S(2)}, u32[]{:S(2)}) %collective-permute-start.7) | collective-permute-done | bytes 98336 | tf_op jit(solution)/shard_map/ppermute | solution.py:162
  30.8 0.2 collective-permute-done.8.refs_1_
  31.0 0.8 %unpack_2.1 = (bf16[128,1024]{1,0:T(8,128)(2,1)}, bf16[128,1024]{1,0:T(8,128)(2,1)}, bf16[128,1024]{1,0:T(8,128)(2,1)}) custom-call(bf16[128,384]{1,0:T(8,128)(2,1)S(1)} %collective-permute-done.7.refs_0_, bf16[128,384]{1,0:T(8,128)(2,1)S(1)} %collective-permute-done.8.refs_1_, ...), custom_call_target="tpu_custom_call", output_to_operand_aliasing={{0}: (3, {}), {1}: (4, {}), {2}: (5, {})} | custom-call | tf_op jit(solution)/shard_map/unpack_2/pallas_call | solution.py:470
  (5 shorter events, 0.0 us)
Async XLA Ops:
  1.6 8.0 %collective-permute-start.1 = (bf16[128,512]{1,0:T(8,128)(2,1)S(1)}, bf16[128,512]{1,0:T(8,128)(2,1)S(1)}, u32[]{:S(2)}, u32[]{:S(2)}) collective-permute-start(bf16[128,512]{1,0:T(8,128)(2,1)S(1)} %get-tuple-element.51), channel_id=1, source_target_pairs={{0,20},{4,16},{8,28},{12,24},{16,4},{20,0},{24,12},{28,8},{1,21},{... | collective-permute-start | bytes 393224 | tf_op jit(solution)/shard_map/ppermute | solution.py:162
  5.6 5.2 %collective-permute-start.2 = (bf16[128,512]{1,0:T(8,128)(2,1)S(1)}, bf16[128,512]{1,0:T(8,128)(2,1)S(1)}, u32[]{:S(2)}, u32[]{:S(2)}) collective-permute-start(bf16[128,512]{1,0:T(8,128)(2,1)S(1)} %get-tuple-element.52), channel_id=1, source_target_pairs={{0,24},{4,8},{8,4},{12,20},{16,28},{20,12},{24,0},{28,16},{1,25},{... | collective-permute-start | bytes 393224 | tf_op jit(solution)/shard_map/ppermute | solution.py:162
  6.9 7.9 %collective-permute-start.3 = (bf16[128,512]{1,0:T(8,128)(2,1)S(1)}, bf16[128,512]{1,0:T(8,128)(2,1)S(1)}, u32[]{:S(2)}, u32[]{:S(2)}) collective-permute-start(bf16[128,512]{1,0:T(8,128)(2,1)S(1)} %get-tuple-element.53), channel_id=1, source_target_pairs={{0,8},{4,12},{8,0},{12,4},{16,24},{20,28},{24,16},{28,20},{1,9},{5... | collective-permute-start | bytes 393224 | tf_op jit(solution)/shard_map/ppermute | solution.py:162
  7.6 7.2 %collective-permute-start.4 = (bf16[128,512]{1,0:T(8,128)(2,1)S(1)}, bf16[128,512]{1,0:T(8,128)(2,1)S(1)}, u32[]{:S(2)}, u32[]{:S(2)}) collective-permute-start(bf16[128,512]{1,0:T(8,128)(2,1)S(1)} %get-tuple-element.54), channel_id=1, source_target_pairs={{0,16},{4,20},{8,12},{12,8},{16,0},{20,4},{24,28},{28,24},{1,17},{... | collective-permute-start | bytes 393224 | tf_op jit(solution)/shard_map/ppermute | solution.py:162
  9.1 6.3 %collective-permute-start.5 = (bf16[128,512]{1,0:T(8,128)(2,1)S(1)}, bf16[128,512]{1,0:T(8,128)(2,1)S(1)}, u32[]{:S(2)}, u32[]{:S(2)}) collective-permute-start(bf16[128,512]{1,0:T(8,128)(2,1)S(1)} %get-tuple-element.55), channel_id=1, source_target_pairs={{0,4},{4,0},{8,24},{12,28},{16,20},{20,16},{24,8},{28,12},{1,5},{5... | collective-permute-start | bytes 393224 | tf_op jit(solution)/shard_map/ppermute | solution.py:162
  9.6 5.8 %collective-permute-start.6 = (bf16[128,512]{1,0:T(8,128)(2,1)S(1)}, bf16[128,512]{1,0:T(8,128)(2,1)S(1)}, u32[]{:S(2)}, u32[]{:S(2)}) collective-permute-start(bf16[128,512]{1,0:T(8,128)(2,1)S(1)} %get-tuple-element.56), channel_id=1, source_target_pairs={{0,12},{4,28},{8,16},{12,0},{16,8},{20,24},{24,20},{28,4},{1,13},{... | collective-permute-start | bytes 393224 | tf_op jit(solution)/shard_map/ppermute | solution.py:162
  10.7 6.8 %collective-permute-start = (bf16[128,512]{1,0:T(8,128)(2,1)S(1)}, bf16[128,512]{1,0:T(8,128)(2,1)S(1)}, u32[]{:S(2)}, u32[]{:S(2)}) collective-permute-start(bf16[128,512]{1,0:T(8,128)(2,1)S(1)} %get-tuple-element.49), channel_id=1, source_target_pairs={{0,28},{4,24},{8,20},{12,16},{16,12},{20,8},{24,4},{28,0},{1,29},{... | collective-permute-start | bytes 393224 | tf_op jit(solution)/shard_map/ppermute | solution.py:162
  18.8 6.6 %collective-permute-start.12 = (bf16[128,384]{1,0:T(8,128)(2,1)S(1)}, bf16[128,384]{1,0:T(8,128)(2,1)S(1)}, u32[]{:S(2)}, u32[]{:S(2)}) collective-permute-start(bf16[128,384]{1,0:T(8,128)(2,1)S(1)} %get-tuple-element.75), channel_id=1, source_target_pairs={{0,20},{4,16},{8,28},{12,24},{16,4},{20,0},{24,12},{28,8},{1,21},{... | collective-permute-start | bytes 294920 | tf_op jit(solution)/shard_map/ppermute | solution.py:162
  20.3 6.6 %collective-permute-start.13 = (bf16[128,384]{1,0:T(8,128)(2,1)S(1)}, bf16[128,384]{1,0:T(8,128)(2,1)S(1)}, u32[]{:S(2)}, u32[]{:S(2)}) collective-permute-start(bf16[128,384]{1,0:T(8,128)(2,1)S(1)} %get-tuple-element.76), channel_id=1, source_target_pairs={{0,28},{4,24},{8,20},{12,16},{16,12},{20,8},{24,4},{28,0},{1,29},{... | collective-permute-start | bytes 294920 | tf_op jit(solution)/shard_map/ppermute | solution.py:162
  22.4 6.8 %collective-permute-start.10 = (bf16[128,384]{1,0:T(8,128)(2,1)S(1)}, bf16[128,384]{1,0:T(8,128)(2,1)S(1)}, u32[]{:S(2)}, u32[]{:S(2)}) collective-permute-start(bf16[128,384]{1,0:T(8,128)(2,1)S(1)} %get-tuple-element.72), channel_id=1, source_target_pairs={{0,16},{4,20},{8,12},{12,8},{16,0},{20,4},{24,28},{28,24},{1,17},{... | collective-permute-start | bytes 294920 | tf_op jit(solution)/shard_map/ppermute | solution.py:162
  23.9 5.7 %collective-permute-start.11 = (bf16[128,384]{1,0:T(8,128)(2,1)S(1)}, bf16[128,384]{1,0:T(8,128)(2,1)S(1)}, u32[]{:S(2)}, u32[]{:S(2)}) collective-permute-start(bf16[128,384]{1,0:T(8,128)(2,1)S(1)} %get-tuple-element.73), channel_id=1, source_target_pairs={{0,4},{4,0},{8,24},{12,28},{16,20},{20,16},{24,8},{28,12},{1,5},{5... | collective-permute-start | bytes 294920 | tf_op jit(solution)/shard_map/ppermute | solution.py:162
  24.9 5.9 %collective-permute-start.7 = (bf16[128,384]{1,0:T(8,128)(2,1)S(1)}, bf16[128,384]{1,0:T(8,128)(2,1)S(1)}, u32[]{:S(2)}, u32[]{:S(2)}) collective-permute-start(bf16[128,384]{1,0:T(8,128)(2,1)S(1)} %get-tuple-element.69), channel_id=1, source_target_pairs={{0,24},{4,8},{8,4},{12,20},{16,28},{20,12},{24,0},{28,16},{1,25},{... | collective-permute-start | bytes 294920 | tf_op jit(solution)/shard_map/ppermute | solution.py:162
  25.4 5.6 %collective-permute-start.8 = (bf16[128,384]{1,0:T(8,128)(2,1)S(1)}, bf16[128,384]{1,0:T(8,128)(2,1)S(1)}, u32[]{:S(2)}, u32[]{:S(2)}) collective-permute-start(bf16[128,384]{1,0:T(8,128)(2,1)S(1)} %get-tuple-element.70), channel_id=1, source_target_pairs={{0,12},{4,28},{8,16},{12,0},{16,8},{20,24},{24,20},{28,4},{1,13},{... | collective-permute-start | bytes 294920 | tf_op jit(solution)/shard_map/ppermute | solution.py:162
  26.8 4.2 %collective-permute-start.9 = (bf16[128,384]{1,0:T(8,128)(2,1)S(1)}, bf16[128,384]{1,0:T(8,128)(2,1)S(1)}, u32[]{:S(2)}, u32[]{:S(2)}) collective-permute-start(bf16[128,384]{1,0:T(8,128)(2,1)S(1)} %get-tuple-element.71), channel_id=1, source_target_pairs={{0,8},{4,12},{8,0},{12,4},{16,24},{20,28},{24,16},{28,20},{1,9},{5... | collective-permute-start | bytes 294920 | tf_op jit(solution)/shard_map/ppermute | solution.py:162

commit v11 on v10

--- a/solution.py
+++ b/solution.py
@@ -145,7 +145,7 @@
 OTHER_SIDE_CORE = hop(3, 6, even_places)
 
 INWARD = (FAR, SIDE_CORE, CORE, SIDE, OTHER_SIDE, OTHER_SIDE_CORE, FAR_CORE)
-OUTWARD = (FAR, FAR_CORE, SIDE, OTHER_SIDE, SIDE_CORE, OTHER_SIDE_CORE, CORE)
+OUTWARD = (FAR, FAR_CORE, SIDE, OTHER_SIDE, OTHER_SIDE_CORE, SIDE_CORE, CORE)
 FIRST = 2
 UNPACKED = ((-1, 0, 1), (2, 3), (4, 5, 6))
 LATE_HOP = FAR_CORE

time: 32.1 us -> 32.1 us (level)
  transfers between devices with their start and end apart: 14 -> 14, of which waited for: 9 -> 7; matrix products, arithmetic and copies ran while one was open for 0% -> 0% of each run, Pallas kernels for 18% -> 18%
where the time goes in v11:
time: 32.1 us; the launch traced here: 31.8 us
  starting transfers between devices  17.9 us (56%)
  Pallas kernels  8.85 us (28%)
  waiting for transfers between devices  4.34 us (14%)
  between operations  0.71 us (2%)
    ppermute x14, starting transfers between devices, exchange(): return lax.ppermute(block, GROUP, [(i, i ^ distance(i)) for i in places])  17.9 us
    ppermute x14, waiting for transfers between devices, exchange(): return lax.ppermute(block, GROUP, [(i, i ^ distance(i)) for i in places])  4.34 us
    pallas_call x2, Pallas kernels, pack(): pl.pallas_call(functools.partial(pack_kernel, distances), out_shape=outs,...  2.3 us
    pallas_call x3, Pallas kernels, unpack(): pl.pallas_call(functools.partial(unpack_kernel, distances), out_shape=[wh...  2.28 us
    pallas_call x1, Pallas kernels, by_heads(): pl.pallas_call(functools.partial(early_kernel, [INWARD[n] for n in soon]...  1.62 us
    pallas_call x1, Pallas kernels, by_heads(): pl.pallas_call(late_kernel, out_shape=[slab_shape(tokens, 3)] * len(BEYON...  1.27 us
    pallas_call x1, Pallas kernels, by_heads(): pl.pallas_call(functools.partial(rest_kernel, distances[2:]), out_shape=[...  0.72 us
    pallas_call x1, Pallas kernels, by_heads(): pl.pallas_call(seen_kernel, out_shape=jax.ShapeDtypeStruct((cells, 8, 2 *...  0.68 us
  transfers between devices with their start and end apart: 14, of which 7 were waited for; matrix products, arithmetic and copies ran while one was open for 0% of the time, Pallas kernels for 18%

profile of v11, /device:TPU:0, one launch (start us, length us, event | category | flops | bytes accessed | tf_op | source)
XLA Modules:
  0.0 31.8 jit_solution(17061662847399092825)
XLA Ops:
  0.6 1.0 %pack_first.1 = (bf16[128,512]{1,0:T(8,128)(2,1)S(1)}, bf16[128,512]{1,0:T(8,128)(2,1)S(1)}) custom-call(bf16[128,1024]{1,0:T(8,128)(2,1)} %refs_0_.2, bf16[128,1024]{1,0:T(8,128)(2,1)} %refs_1_.2, bf16[128,1024]{1,0:T(8,128)(2,1)} %refs_2_.2, bf16[128,1024]{1,0:T(8,128)(2,1)} %refs_3_.2), custom_call_target="tpu_custom_call" | custom-call | tf_op jit(solution)/shard_map/pack_first/pallas_call | solution.py:457
  1.6 4.0 %collective-permute-start.1 = (bf16[128,512]{1,0:T(8,128)(2,1)S(1)}, bf16[128,512]{1,0:T(8,128)(2,1)S(1)}, u32[]{:S(2)}, u32[]{:S(2)}) collective-permute-start(bf16[128,512]{1,0:T(8,128)(2,1)S(1)} %get-tuple-element.51), channel_id=1, source_target_pairs={{0,20},{4,16},{8,28},{12,24},{16,4},{20,0},{24,12},{28,8},{1,21},{... | collective-permute-start | bytes 393224 | tf_op jit(solution)/shard_map/ppermute | solution.py:162
  5.6 1.3 %pack_rest.1 = (bf16[128,512]{1,0:T(8,128)(2,1)S(1)}, bf16[128,512]{1,0:T(8,128)(2,1)S(1)}, bf16[128,512]{1,0:T(8,128)(2,1)S(1)}, bf16[128,512]{1,0:T(8,128)(2,1...) custom-call(bf16[128,1024]{1,0:T(8,128)(2,1)} %refs_0_.2, ...), custom_call_target="tpu_custom_call" | custom-call | tf_op jit(solution)/shard_map/pack_rest/pallas_call | solution.py:457
  6.9 0.7 %collective-permute-start.3 = (bf16[128,512]{1,0:T(8,128)(2,1)S(1)}, bf16[128,512]{1,0:T(8,128)(2,1)S(1)}, u32[]{:S(2)}, u32[]{:S(2)}) collective-permute-start(bf16[128,512]{1,0:T(8,128)(2,1)S(1)} %get-tuple-element.53), channel_id=1, source_target_pairs={{0,8},{4,12},{8,0},{12,4},{16,24},{20,28},{24,16},{28,20},{1,9},{5... | collective-permute-start | bytes 393224 | tf_op jit(solution)/shard_map/ppermute | solution.py:162
  7.6 1.5 %collective-permute-start.4 = (bf16[128,512]{1,0:T(8,128)(2,1)S(1)}, bf16[128,512]{1,0:T(8,128)(2,1)S(1)}, u32[]{:S(2)}, u32[]{:S(2)}) collective-permute-start(bf16[128,512]{1,0:T(8,128)(2,1)S(1)} %get-tuple-element.54), channel_id=1, source_target_pairs={{0,16},{4,20},{8,12},{12,8},{16,0},{20,4},{24,28},{28,24},{1,17},{... | collective-permute-start | bytes 393224 | tf_op jit(solution)/shard_map/ppermute | solution.py:162
  9.1 0.5 %collective-permute-start.5 = (bf16[128,512]{1,0:T(8,128)(2,1)S(1)}, bf16[128,512]{1,0:T(8,128)(2,1)S(1)}, u32[]{:S(2)}, u32[]{:S(2)}) collective-permute-start(bf16[128,512]{1,0:T(8,128)(2,1)S(1)} %get-tuple-element.55), channel_id=1, source_target_pairs={{0,4},{4,0},{8,24},{12,28},{16,20},{20,16},{24,8},{28,12},{1,5},{5... | collective-permute-start | bytes 393224 | tf_op jit(solution)/shard_map/ppermute | solution.py:162
  9.6 0.0 collective-permute-done.1.refs_0_
  9.6 0.6 %collective-permute-start.6 = (bf16[128,512]{1,0:T(8,128)(2,1)S(1)}, bf16[128,512]{1,0:T(8,128)(2,1)S(1)}, u32[]{:S(2)}, u32[]{:S(2)}) collective-permute-start(bf16[128,512]{1,0:T(8,128)(2,1)S(1)} %get-tuple-element.56), channel_id=1, source_target_pairs={{0,12},{4,28},{8,16},{12,0},{16,8},{20,24},{24,20},{28,4},{1,13},{... | collective-permute-start | bytes 393224 | tf_op jit(solution)/shard_map/ppermute | solution.py:162
  10.3 0.4 %collective-permute-done.2.refs_1_ = bf16[128,512]{1,0:T(8,128)(2,1)S(1)} collective-permute-done((bf16[128,512]{1,0:T(8,128)(2,1)S(1)}, bf16[128,512]{1,0:T(8,128)(2,1)S(1)}, u32[]{:S(2)}, u32[]{:S(2)}) %collective-permute-start.2) | collective-permute-done | bytes 131104 | tf_op jit(solution)/shard_map/ppermute | solution.py:162
  10.7 3.4 %collective-permute-start = (bf16[128,512]{1,0:T(8,128)(2,1)S(1)}, bf16[128,512]{1,0:T(8,128)(2,1)S(1)}, u32[]{:S(2)}, u32[]{:S(2)}) collective-permute-start(bf16[128,512]{1,0:T(8,128)(2,1)S(1)} %get-tuple-element.49), channel_id=1, source_target_pairs={{0,28},{4,24},{8,20},{12,16},{16,12},{20,8},{24,4},{28,0},{1,29},{... | collective-permute-start | bytes 393224 | tf_op jit(solution)/shard_map/ppermute | solution.py:162
  14.1 0.7 %seen.1.seen_ref.refs_0_ = f32[4,8,256]{2,1,0:T(8,128)S(1)} custom-call(s32[8,8]{1,0:T(8,128)S(1)} %get-tuple-element.50.mask_ref), custom_call_target="tpu_custom_call" | custom-call | tf_op jit(solution)/shard_map/seen/pallas_call | solution.py:499
  14.8 0.0 collective-permute-done.3.refs_2_
  14.8 0.6 %collective-permute-done.5.refs_4_ = bf16[128,512]{1,0:T(8,128)(2,1)S(1)} collective-permute-done((bf16[128,512]{1,0:T(8,128)(2,1)S(1)}, bf16[128,512]{1,0:T(8,128)(2,1)S(1)}, u32[]{:S(2)}, u32[]{:S(2)}) %collective-permute-start.5) | collective-permute-done | bytes 131104 | tf_op jit(solution)/shard_map/ppermute | solution.py:162
  15.4 0.0 collective-permute-done.6.refs_5_
  15.4 1.6 %early.1 = (bf16[8,128,512]{2,1,0:T(8,128)(2,1)S(1)}, f32[4,768,256]{2,1,0:T(8,128)S(1)}, f32[4,768,256]{2,1,0:T(8,128)S(1)}, f32[4,8,256]{2,1,0:T(8,128)S(1)}, ...) custom-call(f32[4,8,256]{2,1,0:T(8,128)S(1)} %seen.1.seen_ref.refs_0_, ...), custom_call_target="tpu_custom_call" | custom-call | tf_op jit(solution)/shard_map/early/pallas_call | solution.py:508
  17.1 0.5 %collective-permute-done.slab = bf16[128,512]{1,0:T(8,128)(2,1)S(1)} collective-permute-done((bf16[128,512]{1,0:T(8,128)(2,1)S(1)}, bf16[128,512]{1,0:T(8,128)(2,1)S(1)}, u32[]{:S(2)}, u32[]{:S(2)}) %collective-permute-start) | collective-permute-done | bytes 131104 | tf_op jit(solution)/shard_map/ppermute | solution.py:162
  17.6 1.3 %late.1 = (bf16[128,384]{1,0:T(8,128)(2,1)S(1)}, bf16[128,384]{1,0:T(8,128)(2,1)S(1)}, bf16[128,384]{1,0:T(8,128)(2,1)S(1)}, bf16[128,384]{1,0:T(8,128)(2,1)S(1)...) custom-call(bf16[128,512]{1,0:T(8,128)(2,1)S(1)} %collective-permute-done.slab, ...), custom_call_target="tpu_custom_call" | custom-call | tf_op jit(solution)/shard_map/late/pallas_call | solution.py:526
  18.8 1.5 %collective-permute-start.12 = (bf16[128,384]{1,0:T(8,128)(2,1)S(1)}, bf16[128,384]{1,0:T(8,128)(2,1)S(1)}, u32[]{:S(2)}, u32[]{:S(2)}) collective-permute-start(bf16[128,384]{1,0:T(8,128)(2,1)S(1)} %get-tuple-element.75), channel_id=1, source_target_pairs={{0,20},{4,16},{8,28},{12,24},{16,4},{20,0},{24,12},{28,8},{1,21},{... | collective-permute-start | bytes 294920 | tf_op jit(solution)/shard_map/ppermute | solution.py:162
  20.3 1.4 %collective-permute-start.13 = (bf16[128,384]{1,0:T(8,128)(2,1)S(1)}, bf16[128,384]{1,0:T(8,128)(2,1)S(1)}, u32[]{:S(2)}, u32[]{:S(2)}) collective-permute-start(bf16[128,384]{1,0:T(8,128)(2,1)S(1)} %get-tuple-element.76), channel_id=1, source_target_pairs={{0,28},{4,24},{8,20},{12,16},{16,12},{20,8},{24,4},{28,0},{1,29},{... | collective-permute-start | bytes 294920 | tf_op jit(solution)/shard_map/ppermute | solution.py:162
  21.7 0.7 %rest.1 = (bf16[128,384]{1,0:T(8,128)(2,1)S(1)}, bf16[128,384]{1,0:T(8,128)(2,1)S(1)}, bf16[128,384]{1,0:T(8,128)(2,1)S(1)}, bf16[128,384]{1,0:T(8,128)(2,1)S(1)...) custom-call(bf16[128,512]{1,0:T(8,128)(2,1)S(1)} %collective-permute-done.slab, ...), custom_call_target="tpu_custom_call" | custom-call | tf_op jit(solution)/shard_map/rest/pallas_call | solution.py:540
  22.4 1.5 %collective-permute-start.10 = (bf16[128,384]{1,0:T(8,128)(2,1)S(1)}, bf16[128,384]{1,0:T(8,128)(2,1)S(1)}, u32[]{:S(2)}, u32[]{:S(2)}) collective-permute-start(bf16[128,384]{1,0:T(8,128)(2,1)S(1)} %get-tuple-element.72), channel_id=1, source_target_pairs={{0,16},{4,20},{8,12},{12,8},{16,0},{20,4},{24,28},{28,24},{1,17},{... | collective-permute-start | bytes 294920 | tf_op jit(solution)/shard_map/ppermute | solution.py:162
  23.9 1.1 %collective-permute-start.11 = (bf16[128,384]{1,0:T(8,128)(2,1)S(1)}, bf16[128,384]{1,0:T(8,128)(2,1)S(1)}, u32[]{:S(2)}, u32[]{:S(2)}) collective-permute-start(bf16[128,384]{1,0:T(8,128)(2,1)S(1)} %get-tuple-element.73), channel_id=1, source_target_pairs={{0,4},{4,0},{8,24},{12,28},{16,20},{20,16},{24,8},{28,12},{1,5},{5... | collective-permute-start | bytes 294920 | tf_op jit(solution)/shard_map/ppermute | solution.py:162
  24.9 0.6 %collective-permute-start.7 = (bf16[128,384]{1,0:T(8,128)(2,1)S(1)}, bf16[128,384]{1,0:T(8,128)(2,1)S(1)}, u32[]{:S(2)}, u32[]{:S(2)}) collective-permute-start(bf16[128,384]{1,0:T(8,128)(2,1)S(1)} %get-tuple-element.69), channel_id=1, source_target_pairs={{0,12},{4,28},{8,16},{12,0},{16,8},{20,24},{24,20},{28,4},{1,13},{... | collective-permute-start | bytes 294920 | tf_op jit(solution)/shard_map/ppermute | solution.py:162
  25.5 0.7 %collective-permute-start.8 = (bf16[128,384]{1,0:T(8,128)(2,1)S(1)}, bf16[128,384]{1,0:T(8,128)(2,1)S(1)}, u32[]{:S(2)}, u32[]{:S(2)}) collective-permute-start(bf16[128,384]{1,0:T(8,128)(2,1)S(1)} %get-tuple-element.70), channel_id=1, source_target_pairs={{0,24},{4,8},{8,4},{12,20},{16,28},{20,12},{24,0},{28,16},{1,25},{... | collective-permute-start | bytes 294920 | tf_op jit(solution)/shard_map/ppermute | solution.py:162
  26.2 0.6 %collective-permute-done.13.refs_2_ = bf16[128,384]{1,0:T(8,128)(2,1)S(1)} collective-permute-done((bf16[128,384]{1,0:T(8,128)(2,1)S(1)}, bf16[128,384]{1,0:T(8,128)(2,1)S(1)}, u32[]{:S(2)}, u32[]{:S(2)}) %collective-permute-start.13) | collective-permute-done | bytes 98336 | tf_op jit(solution)/shard_map/ppermute | solution.py:162
  26.8 0.5 %collective-permute-start.9 = (bf16[128,384]{1,0:T(8,128)(2,1)S(1)}, bf16[128,384]{1,0:T(8,128)(2,1)S(1)}, u32[]{:S(2)}, u32[]{:S(2)}) collective-permute-start(bf16[128,384]{1,0:T(8,128)(2,1)S(1)} %get-tuple-element.71), channel_id=1, source_target_pairs={{0,8},{4,12},{8,0},{12,4},{16,24},{20,28},{24,16},{28,20},{1,9},{5... | collective-permute-start | bytes 294920 | tf_op jit(solution)/shard_map/ppermute | solution.py:162
  27.3 0.8 %unpack_0.1 = (bf16[128,1024]{1,0:T(8,128)(2,1)}, bf16[128,1024]{1,0:T(8,128)(2,1)}, bf16[128,1024]{1,0:T(8,128)(2,1)}) custom-call(bf16[128,384]{1,0:T(8,128)(2,1)S(1)} %get-tuple-element.74.refs_0_, bf16[128,384]{1,0:T(8,128)(2,1)S(1)} %collective-permute-done.12.refs_1_, bf16[128,384]{1,0:T(8,128)(2,1)S(1)} %collective-permute-done.13.refs_2_), custom_call_target="tpu_custom_call" | custom-call | tf_op jit(solution)/shard_map/unpack_0/pallas_call | solution.py:470
  28.1 1.1 %collective-permute-done.10.refs_0_ = bf16[128,384]{1,0:T(8,128)(2,1)S(1)} collective-permute-done((bf16[128,384]{1,0:T(8,128)(2,1)S(1)}, bf16[128,384]{1,0:T(8,128)(2,1)S(1)}, u32[]{:S(2)}, u32[]{:S(2)}) %collective-permute-start.10) | collective-permute-done | bytes 98336 | tf_op jit(solution)/shard_map/ppermute | solution.py:162
  29.2 0.3 %collective-permute-done.11.refs_1_ = bf16[128,384]{1,0:T(8,128)(2,1)S(1)} collective-permute-done((bf16[128,384]{1,0:T(8,128)(2,1)S(1)}, bf16[128,384]{1,0:T(8,128)(2,1)S(1)}, u32[]{:S(2)}, u32[]{:S(2)}) %collective-permute-start.11) | collective-permute-done | bytes 98336 | tf_op jit(solution)/shard_map/ppermute | solution.py:162
  29.6 0.7 %unpack_1.1 = (bf16[128,1024]{1,0:T(8,128)(2,1)}, bf16[128,1024]{1,0:T(8,128)(2,1)}, bf16[128,1024]{1,0:T(8,128)(2,1)}) custom-call(bf16[128,384]{1,0:T(8,128)(2,1)S(1)} %collective-permute-done.10.refs_0_, bf16[128,384]{1,0:T(8,128)(2,1)S(1)} %collective-permute-done.11.refs_1_, ...), custom_call_target="tpu_custom_call", output_to_operand_aliasing={{0}: (2, {}), {1}: (3, {}), {2}: (4, {})} | custom-call | tf_op jit(solution)/shard_map/unpack_1/pallas_call | solution.py:470
  30.3 0.7 %collective-permute-done.7.refs_0_ = bf16[128,384]{1,0:T(8,128)(2,1)S(1)} collective-permute-done((bf16[128,384]{1,0:T(8,128)(2,1)S(1)}, bf16[128,384]{1,0:T(8,128)(2,1)S(1)}, u32[]{:S(2)}, u32[]{:S(2)}) %collective-permute-start.7) | collective-permute-done | bytes 98336 | tf_op jit(solution)/shard_map/ppermute | solution.py:162
  31.0 0.8 %unpack_2.1 = (bf16[128,1024]{1,0:T(8,128)(2,1)}, bf16[128,1024]{1,0:T(8,128)(2,1)}, bf16[128,1024]{1,0:T(8,128)(2,1)}) custom-call(bf16[128,384]{1,0:T(8,128)(2,1)S(1)} %collective-permute-done.7.refs_0_, bf16[128,384]{1,0:T(8,128)(2,1)S(1)} %collective-permute-done.8.refs_1_, ...), custom_call_target="tpu_custom_call", output_to_operand_aliasing={{0}: (3, {}), {1}: (4, {}), {2}: (5, {})} | custom-call | tf_op jit(solution)/shard_map/unpack_2/pallas_call | solution.py:470
  (5 shorter events, 0.0 us)
Async XLA Ops:
  1.6 8.0 %collective-permute-start.1 = (bf16[128,512]{1,0:T(8,128)(2,1)S(1)}, bf16[128,512]{1,0:T(8,128)(2,1)S(1)}, u32[]{:S(2)}, u32[]{:S(2)}) collective-permute-start(bf16[128,512]{1,0:T(8,128)(2,1)S(1)} %get-tuple-element.51), channel_id=1, source_target_pairs={{0,20},{4,16},{8,28},{12,24},{16,4},{20,0},{24,12},{28,8},{1,21},{... | collective-permute-start | bytes 393224 | tf_op jit(solution)/shard_map/ppermute | solution.py:162
  5.6 5.2 %collective-permute-start.2 = (bf16[128,512]{1,0:T(8,128)(2,1)S(1)}, bf16[128,512]{1,0:T(8,128)(2,1)S(1)}, u32[]{:S(2)}, u32[]{:S(2)}) collective-permute-start(bf16[128,512]{1,0:T(8,128)(2,1)S(1)} %get-tuple-element.52), channel_id=1, source_target_pairs={{0,24},{4,8},{8,4},{12,20},{16,28},{20,12},{24,0},{28,16},{1,25},{... | collective-permute-start | bytes 393224 | tf_op jit(solution)/shard_map/ppermute | solution.py:162
  6.9 7.9 %collective-permute-start.3 = (bf16[128,512]{1,0:T(8,128)(2,1)S(1)}, bf16[128,512]{1,0:T(8,128)(2,1)S(1)}, u32[]{:S(2)}, u32[]{:S(2)}) collective-permute-start(bf16[128,512]{1,0:T(8,128)(2,1)S(1)} %get-tuple-element.53), channel_id=1, source_target_pairs={{0,8},{4,12},{8,0},{12,4},{16,24},{20,28},{24,16},{28,20},{1,9},{5... | collective-permute-start | bytes 393224 | tf_op jit(solution)/shard_map/ppermute | solution.py:162
  7.6 7.2 %collective-permute-start.4 = (bf16[128,512]{1,0:T(8,128)(2,1)S(1)}, bf16[128,512]{1,0:T(8,128)(2,1)S(1)}, u32[]{:S(2)}, u32[]{:S(2)}) collective-permute-start(bf16[128,512]{1,0:T(8,128)(2,1)S(1)} %get-tuple-element.54), channel_id=1, source_target_pairs={{0,16},{4,20},{8,12},{12,8},{16,0},{20,4},{24,28},{28,24},{1,17},{... | collective-permute-start | bytes 393224 | tf_op jit(solution)/shard_map/ppermute | solution.py:162
  9.1 6.3 %collective-permute-start.5 = (bf16[128,512]{1,0:T(8,128)(2,1)S(1)}, bf16[128,512]{1,0:T(8,128)(2,1)S(1)}, u32[]{:S(2)}, u32[]{:S(2)}) collective-permute-start(bf16[128,512]{1,0:T(8,128)(2,1)S(1)} %get-tuple-element.55), channel_id=1, source_target_pairs={{0,4},{4,0},{8,24},{12,28},{16,20},{20,16},{24,8},{28,12},{1,5},{5... | collective-permute-start | bytes 393224 | tf_op jit(solution)/shard_map/ppermute | solution.py:162
  9.6 5.8 %collective-permute-start.6 = (bf16[128,512]{1,0:T(8,128)(2,1)S(1)}, bf16[128,512]{1,0:T(8,128)(2,1)S(1)}, u32[]{:S(2)}, u32[]{:S(2)}) collective-permute-start(bf16[128,512]{1,0:T(8,128)(2,1)S(1)} %get-tuple-element.56), channel_id=1, source_target_pairs={{0,12},{4,28},{8,16},{12,0},{16,8},{20,24},{24,20},{28,4},{1,13},{... | collective-permute-start | bytes 393224 | tf_op jit(solution)/shard_map/ppermute | solution.py:162
  10.7 6.8 %collective-permute-start = (bf16[128,512]{1,0:T(8,128)(2,1)S(1)}, bf16[128,512]{1,0:T(8,128)(2,1)S(1)}, u32[]{:S(2)}, u32[]{:S(2)}) collective-permute-start(bf16[128,512]{1,0:T(8,128)(2,1)S(1)} %get-tuple-element.49), channel_id=1, source_target_pairs={{0,28},{4,24},{8,20},{12,16},{16,12},{20,8},{24,4},{28,0},{1,29},{... | collective-permute-start | bytes 393224 | tf_op jit(solution)/shard_map/ppermute | solution.py:162
  18.8 6.7 %collective-permute-start.12 = (bf16[128,384]{1,0:T(8,128)(2,1)S(1)}, bf16[128,384]{1,0:T(8,128)(2,1)S(1)}, u32[]{:S(2)}, u32[]{:S(2)}) collective-permute-start(bf16[128,384]{1,0:T(8,128)(2,1)S(1)} %get-tuple-element.75), channel_id=1, source_target_pairs={{0,20},{4,16},{8,28},{12,24},{16,4},{20,0},{24,12},{28,8},{1,21},{... | collective-permute-start | bytes 294920 | tf_op jit(solution)/shard_map/ppermute | solution.py:162
  20.3 6.6 %collective-permute-start.13 = (bf16[128,384]{1,0:T(8,128)(2,1)S(1)}, bf16[128,384]{1,0:T(8,128)(2,1)S(1)}, u32[]{:S(2)}, u32[]{:S(2)}) collective-permute-start(bf16[128,384]{1,0:T(8,128)(2,1)S(1)} %get-tuple-element.76), channel_id=1, source_target_pairs={{0,28},{4,24},{8,20},{12,16},{16,12},{20,8},{24,4},{28,0},{1,29},{... | collective-permute-start | bytes 294920 | tf_op jit(solution)/shard_map/ppermute | solution.py:162
  22.4 6.8 %collective-permute-start.10 = (bf16[128,384]{1,0:T(8,128)(2,1)S(1)}, bf16[128,384]{1,0:T(8,128)(2,1)S(1)}, u32[]{:S(2)}, u32[]{:S(2)}) collective-permute-start(bf16[128,384]{1,0:T(8,128)(2,1)S(1)} %get-tuple-element.72), channel_id=1, source_target_pairs={{0,16},{4,20},{8,12},{12,8},{16,0},{20,4},{24,28},{28,24},{1,17},{... | collective-permute-start | bytes 294920 | tf_op jit(solution)/shard_map/ppermute | solution.py:162
  23.9 5.7 %collective-permute-start.11 = (bf16[128,384]{1,0:T(8,128)(2,1)S(1)}, bf16[128,384]{1,0:T(8,128)(2,1)S(1)}, u32[]{:S(2)}, u32[]{:S(2)}) collective-permute-start(bf16[128,384]{1,0:T(8,128)(2,1)S(1)} %get-tuple-element.73), channel_id=1, source_target_pairs={{0,4},{4,0},{8,24},{12,28},{16,20},{20,16},{24,8},{28,12},{1,5},{5... | collective-permute-start | bytes 294920 | tf_op jit(solution)/shard_map/ppermute | solution.py:162
  24.9 6.1 %collective-permute-start.7 = (bf16[128,384]{1,0:T(8,128)(2,1)S(1)}, bf16[128,384]{1,0:T(8,128)(2,1)S(1)}, u32[]{:S(2)}, u32[]{:S(2)}) collective-permute-start(bf16[128,384]{1,0:T(8,128)(2,1)S(1)} %get-tuple-element.69), channel_id=1, source_target_pairs={{0,12},{4,28},{8,16},{12,0},{16,8},{20,24},{24,20},{28,4},{1,13},{... | collective-permute-start | bytes 294920 | tf_op jit(solution)/shard_map/ppermute | solution.py:162
  25.5 5.5 %collective-permute-start.8 = (bf16[128,384]{1,0:T(8,128)(2,1)S(1)}, bf16[128,384]{1,0:T(8,128)(2,1)S(1)}, u32[]{:S(2)}, u32[]{:S(2)}) collective-permute-start(bf16[128,384]{1,0:T(8,128)(2,1)S(1)} %get-tuple-element.70), channel_id=1, source_target_pairs={{0,24},{4,8},{8,4},{12,20},{16,28},{20,12},{24,0},{28,16},{1,25},{... | collective-permute-start | bytes 294920 | tf_op jit(solution)/shard_map/ppermute | solution.py:162
  26.8 4.2 %collective-permute-start.9 = (bf16[128,384]{1,0:T(8,128)(2,1)S(1)}, bf16[128,384]{1,0:T(8,128)(2,1)S(1)}, u32[]{:S(2)}, u32[]{:S(2)}) collective-permute-start(bf16[128,384]{1,0:T(8,128)(2,1)S(1)} %get-tuple-element.71), channel_id=1, source_target_pairs={{0,8},{4,12},{8,0},{12,4},{16,24},{20,28},{24,16},{28,20},{1,9},{5... | collective-permute-start | bytes 294920 | tf_op jit(solution)/shard_map/ppermute | solution.py:162
